TPU v7x, 32 devices: a whole 2x2x4 slice. The times are simulated.
32 devices in a mesh: slab: 2 (over x), outer: 2 (over core), inner: 8 (over z, y).
Axes of the slice: x: 2, y: 2, z: 4, core: 2. Of those that a mesh axis runs over, the one named last changes fastest.
Arguments:
- x_stream: bfloat16 [8192, 8192], P(('slab', 'outer', 'inner')), parts along dimension 0, may hold values from -6 to 6
- b_stream: bfloat16 [8192, 1024], P(('slab', 'outer', 'inner')), parts along dimension 0, may hold values from -6 to 6
- c_stream: bfloat16 [8192, 1024], P(('slab', 'outer', 'inner')), parts along dimension 0, may hold values from -6 to 6
- dt_input: bfloat16 [8192, 128], P(('slab', 'outer', 'inner')), parts along dimension 0, may hold values from -20 to 16, as said below
- decay_log: float32 [256], P('slab'), parts along dimension 0, may hold values from -3.5 to 0.6
- skip_weight: float32 [128], replicated, may hold values from 0.1 to 1.9
- conv_weight: bfloat16 [4, 10240], replicated, may hold values from -3 to 3
Outputs:
- scan_out: bfloat16 [8192, 8192], P(('slab', 'outer', 'inner')), parts along dimension 0
There are 2 independent parts, one for each index of `slab`. A program takes and returns all parts, laid end to end along the dimension named above; an argument that names none is the same for every part. Nothing has to cross between parts.
Inputs may be any that keep to these rules, and one draw needn't show every extreme that they name: `dt_input`: the softplus inverse of a positive time step.
All inputs are finite; a program needn't handle non-finite values.
Results may differ from a plain program's by a relative error of at most 0.0039.
Values may be sent and summed in bfloat16 or wider, within the bound.
No kernel may reach another device: no remote copies, remote signals or barrier semaphores. Data moves between devices by JAX's collectives and lax.ppermute only.
A program may use at most 320 MiB of HBM per device.

v0:
```python
import jax
import jax.numpy as jnp
from jax import lax
from jax.experimental import pallas as pl
from jax.experimental.pallas import tpu as pltpu
from jax.sharding import PartitionSpec as P

H = 128
P_SIZE = 64
N = 128
G = 8
KERNEL_TAPS = 4
SPAN = 256

HEADS = H // G
COLS = HEADS * P_SIZE
HALF = N // 2
RIM = KERNEL_TAPS - 1
PAD = 8
LOG2E = 1.4426950408889634
VMEM = 48 * 1024 * 1024
F32 = jnp.float32
BF16 = jnp.bfloat16
CHUNKS = (2, 2, 2, 2)


def params():
    return pltpu.CompilerParams(vmem_limit_bytes=VMEM)


def cost(us, moved):
    return pl.CostEstimate(flops=int(us * 6e8), bytes_accessed=moved, transcendentals=0)


def steps_body(dt_ref, decay_ref, cols_ref, rows_ref, to_end_ref, from_start_ref, last_ref):
    raw = dt_ref[...].astype(F32)
    dt = jnp.maximum(raw, 0.0) + jnp.log1p(jnp.exp(-jnp.abs(raw)))
    step = dt * (-jnp.exp(decay_ref[...]))
    row = lax.broadcasted_iota(jnp.int32, (SPAN, SPAN), 0)
    col = lax.broadcasted_iota(jnp.int32, (SPAN, SPAN), 1)
    tri = jnp.where(row >= col, 1.0, 0.0).astype(F32)
    cum = jnp.dot(tri, step, precision=lax.Precision.HIGHEST, preferred_element_type=F32)
    last = cum[SPAN - 1 :, :]
    last_ref[...] = last
    rows_ref[...] = jnp.transpose((cum - jnp.log(dt)) * LOG2E)
    to_end = jnp.exp(last - cum) * dt
    from_start = jnp.exp(cum)
    scaled = cum * LOG2E
    for group in range(G):
        lo = group * HEADS
        cols_ref[group] = scaled[:, lo : lo + HEADS]
        for value, ref in ((to_end, to_end_ref), (from_start, from_start_ref)):
            part = value[:, lo : lo + HEADS]
            high = part.astype(BF16)
            low = (part - high.astype(F32)).astype(BF16)
            ref[group] = jnp.concatenate([high, low], axis=1)


def time_steps(dt_input, decay_log):
    return pl.pallas_call(
        steps_body,
        out_shape=(
            jax.ShapeDtypeStruct((G, SPAN, HEADS), F32),
            jax.ShapeDtypeStruct((H, SPAN), F32),
            jax.ShapeDtypeStruct((G, SPAN, 2 * HEADS), BF16),
            jax.ShapeDtypeStruct((G, SPAN, 2 * HEADS), BF16),
            jax.ShapeDtypeStruct((1, H), F32),
        ),
        compiler_params=params(),
        cost_estimate=cost(2.0, 1 << 20),
        name="time_steps",
    )(dt_input, decay_log.reshape(1, H))


def convolved(ref, rim_ref, kernel_ref, scratch):
    kernel = kernel_ref[...].astype(F32) * 0.5
    width = ref.shape[1]
    parts = []
    for lo in range(0, width, 128):
        sl = slice(lo, lo + 128)
        scratch[PAD - RIM : PAD, :] = rim_ref[:, sl].astype(F32)
        scratch[PAD : PAD + SPAN, :] = ref[:, sl].astype(F32)
        half = kernel[RIM : RIM + 1, sl] * scratch[PAD : PAD + SPAN, :]
        for tap in range(RIM):
            first = PAD - RIM + tap
            half = half + kernel[tap : tap + 1, sl] * scratch[first : first + SPAN, :]
        parts.append((half + half * jnp.tanh(half)).astype(BF16))
    return parts


def states_body(
    side_ref,
    x_ref,
    b_ref,
    c_ref,
    rim_x_ref,
    rim_b_ref,
    rim_c_ref,
    kernel_x_ref,
    kernel_b_ref,
    kernel_c_ref,
    to_end_ref,
    spread_ref,
    values_ref,
    conv_b_ref,
    conv_c_ref,
    keep_ref,
    send_ref,
    scratch,
):
    (conv_b,) = convolved(b_ref, rim_b_ref, kernel_b_ref, scratch)
    (conv_c,) = convolved(c_ref, rim_c_ref, kernel_c_ref, scratch)
    conv_b_ref[...] = conv_b
    conv_c_ref[...] = conv_c
    parts = convolved(x_ref, rim_x_ref, kernel_x_ref, scratch)
    for at, part in enumerate(parts):
        values_ref[:, at * 128 : (at + 1) * 128] = part
    gain = jnp.dot(to_end_ref[0], spread_ref[...], preferred_element_type=F32)
    weighted = (values_ref[...].astype(F32) * gain).astype(BF16)
    state = lax.dot_general(
        conv_b, weighted, (((0,), (0,)), ((), ())), preferred_element_type=F32
    ).astype(BF16)
    upper = side_ref[0] == 1
    top, bottom = state[:HALF], state[HALF:]

    @pl.when(upper)
    def _():
        keep_ref[0] = bottom
        send_ref[0] = top

    @pl.when(jnp.logical_not(upper))
    def _():
        keep_ref[0] = top
        send_ref[0] = bottom


def end_states(first, count, side, x, b, c, rim, conv_weight, to_end, spread):
    def cols(offset):
        return lambda i: (0, offset + first + i)

    def own(i):
        return (0, i)

    def lead(i):
        return (first + i, 0, 0)

    def lead_own(i):
        return (i, 0, 0)

    b_at, c_at = H * P_SIZE // N, H * P_SIZE // N + G
    return pl.pallas_call(
        states_body,
        grid=(count,),
        in_specs=[
            pl.BlockSpec(memory_space=pltpu.SMEM),
            pl.BlockSpec((SPAN, COLS), cols(0)),
            pl.BlockSpec((SPAN, N), cols(0)),
            pl.BlockSpec((SPAN, N), cols(0)),
            pl.BlockSpec((RIM, COLS), cols(0)),
            pl.BlockSpec((RIM, N), cols(b_at)),
            pl.BlockSpec((RIM, N), cols(c_at)),
            pl.BlockSpec((KERNEL_TAPS, COLS), cols(0)),
            pl.BlockSpec((KERNEL_TAPS, N), cols(b_at)),
            pl.BlockSpec((KERNEL_TAPS, N), cols(c_at)),
            pl.BlockSpec((1, SPAN, 2 * HEADS), lead),
            pl.BlockSpec((2 * HEADS, COLS), lambda i: (0, 0)),
        ],
        out_specs=[
            pl.BlockSpec((SPAN, COLS), own),
            pl.BlockSpec((SPAN, N), own),
            pl.BlockSpec((SPAN, N), own),
            pl.BlockSpec((1, HALF, COLS), lead_own),
            pl.BlockSpec((1, HALF, COLS), lead_own),
        ],
        out_shape=[
            jax.ShapeDtypeStruct((SPAN, count * COLS), BF16),
            jax.ShapeDtypeStruct((SPAN, count * N), BF16),
            jax.ShapeDtypeStruct((SPAN, count * N), BF16),
            jax.ShapeDtypeStruct((count, HALF, COLS), BF16),
            jax.ShapeDtypeStruct((count, HALF, COLS), BF16),
        ],
        scratch_shapes=[pltpu.VMEM((PAD + SPAN, 128), F32)],
        compiler_params=params(),
        cost_estimate=cost(1.2 * count, count << 20),
        name="end_states",
    )(side, x, b, c, rim, rim, rim, conv_weight, conv_weight, conv_weight, to_end, spread)


def inside_body(values_ref, b_ref, c_ref, cols_ref, rows_ref, skip_ref, part_ref):
    half = SPAN // 2
    scores = lax.dot_general(
        c_ref[...], b_ref[...], (((1,), (1,)), ((), ())), preferred_element_type=F32
    )
    row = lax.broadcasted_iota(jnp.int32, (half, half), 0)
    col = lax.broadcasted_iota(jnp.int32, (half, half), 1)
    causal = row >= col
    lane = lax.broadcasted_iota(jnp.int32, (half, 2 * P_SIZE), 1)
    first_head = lane < P_SIZE
    cols = cols_ref[0]
    rows = rows_ref[...]
    corner, below, later = scores[:half, :half], scores[half:, :half], scores[half:, half:]
    for pair in range(HEADS // 2):
        upper, lower = [], []
        for head in (2 * pair, 2 * pair + 1):
            at_t = cols[:, head : head + 1]
            at_s = rows[head : head + 1, :]
            e = jnp.exp2(at_t[:half] - at_s[:, :half])
            upper.append(jnp.where(causal, corner * e, 0.0).astype(BF16))
            e = jnp.exp2(at_t[half:] - at_s[:, :half])
            left = (below * e).astype(BF16)
            e = jnp.exp2(at_t[half:] - at_s[:, half:])
            right = jnp.where(causal, later * e, 0.0).astype(BF16)
            lower.append(jnp.concatenate([left, right], axis=1))
        sl = slice(pair * 2 * P_SIZE, (pair + 1) * 2 * P_SIZE)
        values = values_ref[:, sl]
        skip = skip_ref[:, sl]
        for lo, mix, depth in ((0, upper, half), (half, lower, SPAN)):
            both = jnp.dot(
                jnp.concatenate(mix, axis=0), values[:depth], preferred_element_type=F32
            )
            inside = jnp.where(first_head, both[:half], both[half:])
            part_ref[lo : lo + half, sl] = inside + skip * values[lo : lo + half].astype(F32)


def inside_block(first, count, values, conv_b, conv_c, cols, rows, skip):
    def own(i):
        return (0, i)

    return pl.pallas_call(
        inside_body,
        grid=(count,),
        in_specs=[
            pl.BlockSpec((SPAN, COLS), own),
            pl.BlockSpec((SPAN, N), own),
            pl.BlockSpec((SPAN, N), own),
            pl.BlockSpec((1, SPAN, HEADS), lambda i: (first + i, 0, 0)),
            pl.BlockSpec((HEADS, SPAN), lambda i: (first + i, 0)),
            pl.BlockSpec((1, COLS), lambda i: (0, first + i)),
        ],
        out_specs=pl.BlockSpec((SPAN, COLS), own),
        out_shape=jax.ShapeDtypeStruct((SPAN, count * COLS), F32),
        compiler_params=params(),
        cost_estimate=cost(1.6 * count, count << 20),
        name="inside_block",
    )(values, conv_b, conv_c, cols, rows, skip)


def carried_body(*refs):
    side_ref, c_ref, part_ref, keep_ref, got_ref, from_start_ref, spread_ref = refs[:7]
    out_ref = refs[-1]
    upper = side_ref[0] == 1
    keep, got = keep_ref[0], got_ref[0]
    carry = jnp.concatenate(
        [jnp.where(upper, got, keep), jnp.where(upper, keep, got)], axis=0
    )
    gain = jnp.dot(from_start_ref[0], spread_ref[...], preferred_element_type=F32)
    carried = jnp.dot(c_ref[...], carry, preferred_element_type=F32)
    out_ref[...] = (part_ref[...] + carried * gain).astype(BF16)


def with_carry(first, count, side, conv_c, part, keep, got, from_start, spread, out):
    def own(i):
        return (0, i)

    def lead_own(i):
        return (i, 0, 0)

    given = [] if out is None else [out]
    return pl.pallas_call(
        carried_body,
        grid=(count,),
        in_specs=[
            pl.BlockSpec(memory_space=pltpu.SMEM),
            pl.BlockSpec((SPAN, N), own),
            pl.BlockSpec((SPAN, COLS), own),
            pl.BlockSpec((1, HALF, COLS), lead_own),
            pl.BlockSpec((1, HALF, COLS), lead_own),
            pl.BlockSpec((1, SPAN, 2 * HEADS), lambda i: (first + i, 0, 0)),
            pl.BlockSpec((2 * HEADS, COLS), lambda i: (0, 0)),
        ]
        + [pl.BlockSpec(memory_space=pl.ANY)] * len(given),
        out_specs=pl.BlockSpec((SPAN, COLS), lambda i: (0, first + i)),
        out_shape=jax.ShapeDtypeStruct((SPAN, H * P_SIZE), BF16),
        input_output_aliases={7: 0} if given else {},
        compiler_params=params(),
        cost_estimate=cost(0.7 * count, count << 20),
        name="with_carry",
    )(side, conv_c, part, keep, got, from_start, spread, *given)


def swap(value, axis, pairs):
    both = [(a, b) for a, b in pairs] + [(b, a) for a, b in pairs]
    return lax.ppermute(value, axis, both)


def gathered_logs(last, y_pairs, z_pairs, far_pairs):
    at = lax.axis_index("inner")
    rows = last
    for bit, pairs in ((1, y_pairs), (2, z_pairs), (4, far_pairs)):
        other = swap(rows, "inner", pairs)
        low = (at & bit) == 0
        rows = jnp.concatenate(
            [jnp.where(low, rows, other), jnp.where(low, other, rows)], axis=0
        )
    other = swap(rows, "outer", [(0, 1)])
    low = lax.axis_index("outer") == 0
    return jnp.stack([jnp.where(low, rows, other), jnp.where(low, other, rows)])


def enter_by_swaps(last, kept, sent):
    size = lax.axis_size("inner")
    y_pairs = [(i, i + 1) for i in range(0, size, 2)]
    z_pairs = [(i, i + 2) for i in range(size) if i & 2 == 0]
    mid_pairs = [(2, 4), (3, 5)]
    far_pairs = [(i, i + 4) for i in range(4)]
    at, core = lax.axis_index("inner"), lax.axis_index("outer")
    y, z = at & 1, at >> 1
    odd, high, upper = (z & 1) == 1, z >= 2, y == 1
    logs = gathered_logs(last, y_pairs, z_pairs, far_pairs)
    mine = jnp.where(core == 0, logs[0], logs[1])
    index = jnp.arange(size)
    chip = index // 2

    def decay(mask):
        return jnp.exp(jnp.sum(jnp.where(mask[:, None], mine, 0.0), axis=0))

    pair_top = (z & 2) + 1
    weights = jnp.stack(
        [
            decay(index == 2 * z + 1),
            decay(chip == pair_top),
            jnp.where(high, decay((chip >= 2) & (chip < z)), 0.0),
            decay((chip >= 2) & jnp.logical_not(high)),
            decay((chip >= 2) & high),
            jnp.where(core == 1, decay(chip < z), 0.0),
            decay(index == 2 * z),
        ]
    )
    weights = jnp.repeat(weights, P_SIZE, axis=1).reshape(7, G, 1, COLS)
    entered = []
    first = 0
    for keep, send in zip(kept, sent):
        count = keep.shape[0]
        w = weights[:, first : first + count]
        got = swap(send, "inner", y_pairs).astype(F32)
        own = keep.astype(F32)
        below = jnp.where(upper, got, own)
        above = jnp.where(upper, own, got)
        chip_state = (below * w[0] + above).astype(BF16)
        got = swap(chip_state, "inner", z_pairs)
        low_chip = jnp.where(odd, got, chip_state).astype(F32)
        high_chip = jnp.where(odd, chip_state, got).astype(F32)
        two_chips = (low_chip * w[1] + high_chip).astype(BF16)
        got = swap(two_chips, "inner", mid_pairs)
        further = swap(got, "inner", z_pairs)
        inner_chip = odd != high
        others = jnp.where(inner_chip, got, further).astype(F32)
        ahead = others * w[2] + jnp.where(odd, low_chip, 0.0)
        total = (two_chips.astype(F32) * w[3] + others * w[4]).astype(BF16)
        before = swap(total, "outer", [(0, 1)]).astype(F32)
        entering = ahead + before * w[5]
        entering_above = entering * w[6] + below
        stay = jnp.where(upper, entering_above, entering).astype(BF16)
        leave = jnp.where(upper, entering, entering_above).astype(BF16)
        entered.append((stay, swap(leave, "inner", y_pairs)))
        first += count
    return entered


def combine(earlier, later):
    return (earlier[0] * later[0], later[0][:, None, :] * earlier[1] + later[1])


def enter_by_all_to_all(last, kept, sent):
    size = lax.axis_size("inner")
    upper = (lax.axis_index("inner") & 1) == 1
    keep, send = jnp.concatenate(kept), jnp.concatenate(sent)
    halves = [jnp.where(upper, send, keep), jnp.where(upper, keep, send)]
    wide = 2 * P_SIZE
    pairs = H // 2
    state = jnp.concatenate(halves, axis=1).reshape(G, N, pairs // G, wide)
    state = jnp.swapaxes(state, 1, 2).reshape(pairs, N, wide)
    decay = jnp.repeat(jnp.exp(last[0]), P_SIZE).reshape(pairs, wide)

    def spread(a):
        return lax.all_to_all(a[None], "inner", split_axis=1, concat_axis=0, tiled=True)

    decays, states = spread(decay), spread(state).astype(F32)
    run = (jnp.ones_like(decays[0]), jnp.zeros_like(states[0]))

    def lap(run, item):
        return combine(run, item), run

    total, before = lax.scan(lap, run, (decays, states))
    first = lax.ppermute(total[1].astype(BF16), "outer", [(0, 1)]).astype(F32)
    entering = before[0][:, :, None, :] * first[None] + before[1]
    carry = lax.all_to_all(
        entering.astype(BF16), "inner", split_axis=0, concat_axis=1, tiled=True
    )[0]
    carry = carry.reshape(G, pairs // G, N, wide)
    carry = jnp.swapaxes(carry, 1, 2).reshape(G, N, COLS)
    top, bottom = carry[:, :HALF], carry[:, HALF:]
    stay, got = jnp.where(upper, bottom, top), jnp.where(upper, top, bottom)
    entered = []
    at = 0
    for keep in kept:
        count = keep.shape[0]
        entered.append((stay[at : at + count], got[at : at + count]))
        at += count
    return entered


def shards(x_stream, b_stream, c_stream, dt_input, decay_log, skip_weight, conv_weight):
    tokens = x_stream.shape[0]
    rim_rows = jnp.concatenate(
        [a[tokens - RIM :] for a in (x_stream, b_stream, c_stream)], axis=1
    )
    devices = lax.axis_size("outer") * lax.axis_size("inner")
    rim = lax.ppermute(
        rim_rows, ("outer", "inner"), [(i, i + 1) for i in range(devices - 1)]
    )
    cols, rows, to_end, from_start, last = time_steps(dt_input, decay_log)
    heads = jnp.arange(2 * HEADS)[:, None] % HEADS
    spread = (jnp.arange(COLS)[None, :] // P_SIZE == heads).astype(BF16)
    skip = jnp.repeat(skip_weight, P_SIZE)[None, :]
    side = (lax.axis_index("inner") & 1).astype(jnp.int32).reshape(1)
    local = []
    first = 0
    for count in CHUNKS:
        local.append(
            end_states(
                first,
                count,
                side,
                x_stream,
                b_stream,
                c_stream,
                rim,
                conv_weight,
                to_end,
                spread,
            )
        )
        first += count
    by_swaps = lax.axis_size("inner") == 8 and lax.axis_size("outer") == 2
    enter = enter_by_swaps if by_swaps else enter_by_all_to_all
    entered = enter(last, [a[3] for a in local], [a[4] for a in local])
    out = None
    first = 0
    for count, (values, conv_b, conv_c, _, _), (keep, got) in zip(CHUNKS, local, entered):
        part = inside_block(first, count, values, conv_b, conv_c, cols, rows, skip)
        out = with_carry(
            first, count, side, conv_c, part, keep, got, from_start, spread, out
        )
        first += count
    return out


def solution(mesh):
    return jax.shard_map(
        shards,
        mesh=mesh,
        in_specs=(
            P(("slab", "outer", "inner"), None),
            P(("slab", "outer", "inner"), None),
            P(("slab", "outer", "inner"), None),
            P(("slab", "outer", "inner"), None),
            P("slab"),
            P(),
            P(),
        ),
        out_specs=P(("slab", "outer", "inner"), None),
        check_vma=False,
    )
```

profile of v0, /device:TPU:0, one launch (start us, length us, event | category | flops | bytes accessed | tf_op | source)
XLA Modules:
  0.0 127.8 jit_solution(975054512391870195)
XLA Ops:
  2.5 4.9 %collective-permute-start = (bf16[3,10240]{1,0:T(4,128)(2,1)S(1)}, bf16[3,10240]{1,0:T(4,128)(2,1)S(1)}, u32[]{:S(2)}, u32[]{:S(2)}) collective-permute-start(bf16[3,10240]{1,0:T(4,128)(2,1)S(1)} %pad_maximum_fusion), channel_id=1, source_target_pairs={{0,1},{1,2},{2,3},{3,4},{4,5},{5,6},{6,7},{7,8},{8,9},{9,10},{10,1... | collective-permute-start | bytes 184328 | tf_op jit(solution)/shard_map/ppermute | solution.py:419
  13.4 1.9 %collective-permute-done.2 = f32[1,128]{1,0:T(1,128)S(1)} collective-permute-done((f32[1,128]{1,0:T(1,128)S(1)}, f32[1,128]{1,0:T(1,128)S(1)}, u32[]{:S(2)}, u32[]{:S(2)}) %collective-permute-start.2) | collective-permute-done | bytes 544 | tf_op jit(solution)/shard_map/ppermute | solution.py:293
  15.3 1.6 %collective-permute-start.3 = (f32[2,128]{1,0:T(2,128)S(1)}, f32[2,128]{1,0:T(2,128)S(1)}, u32[]{:S(2)}, u32[]{:S(2)}) collective-permute-start(f32[2,128]{1,0:T(2,128)S(1)} %pad_maximum_fusion.3), channel_id=1, source_target_pairs={{0,2},{1,3},{4,6},{5,7},{2,0},{3,1},{6,4},{7,5},{8,10},{9,11},{12,... | collective-permute-start | bytes 3080 | tf_op jit(solution)/shard_map/ppermute | solution.py:293
  17.0 2.0 %collective-permute-done.3 = f32[2,128]{1,0:T(2,128)S(1)} collective-permute-done((f32[2,128]{1,0:T(2,128)S(1)}, f32[2,128]{1,0:T(2,128)S(1)}, u32[]{:S(2)}, u32[]{:S(2)}) %collective-permute-start.3) | collective-permute-done | bytes 1056 | tf_op jit(solution)/shard_map/ppermute | solution.py:293
  19.0 2.7 %collective-permute-start.4 = (f32[4,128]{1,0:T(4,128)S(1)}, f32[4,128]{1,0:T(4,128)S(1)}, u32[]{:S(2)}, u32[]{:S(2)}) collective-permute-start(f32[4,128]{1,0:T(4,128)S(1)} %pad_maximum_fusion.2), channel_id=1, source_target_pairs={{0,4},{1,5},{2,6},{3,7},{4,0},{5,1},{6,2},{7,3},{8,12},{9,13},{10,... | collective-permute-start | bytes 6152 | tf_op jit(solution)/shard_map/ppermute | solution.py:293
  21.6 1.9 %collective-permute-done.4 = f32[4,128]{1,0:T(4,128)S(1)} collective-permute-done((f32[4,128]{1,0:T(4,128)S(1)}, f32[4,128]{1,0:T(4,128)S(1)}, u32[]{:S(2)}, u32[]{:S(2)}) %collective-permute-start.4) | collective-permute-done | bytes 2080 | tf_op jit(solution)/shard_map/ppermute | solution.py:293
  25.5 3.5 %end_states.7 = (bf16[256,2048]{1,0:T(8,128)(2,1)S(1)}, bf16[256,256]{1,0:T(8,128)(2,1)S(1)}, bf16[256,256]{1,0:T(8,128)(2,1)S(1)}, bf16[2,64,1024]{2,1,0:T(8,128)(2,1)S(1)}, bf16[2,64,1024]{2,1,0:T(8,128)(2,1)S(1)}) custom-call(s32[1]{0:T(128)} %bitcast.side_ref.refs_0_, bf16[256,8192]{1,0:T(8,128)(2,1)} %x_ref.7, bf16[256,1024]{1,0:T(8,128)(2,1)S(1)} %copy-done.1, ...), custom_call_target="tpu_custom_call" | custom-call | flops 1440000000 | bytes 2097152 | tf_op jit(solution)/shard_map/end_states/pallas_call | solution.py:151
  30.6 3.5 %end_states.6 = (bf16[256,2048]{1,0:T(8,128)(2,1)S(1)}, bf16[256,256]{1,0:T(8,128)(2,1)S(1)}, bf16[256,256]{1,0:T(8,128)(2,1)S(1)}, bf16[2,64,1024]{2,1,0:T(8,128)(2,1)S(1)}, bf16[2,64,1024]{2,1,0:T(8,128)(2,1)S(1)}) custom-call(s32[1]{0:T(128)} %bitcast.side_ref.refs_0_, bf16[256,8192]{1,0:T(8,128)(2,1)} %x_ref.7, bf16[256,1024]{1,0:T(8,128)(2,1)S(1)} %copy-done.1, ...), custom_call_target="tpu_custom_call" | custom-call | flops 1440000000 | bytes 2097152 | tf_op jit(solution)/shard_map/end_states/pallas_call | solution.py:151
  34.7 3.5 %end_states.5 = (bf16[256,2048]{1,0:T(8,128)(2,1)S(1)}, bf16[256,256]{1,0:T(8,128)(2,1)S(1)}, bf16[256,256]{1,0:T(8,128)(2,1)S(1)}, bf16[2,64,1024]{2,1,0:T(8,128)(2,1)S(1)}, bf16[2,64,1024]{2,1,0:T(8,128)(2,1)S(1)}) custom-call(s32[1]{0:T(128)} %bitcast.side_ref.refs_0_, bf16[256,8192]{1,0:T(8,128)(2,1)} %x_ref.7, bf16[256,1024]{1,0:T(8,128)(2,1)S(1)} %copy-done.1, ...), custom_call_target="tpu_custom_call" | custom-call | flops 1440000000 | bytes 2097152 | tf_op jit(solution)/shard_map/end_states/pallas_call | solution.py:151
  39.9 3.5 %end_states.4 = (bf16[256,2048]{1,0:T(8,128)(2,1)S(1)}, bf16[256,256]{1,0:T(8,128)(2,1)S(1)}, bf16[256,256]{1,0:T(8,128)(2,1)S(1)}, bf16[2,64,1024]{2,1,0:T(8,128)(2,1)S(1)}, bf16[2,64,1024]{2,1,0:T(8,128)(2,1)S(1)}) custom-call(s32[1]{0:T(128)} %bitcast.side_ref.refs_0_, bf16[256,8192]{1,0:T(8,128)(2,1)} %x_ref.7, bf16[256,1024]{1,0:T(8,128)(2,1)S(1)} %copy-done.1, ...), custom_call_target="tpu_custom_call" | custom-call | flops 1440000000 | bytes 2097152 | tf_op jit(solution)/shard_map/end_states/pallas_call | solution.py:151
  44.0 2.2 %inside_block.7.refs_2_ = f32[256,2048]{1,0:T(8,128)S(1)} custom-call(bf16[256,2048]{1,0:T(8,128)(2,1)S(1)} %get-tuple-element.51.values_ref, bf16[256,256]{1,0:T(8,128)(2,1)S(1)} %get-tuple-element.52.b_ref, bf16[256,256]{1,0:T(8,128)(2,1)S(1)} %get-tuple-element.50.c_ref.refs_1_, f32[8,256,16]{2,1,0:T(8,128)S(1)} %copy-done.6, f32[128,256]{1,0:T(8,128)S(1)} %copy-done.8, ...), custom_call_target="tpu_custom_call" | custom-call | flops 1920000000 | bytes 2097152 | tf_op jit(solution)/shard_map/inside_block/pallas_call | solution.py:229
  46.3 1.6 %collective-permute-start.24 = (bf16[2,64,1024]{2,1,0:T(8,128)(2,1)S(1)}, bf16[2,64,1024]{2,1,0:T(8,128)(2,1)S(1)}, u32[]{:S(2)}, u32[]{:S(2)}) collective-permute-start(bf16[2,64,1024]{2,1,0:T(8,128)(2,1)S(1)} %fusion.25), channel_id=1, source_target_pairs={{0,2},{1,3},{4,6},{5,7},{2,0},{3,1},{6,4},{7,5},{8,10},{9,11},{12,... | collective-permute-start | bytes 786440 | tf_op jit(solution)/shard_map/ppermute | solution.py:293
  51.2 3.2 %collective-permute-done.1 = bf16[2,64,1024]{2,1,0:T(8,128)(2,1)S(1)} collective-permute-done((bf16[2,64,1024]{2,1,0:T(8,128)(2,1)S(1)}, bf16[2,64,1024]{2,1,0:T(8,128)(2,1)S(1)}, u32[]{:S(2)}, u32[]{:S(2)}) %collective-permute-start.1) | collective-permute-done | bytes 262176 | tf_op jit(solution)/shard_map/ppermute | solution.py:293
  57.0 4.2 %collective-permute-done.18 = bf16[2,64,1024]{2,1,0:T(8,128)(2,1)S(1)} collective-permute-done((bf16[2,64,1024]{2,1,0:T(8,128)(2,1)S(1)}, bf16[2,64,1024]{2,1,0:T(8,128)(2,1)S(1)}, u32[]{:S(2)}, u32[]{:S(2)}) %collective-permute-start.18) | collective-permute-done | bytes 262176 | tf_op jit(solution)/shard_map/ppermute | solution.py:293
  62.2 4.7 %collective-permute-done.12 = bf16[2,64,1024]{2,1,0:T(8,128)(2,1)S(1)} collective-permute-done((bf16[2,64,1024]{2,1,0:T(8,128)(2,1)S(1)}, bf16[2,64,1024]{2,1,0:T(8,128)(2,1)S(1)}, u32[]{:S(2)}, u32[]{:S(2)}) %collective-permute-start.12) | collective-permute-done | bytes 262176 | tf_op jit(solution)/shard_map/ppermute | solution.py:293
  68.4 2.1 %collective-permute-done.6 = bf16[2,64,1024]{2,1,0:T(8,128)(2,1)S(1)} collective-permute-done((bf16[2,64,1024]{2,1,0:T(8,128)(2,1)S(1)}, bf16[2,64,1024]{2,1,0:T(8,128)(2,1)S(1)}, u32[]{:S(2)}, u32[]{:S(2)}) %collective-permute-start.6) | collective-permute-done | bytes 262176 | tf_op jit(solution)/shard_map/ppermute | solution.py:293
  72.3 4.4 %collective-permute-start.26 = (bf16[2,64,1024]{2,1,0:T(8,128)(2,1)S(1)}, bf16[2,64,1024]{2,1,0:T(8,128)(2,1)S(1)}, u32[]{:S(2)}, u32[]{:S(2)}) collective-permute-start(bf16[2,64,1024]{2,1,0:T(8,128)(2,1)S(1)} %collective-permute-done.25), channel_id=1, source_target_pairs={{0,2},{1,3},{4,6},{5,7},{2,0},{3,1},{6,4},{7,5},{8,10},{9,11},{12,... | collective-permute-start | bytes 786440 | tf_op jit(solution)/shard_map/ppermute | solution.py:293
  76.8 2.2 %inside_block.6.refs_2_ = f32[256,2048]{1,0:T(8,128)S(1)} custom-call(bf16[256,2048]{1,0:T(8,128)(2,1)S(1)} %get-tuple-element.46.values_ref, bf16[256,256]{1,0:T(8,128)(2,1)S(1)} %get-tuple-element.47.b_ref, bf16[256,256]{1,0:T(8,128)(2,1)S(1)} %get-tuple-element.45.c_ref.refs_1_, f32[8,256,16]{2,1,0:T(8,128)S(1)} %copy-done.6, f32[128,256]{1,0:T(8,128)S(1)} %copy-done.8, ...), custom_call_target="tpu_custom_call" | custom-call | flops 1920000000 | bytes 2097152 | tf_op jit(solution)/shard_map/inside_block/pallas_call | solution.py:229
  79.1 2.2 %inside_block.5.refs_2_ = f32[256,2048]{1,0:T(8,128)S(1)} custom-call(bf16[256,2048]{1,0:T(8,128)(2,1)S(1)} %get-tuple-element.41.values_ref, bf16[256,256]{1,0:T(8,128)(2,1)S(1)} %get-tuple-element.42.b_ref, bf16[256,256]{1,0:T(8,128)(2,1)S(1)} %get-tuple-element.40.c_ref.refs_1_, f32[8,256,16]{2,1,0:T(8,128)S(1)} %copy-done.6, f32[128,256]{1,0:T(8,128)S(1)} %copy-done.8, ...), custom_call_target="tpu_custom_call" | custom-call | flops 1920000000 | bytes 2097152 | tf_op jit(solution)/shard_map/inside_block/pallas_call | solution.py:229
  81.2 2.1 %collective-permute-start.14 = (bf16[2,64,1024]{2,1,0:T(8,128)(2,1)S(1)}, bf16[2,64,1024]{2,1,0:T(8,128)(2,1)S(1)}, u32[]{:S(2)}, u32[]{:S(2)}) collective-permute-start(bf16[2,64,1024]{2,1,0:T(8,128)(2,1)S(1)} %collective-permute-done.13), channel_id=1, source_target_pairs={{0,2},{1,3},{4,6},{5,7},{2,0},{3,1},{6,4},{7,5},{8,10},{9,11},{12,... | collective-permute-start | bytes 786440 | tf_op jit(solution)/shard_map/ppermute | solution.py:293
  84.9 4.2 %collective-permute-done.20 = bf16[2,64,1024]{2,1,0:T(8,128)(2,1)S(1)} collective-permute-done((bf16[2,64,1024]{2,1,0:T(8,128)(2,1)S(1)}, bf16[2,64,1024]{2,1,0:T(8,128)(2,1)S(1)}, u32[]{:S(2)}, u32[]{:S(2)}) %collective-permute-start.20) | collective-permute-done | bytes 262176 | tf_op jit(solution)/shard_map/ppermute | solution.py:293
  89.4 5.0 %collective-permute-done.14 = bf16[2,64,1024]{2,1,0:T(8,128)(2,1)S(1)} collective-permute-done((bf16[2,64,1024]{2,1,0:T(8,128)(2,1)S(1)}, bf16[2,64,1024]{2,1,0:T(8,128)(2,1)S(1)}, u32[]{:S(2)}, u32[]{:S(2)}) %collective-permute-start.14) | collective-permute-done | bytes 262176 | tf_op jit(solution)/shard_map/ppermute | solution.py:293
  95.6 2.4 %collective-permute-done.8 = bf16[2,64,1024]{2,1,0:T(8,128)(2,1)S(1)} collective-permute-done((bf16[2,64,1024]{2,1,0:T(8,128)(2,1)S(1)}, bf16[2,64,1024]{2,1,0:T(8,128)(2,1)S(1)}, u32[]{:S(2)}, u32[]{:S(2)}) %collective-permute-start.8) | collective-permute-done | bytes 262176 | tf_op jit(solution)/shard_map/ppermute | solution.py:293
  105.7 2.2 %inside_block.4.refs_2_ = f32[256,2048]{1,0:T(8,128)S(1)} custom-call(bf16[256,2048]{1,0:T(8,128)(2,1)S(1)} %get-tuple-element.32.values_ref, bf16[256,256]{1,0:T(8,128)(2,1)S(1)} %get-tuple-element.33.b_ref, bf16[256,256]{1,0:T(8,128)(2,1)S(1)} %get-tuple-element.31.c_ref.refs_1_, f32[8,256,16]{2,1,0:T(8,128)S(1)} %copy-done.6, f32[128,256]{1,0:T(8,128)S(1)} %copy-done.8, ...), custom_call_target="tpu_custom_call" | custom-call | flops 1920000000 | bytes 2097152 | tf_op jit(solution)/shard_map/inside_block/pallas_call | solution.py:229
  107.9 1.7 %collective-permute-done.28.refs_4_ = bf16[2,64,1024]{2,1,0:T(8,128)(2,1)S(1)} collective-permute-done((bf16[2,64,1024]{2,1,0:T(8,128)(2,1)}, bf16[2,64,1024]{2,1,0:T(8,128)(2,1)S(1)}, u32[]{:S(2)}, u32[]{:S(2)}) %collective-permute-start.28) | collective-permute-done | bytes 262176 | tf_op jit(solution)/shard_map/ppermute | solution.py:293
  109.6 1.8 %with_carry.4.refs_7_ = bf16[256,8192]{1,0:T(8,128)(2,1)} custom-call(s32[1]{0:T(128)} %bitcast.side_ref.refs_0_, bf16[256,256]{1,0:T(8,128)(2,1)S(1)} %get-tuple-element.50.c_ref.refs_1_, f32[256,2048]{1,0:T(8,128)S(1)} %inside_block.7.refs_2_, bf16[2,64,1024]{2,1,0:T(8,128)(2,1)S(1)} %get-tuple-element.63.refs_3_, ...), custom_call_target="tpu_custom_call" | custom-call | flops 840000000 | bytes 2097152 | tf_op jit(solution)/shard_map/with_carry/pallas_call | solution.py:269
  111.4 3.8 %collective-permute-done.22.refs_4_ = bf16[2,64,1024]{2,1,0:T(8,128)(2,1)S(1)} collective-permute-done((bf16[2,64,1024]{2,1,0:T(8,128)(2,1)S(1)}, bf16[2,64,1024]{2,1,0:T(8,128)(2,1)S(1)}, u32[]{:S(2)}, u32[]{:S(2)}) %collective-permute-start.22) | collective-permute-done | bytes 262176 | tf_op jit(solution)/shard_map/ppermute | solution.py:293
  115.2 1.8 %with_carry.5.refs_7_ = bf16[256,8192]{1,0:T(8,128)(2,1)} custom-call(s32[1]{0:T(128)} %bitcast.side_ref.refs_0_, bf16[256,256]{1,0:T(8,128)(2,1)S(1)} %get-tuple-element.45.c_ref.refs_1_, f32[256,2048]{1,0:T(8,128)S(1)} %inside_block.6.refs_2_, bf16[2,64,1024]{2,1,0:T(8,128)(2,1)S(1)} %get-tuple-element.65.refs_3_, ...), custom_call_target="tpu_custom_call", output_to_operand_aliasing={{}: (7, {})} | custom-call | flops 840000000 | bytes 2097152 | tf_op jit(solution)/shard_map/with_carry/pallas_call | solution.py:269
  117.0 3.8 %collective-permute-done.16.refs_4_ = bf16[2,64,1024]{2,1,0:T(8,128)(2,1)S(1)} collective-permute-done((bf16[2,64,1024]{2,1,0:T(8,128)(2,1)S(1)}, bf16[2,64,1024]{2,1,0:T(8,128)(2,1)S(1)}, u32[]{:S(2)}, u32[]{:S(2)}) %collective-permute-start.16) | collective-permute-done | bytes 262176 | tf_op jit(solution)/shard_map/ppermute | solution.py:293
  120.8 1.8 %with_carry.6.refs_7_ = bf16[256,8192]{1,0:T(8,128)(2,1)} custom-call(s32[1]{0:T(128)} %bitcast.side_ref.refs_0_, bf16[256,256]{1,0:T(8,128)(2,1)S(1)} %get-tuple-element.40.c_ref.refs_1_, f32[256,2048]{1,0:T(8,128)S(1)} %inside_block.5.refs_2_, bf16[2,64,1024]{2,1,0:T(8,128)(2,1)S(1)} %get-tuple-element.67.refs_3_, ...), custom_call_target="tpu_custom_call", output_to_operand_aliasing={{}: (7, {})} | custom-call | flops 840000000 | bytes 2097152 | tf_op jit(solution)/shard_map/with_carry/pallas_call | solution.py:269
  122.6 3.4 %collective-permute-done.10.refs_4_ = bf16[2,64,1024]{2,1,0:T(8,128)(2,1)S(1)} collective-permute-done((bf16[2,64,1024]{2,1,0:T(8,128)(2,1)S(1)}, bf16[2,64,1024]{2,1,0:T(8,128)(2,1)S(1)}, u32[]{:S(2)}, u32[]{:S(2)}) %collective-permute-start.10) | collective-permute-done | bytes 262176 | tf_op jit(solution)/shard_map/ppermute | solution.py:293
  126.0 1.8 %with_carry.7 = bf16[256,8192]{1,0:T(8,128)(2,1)} custom-call(s32[1]{0:T(128)} %bitcast.side_ref.refs_0_, bf16[256,256]{1,0:T(8,128)(2,1)S(1)} %get-tuple-element.31.c_ref.refs_1_, f32[256,2048]{1,0:T(8,128)S(1)} %inside_block.4.refs_2_, bf16[2,64,1024]{2,1,0:T(8,128)(2,1)S(1)} %get-tuple-element.69.refs_3_, ...), custom_call_target="tpu_custom_call", output_to_operand_aliasing={{}: (7, {})} | custom-call | flops 840000000 | bytes 2097152 | tf_op jit(solution)/shard_map/with_carry/pallas_call | solution.py:269
  (113 shorter events, 35.5 us)
Async XLA Ops:
  0.0 25.5 %copy-start.1 = (bf16[256,1024]{1,0:T(8,128)(2,1)S(1)}, bf16[256,1024]{1,0:T(8,128)(2,1)}, u32[]{:S(2)}) copy-start(bf16[256,1024]{1,0:T(8,128)(2,1)} %b_ref.7) | copy-start | bytes 1572868
  0.0 25.5 %copy-start.2 = (bf16[256,1024]{1,0:T(8,128)(2,1)S(1)}, bf16[256,1024]{1,0:T(8,128)(2,1)}, u32[]{:S(2)}) copy-start(bf16[256,1024]{1,0:T(8,128)(2,1)} %c_ref.7) | copy-start | bytes 1572868
  0.0 25.5 %copy-start = (bf16[4,10240]{1,0:T(4,128)(2,1)S(1)}, bf16[4,10240]{1,0:T(4,128)(2,1)}, u32[]{:S(2)}) copy-start(bf16[4,10240]{1,0:T(4,128)(2,1)} %kernel_c_ref.7) | copy-start | bytes 245764
  2.5 22.9 %collective-permute-start = (bf16[3,10240]{1,0:T(4,128)(2,1)S(1)}, bf16[3,10240]{1,0:T(4,128)(2,1)S(1)}, u32[]{:S(2)}, u32[]{:S(2)}) collective-permute-start(bf16[3,10240]{1,0:T(4,128)(2,1)S(1)} %pad_maximum_fusion), channel_id=1, source_target_pairs={{0,1},{1,2},{2,3},{3,4},{4,5},{5,6},{6,7},{7,8},{8,9},{9,10},{10,1... | collective-permute-start | bytes 184328 | tf_op jit(solution)/shard_map/ppermute | solution.py:419
  11.8 3.5 %collective-permute-start.2 = (f32[1,128]{1,0:T(1,128)S(1)}, f32[1,128]{1,0:T(1,128)S(1)}, u32[]{:S(2)}, u32[]{:S(2)}) collective-permute-start(f32[1,128]{1,0:T(1,128)S(1)} %get-tuple-element.38), channel_id=1, source_target_pairs={{0,1},{2,3},{4,5},{6,7},{1,0},{3,2},{5,4},{7,6},{8,9},{10,11},{12,... | collective-permute-start | bytes 1544 | tf_op jit(solution)/shard_map/ppermute | solution.py:293
  15.3 3.6 %collective-permute-start.3 = (f32[2,128]{1,0:T(2,128)S(1)}, f32[2,128]{1,0:T(2,128)S(1)}, u32[]{:S(2)}, u32[]{:S(2)}) collective-permute-start(f32[2,128]{1,0:T(2,128)S(1)} %pad_maximum_fusion.3), channel_id=1, source_target_pairs={{0,2},{1,3},{4,6},{5,7},{2,0},{3,1},{6,4},{7,5},{8,10},{9,11},{12,... | collective-permute-start | bytes 3080 | tf_op jit(solution)/shard_map/ppermute | solution.py:293
  19.0 4.5 %collective-permute-start.4 = (f32[4,128]{1,0:T(4,128)S(1)}, f32[4,128]{1,0:T(4,128)S(1)}, u32[]{:S(2)}, u32[]{:S(2)}) collective-permute-start(f32[4,128]{1,0:T(4,128)S(1)} %pad_maximum_fusion.2), channel_id=1, source_target_pairs={{0,4},{1,5},{2,6},{3,7},{4,0},{5,1},{6,2},{7,3},{8,12},{9,13},{10,... | collective-permute-start | bytes 6152 | tf_op jit(solution)/shard_map/ppermute | solution.py:293
  23.5 1.2 collective-permute-start.5
  29.0 17.2 %collective-permute-start.23 = (bf16[2,64,1024]{2,1,0:T(8,128)(2,1)S(1)}, bf16[2,64,1024]{2,1,0:T(8,128)(2,1)S(1)}, u32[]{:S(2)}, u32[]{:S(2)}) collective-permute-start(bf16[2,64,1024]{2,1,0:T(8,128)(2,1)S(1)} %get-tuple-element.53), channel_id=1, source_target_pairs={{0,1},{2,3},{4,5},{6,7},{1,0},{3,2},{5,4},{7,6},{8,9},{10,11},{12,... | collective-permute-start | bytes 786440 | tf_op jit(solution)/shard_map/ppermute | solution.py:293
  34.2 13.8 %collective-permute-start.17 = (bf16[2,64,1024]{2,1,0:T(8,128)(2,1)S(1)}, bf16[2,64,1024]{2,1,0:T(8,128)(2,1)S(1)}, u32[]{:S(2)}, u32[]{:S(2)}) collective-permute-start(bf16[2,64,1024]{2,1,0:T(8,128)(2,1)S(1)} %get-tuple-element.48), channel_id=1, source_target_pairs={{0,1},{2,3},{4,5},{6,7},{1,0},{3,2},{5,4},{7,6},{8,9},{10,11},{12,... | collective-permute-start | bytes 786440 | tf_op jit(solution)/shard_map/ppermute | solution.py:293
  38.3 11.1 %collective-permute-start.11 = (bf16[2,64,1024]{2,1,0:T(8,128)(2,1)S(1)}, bf16[2,64,1024]{2,1,0:T(8,128)(2,1)S(1)}, u32[]{:S(2)}, u32[]{:S(2)}) collective-permute-start(bf16[2,64,1024]{2,1,0:T(8,128)(2,1)S(1)} %get-tuple-element.43), channel_id=1, source_target_pairs={{0,1},{2,3},{4,5},{6,7},{1,0},{3,2},{5,4},{7,6},{8,9},{10,11},{12,... | collective-permute-start | bytes 786440 | tf_op jit(solution)/shard_map/ppermute | solution.py:293
  43.4 10.9 %collective-permute-start.1 = (bf16[2,64,1024]{2,1,0:T(8,128)(2,1)S(1)}, bf16[2,64,1024]{2,1,0:T(8,128)(2,1)S(1)}, u32[]{:S(2)}, u32[]{:S(2)}) collective-permute-start(bf16[2,64,1024]{2,1,0:T(8,128)(2,1)S(1)} %get-tuple-element.36), channel_id=1, source_target_pairs={{0,1},{2,3},{4,5},{6,7},{1,0},{3,2},{5,4},{7,6},{8,9},{10,11},{12,... | collective-permute-start | bytes 786440 | tf_op jit(solution)/shard_map/ppermute | solution.py:293
  46.3 9.8 %collective-permute-start.24 = (bf16[2,64,1024]{2,1,0:T(8,128)(2,1)S(1)}, bf16[2,64,1024]{2,1,0:T(8,128)(2,1)S(1)}, u32[]{:S(2)}, u32[]{:S(2)}) collective-permute-start(bf16[2,64,1024]{2,1,0:T(8,128)(2,1)S(1)} %fusion.25), channel_id=1, source_target_pairs={{0,2},{1,3},{4,6},{5,7},{2,0},{3,1},{6,4},{7,5},{8,10},{9,11},{12,... | collective-permute-start | bytes 786440 | tf_op jit(solution)/shard_map/ppermute | solution.py:293
  48.1 13.2 %collective-permute-start.18 = (bf16[2,64,1024]{2,1,0:T(8,128)(2,1)S(1)}, bf16[2,64,1024]{2,1,0:T(8,128)(2,1)S(1)}, u32[]{:S(2)}, u32[]{:S(2)}) collective-permute-start(bf16[2,64,1024]{2,1,0:T(8,128)(2,1)S(1)} %fusion.17), channel_id=1, source_target_pairs={{0,2},{1,3},{4,6},{5,7},{2,0},{3,1},{6,4},{7,5},{8,10},{9,11},{12,... | collective-permute-start | bytes 786440 | tf_op jit(solution)/shard_map/ppermute | solution.py:293
  49.5 17.3 %collective-permute-start.12 = (bf16[2,64,1024]{2,1,0:T(8,128)(2,1)S(1)}, bf16[2,64,1024]{2,1,0:T(8,128)(2,1)S(1)}, u32[]{:S(2)}, u32[]{:S(2)}) collective-permute-start(bf16[2,64,1024]{2,1,0:T(8,128)(2,1)S(1)} %fusion.9), channel_id=1, source_target_pairs={{0,2},{1,3},{4,6},{5,7},{2,0},{3,1},{6,4},{7,5},{8,10},{9,11},{12,... | collective-permute-start | bytes 786440 | tf_op jit(solution)/shard_map/ppermute | solution.py:293
  54.5 16.1 %collective-permute-start.6 = (bf16[2,64,1024]{2,1,0:T(8,128)(2,1)S(1)}, bf16[2,64,1024]{2,1,0:T(8,128)(2,1)S(1)}, u32[]{:S(2)}, u32[]{:S(2)}) collective-permute-start(bf16[2,64,1024]{2,1,0:T(8,128)(2,1)S(1)} %fusion.1), channel_id=1, source_target_pairs={{0,2},{1,3},{4,6},{5,7},{2,0},{3,1},{6,4},{7,5},{8,10},{9,11},{12,... | collective-permute-start | bytes 786440 | tf_op jit(solution)/shard_map/ppermute | solution.py:293
  56.3 16.0 %collective-permute-start.25 = (bf16[2,64,1024]{2,1,0:T(8,128)(2,1)S(1)}, bf16[2,64,1024]{2,1,0:T(8,128)(2,1)S(1)}, u32[]{:S(2)}, u32[]{:S(2)}) collective-permute-start(bf16[2,64,1024]{2,1,0:T(8,128)(2,1)S(1)} %fusion.27), channel_id=1, source_target_pairs={{2,4},{3,5},{4,2},{5,3},{10,12},{11,13},{12,10},{13,11},{18,20},{1... | collective-permute-start | bytes 786440 | tf_op jit(solution)/shard_map/ppermute | solution.py:293
  61.5 17.5 %collective-permute-start.19 = (bf16[2,64,1024]{2,1,0:T(8,128)(2,1)S(1)}, bf16[2,64,1024]{2,1,0:T(8,128)(2,1)S(1)}, u32[]{:S(2)}, u32[]{:S(2)}) collective-permute-start(bf16[2,64,1024]{2,1,0:T(8,128)(2,1)S(1)} %fusion.19), channel_id=1, source_target_pairs={{2,4},{3,5},{4,2},{5,3},{10,12},{11,13},{12,10},{13,11},{18,20},{1... | collective-permute-start | bytes 786440 | tf_op jit(solution)/shard_map/ppermute | solution.py:293
  67.8 13.5 %collective-permute-start.13 = (bf16[2,64,1024]{2,1,0:T(8,128)(2,1)}, bf16[2,64,1024]{2,1,0:T(8,128)(2,1)S(1)}, u32[]{:S(2)}, u32[]{:S(2)}) collective-permute-start(bf16[2,64,1024]{2,1,0:T(8,128)(2,1)} %fusion.11), channel_id=1, source_target_pairs={{2,4},{3,5},{4,2},{5,3},{10,12},{11,13},{12,10},{13,11},{18,20},{1... | collective-permute-start | bytes 786440 | tf_op jit(solution)/shard_map/ppermute | solution.py:293
  71.5 11.9 %collective-permute-start.7 = (bf16[2,64,1024]{2,1,0:T(8,128)(2,1)}, bf16[2,64,1024]{2,1,0:T(8,128)(2,1)S(1)}, u32[]{:S(2)}, u32[]{:S(2)}) collective-permute-start(bf16[2,64,1024]{2,1,0:T(8,128)(2,1)} %fusion.3), channel_id=1, source_target_pairs={{2,4},{3,5},{4,2},{5,3},{10,12},{11,13},{12,10},{13,11},{18,20},{1... | collective-permute-start | bytes 786440 | tf_op jit(solution)/shard_map/ppermute | solution.py:293
  72.3 11.4 %collective-permute-start.26 = (bf16[2,64,1024]{2,1,0:T(8,128)(2,1)S(1)}, bf16[2,64,1024]{2,1,0:T(8,128)(2,1)S(1)}, u32[]{:S(2)}, u32[]{:S(2)}) collective-permute-start(bf16[2,64,1024]{2,1,0:T(8,128)(2,1)S(1)} %collective-permute-done.25), channel_id=1, source_target_pairs={{0,2},{1,3},{4,6},{5,7},{2,0},{3,1},{6,4},{7,5},{8,10},{9,11},{12,... | collective-permute-start | bytes 786440 | tf_op jit(solution)/shard_map/ppermute | solution.py:293
  79.0 10.2 %collective-permute-start.20 = (bf16[2,64,1024]{2,1,0:T(8,128)(2,1)S(1)}, bf16[2,64,1024]{2,1,0:T(8,128)(2,1)S(1)}, u32[]{:S(2)}, u32[]{:S(2)}) collective-permute-start(bf16[2,64,1024]{2,1,0:T(8,128)(2,1)S(1)} %collective-permute-done.19), channel_id=1, source_target_pairs={{0,2},{1,3},{4,6},{5,7},{2,0},{3,1},{6,4},{7,5},{8,10},{9,11},{12,... | collective-permute-start | bytes 786440 | tf_op jit(solution)/shard_map/ppermute | solution.py:293
  81.2 13.2 %collective-permute-start.14 = (bf16[2,64,1024]{2,1,0:T(8,128)(2,1)S(1)}, bf16[2,64,1024]{2,1,0:T(8,128)(2,1)S(1)}, u32[]{:S(2)}, u32[]{:S(2)}) collective-permute-start(bf16[2,64,1024]{2,1,0:T(8,128)(2,1)S(1)} %collective-permute-done.13), channel_id=1, source_target_pairs={{0,2},{1,3},{4,6},{5,7},{2,0},{3,1},{6,4},{7,5},{8,10},{9,11},{12,... | collective-permute-start | bytes 786440 | tf_op jit(solution)/shard_map/ppermute | solution.py:293
  83.3 14.7 %collective-permute-start.8 = (bf16[2,64,1024]{2,1,0:T(8,128)(2,1)S(1)}, bf16[2,64,1024]{2,1,0:T(8,128)(2,1)S(1)}, u32[]{:S(2)}, u32[]{:S(2)}) collective-permute-start(bf16[2,64,1024]{2,1,0:T(8,128)(2,1)S(1)} %collective-permute-done.7), channel_id=1, source_target_pairs={{0,2},{1,3},{4,6},{5,7},{2,0},{3,1},{6,4},{7,5},{8,10},{9,11},{12,... | collective-permute-start | bytes 786440 | tf_op jit(solution)/shard_map/ppermute | solution.py:293
  84.9 14.3 %collective-permute-start.27 = (bf16[2,64,1024]{2,1,0:T(8,128)(2,1)S(1)}, bf16[2,64,1024]{2,1,0:T(8,128)(2,1)S(1)}, u32[]{:S(2)}, u32[]{:S(2)}) collective-permute-start(bf16[2,64,1024]{2,1,0:T(8,128)(2,1)S(1)} %fusion.31), channel_id=1, source_target_pairs={{0,8},{8,0},{1,9},{9,1},{2,10},{10,2},{3,11},{11,3},{4,12},{12,4},... | collective-permute-start | bytes 786440 | tf_op jit(solution)/shard_map/ppermute | solution.py:293
  89.3 12.5 %collective-permute-start.21 = (bf16[2,64,1024]{2,1,0:T(8,128)(2,1)S(1)}, bf16[2,64,1024]{2,1,0:T(8,128)(2,1)S(1)}, u32[]{:S(2)}, u32[]{:S(2)}) collective-permute-start(bf16[2,64,1024]{2,1,0:T(8,128)(2,1)S(1)} %fusion.23), channel_id=1, source_target_pairs={{0,8},{8,0},{1,9},{9,1},{2,10},{10,2},{3,11},{11,3},{4,12},{12,4},... | collective-permute-start | bytes 786440 | tf_op jit(solution)/shard_map/ppermute | solution.py:293
  95.5 7.2 %collective-permute-start.15 = (bf16[2,64,1024]{2,1,0:T(8,128)(2,1)S(1)}, bf16[2,64,1024]{2,1,0:T(8,128)(2,1)S(1)}, u32[]{:S(2)}, u32[]{:S(2)}) collective-permute-start(bf16[2,64,1024]{2,1,0:T(8,128)(2,1)S(1)} %fusion.15), channel_id=1, source_target_pairs={{0,8},{8,0},{1,9},{9,1},{2,10},{10,2},{3,11},{11,3},{4,12},{12,4},... | collective-permute-start | bytes 786440 | tf_op jit(solution)/shard_map/ppermute | solution.py:293
  99.1 5.6 %collective-permute-start.9 = (bf16[2,64,1024]{2,1,0:T(8,128)(2,1)S(1)}, bf16[2,64,1024]{2,1,0:T(8,128)(2,1)S(1)}, u32[]{:S(2)}, u32[]{:S(2)}) collective-permute-start(bf16[2,64,1024]{2,1,0:T(8,128)(2,1)S(1)} %fusion.7), channel_id=1, source_target_pairs={{0,8},{8,0},{1,9},{9,1},{2,10},{10,2},{3,11},{11,3},{4,12},{12,4},... | collective-permute-start | bytes 786440 | tf_op jit(solution)/shard_map/ppermute | solution.py:293
  100.3 9.3 %collective-permute-start.28 = (bf16[2,64,1024]{2,1,0:T(8,128)(2,1)}, bf16[2,64,1024]{2,1,0:T(8,128)(2,1)S(1)}, u32[]{:S(2)}, u32[]{:S(2)}) collective-permute-start(bf16[2,64,1024]{2,1,0:T(8,128)(2,1)} %get-tuple-element.62), channel_id=1, source_target_pairs={{0,1},{2,3},{4,5},{6,7},{1,0},{3,2},{5,4},{7,6},{8,9},{10,11},{12,... | collective-permute-start | bytes 786440 | tf_op jit(solution)/shard_map/ppermute | solution.py:293
  102.1 13.0 %collective-permute-start.22 = (bf16[2,64,1024]{2,1,0:T(8,128)(2,1)S(1)}, bf16[2,64,1024]{2,1,0:T(8,128)(2,1)S(1)}, u32[]{:S(2)}, u32[]{:S(2)}) collective-permute-start(bf16[2,64,1024]{2,1,0:T(8,128)(2,1)S(1)} %get-tuple-element.64), channel_id=1, source_target_pairs={{0,1},{2,3},{4,5},{6,7},{1,0},{3,2},{5,4},{7,6},{8,9},{10,11},{12,... | collective-permute-start | bytes 786440 | tf_op jit(solution)/shard_map/ppermute | solution.py:293
  103.1 17.7 %collective-permute-start.16 = (bf16[2,64,1024]{2,1,0:T(8,128)(2,1)S(1)}, bf16[2,64,1024]{2,1,0:T(8,128)(2,1)S(1)}, u32[]{:S(2)}, u32[]{:S(2)}) collective-permute-start(bf16[2,64,1024]{2,1,0:T(8,128)(2,1)S(1)} %get-tuple-element.66), channel_id=1, source_target_pairs={{0,1},{2,3},{4,5},{6,7},{1,0},{3,2},{5,4},{7,6},{8,9},{10,11},{12,... | collective-permute-start | bytes 786440 | tf_op jit(solution)/shard_map/ppermute | solution.py:293
  105.1 20.9 %collective-permute-start.10 = (bf16[2,64,1024]{2,1,0:T(8,128)(2,1)S(1)}, bf16[2,64,1024]{2,1,0:T(8,128)(2,1)S(1)}, u32[]{:S(2)}, u32[]{:S(2)}) collective-permute-start(bf16[2,64,1024]{2,1,0:T(8,128)(2,1)S(1)} %get-tuple-element.68), channel_id=1, source_target_pairs={{0,1},{2,3},{4,5},{6,7},{1,0},{3,2},{5,4},{7,6},{8,9},{10,11},{12,... | collective-permute-start | bytes 786440 | tf_op jit(solution)/shard_map/ppermute | solution.py:293
  (10 other events, 73.0 us)
where the time goes:
time: 128 us
  waiting for transfers between devices  46.2 us (36%)
  starting transfers between devices  34.9 us (27%)
  Pallas kernels  31.2 us (24%)
  other arithmetic  8.68 us (7%)
  local copies, waits for them, and re-layouts  6.26 us (5%)
    ppermute x28, waiting for transfers between devices, swap(): return lax.ppermute(value, axis, both)  46.2 us
    ppermute x28, starting transfers between devices, swap(): return lax.ppermute(value, axis, both)  30 us
    pallas_call x4, Pallas kernels, end_states(): pl.pallas_call(states_body, grid=(count,), in_specs=[pl.BlockSpec(memory_...  14.2 us
    pallas_call x4, Pallas kernels, inside_block(): pl.pallas_call(inside_body, grid=(count,), in_specs=[pl.BlockSpec((SPAN,...  8.66 us
    pallas_call x4, Pallas kernels, with_carry(): pl.pallas_call(carried_body, grid=(count,), in_specs=[pl.BlockSpec(memory...  7.21 us
    ppermute x1, starting transfers between devices, shards(): lax.ppermute(rim_rows, ('outer', 'inner'), [(i, i + 1) for i in range(dev...  4.88 us
    convert_element_type x4, other arithmetic, enter_by_swaps(): total = (two_chips.astype(F32) * w[3] + others * w[4]).astype(BF16)  3.42 us
    unnamed x26, local copies, waits for them, and re-layouts  3.13 us
  transfers between devices with their start and end apart: 29, of which 16 were waited for; matrix products, arithmetic and copies ran while one was open for 7% of the time, Pallas kernels for 20%

commit v1 on v0

v1 whole, which is shorter than its diff:
```python
import jax
import jax.numpy as jnp
from jax import lax
from jax.experimental import pallas as pl
from jax.experimental.pallas import tpu as pltpu
from jax.sharding import PartitionSpec as P

H = 128
P_SIZE = 64
N = 128
G = 8
KERNEL_TAPS = 4
SPAN = 256

HEADS = H // G
COLS = HEADS * P_SIZE
HALF = N // 2
RIM = KERNEL_TAPS - 1
PAD = 8
LOG2E = 1.4426950408889634
VMEM = 16 * 1024 * 1024
TILE = 16
WIDE = H * P_SIZE
F32 = jnp.float32
BF16 = jnp.bfloat16
CHUNKS = (2, 2, 2, 2)


def params():
    return pltpu.CompilerParams(vmem_limit_bytes=VMEM)


def cost(us, moved=0):
    return pl.CostEstimate(flops=int(us * 9e8), bytes_accessed=moved, transcendentals=0)


def mark():
    return jax.ShapeDtypeStruct((8, 128), F32)


MARK = pl.BlockSpec((8, 128), lambda i: (0, 0))


def corner(a):
    tile = tuple(min(n, m) for n, m in zip(a.shape[-2:], (TILE, 128)))
    block = (1,) * (a.ndim - 2) + tile
    return pl.BlockSpec(block, lambda i: (0,) * a.ndim)


def rim_body(x_ref, b_ref, c_ref, rim_ref):
    rim_ref[:, :WIDE] = x_ref[TILE - RIM :, :]
    rim_ref[:, WIDE : WIDE + G * N] = b_ref[TILE - RIM :, :]
    rim_ref[:, WIDE + G * N :] = c_ref[TILE - RIM :, :]


def rim_rows(x, b, c):
    at = x.shape[0] // TILE - 1
    width = x.shape[1] + b.shape[1] + c.shape[1]
    return pl.pallas_call(
        rim_body,
        grid=(1,),
        in_specs=[pl.BlockSpec((TILE, a.shape[1]), lambda i: (at, 0)) for a in (x, b, c)],
        out_specs=pl.BlockSpec((RIM, width), lambda i: (0, 0)),
        out_shape=jax.ShapeDtypeStruct((RIM, width), BF16),
        compiler_params=params(),
        cost_estimate=cost(1.0),
        name="rim_rows",
    )(*[pltpu.with_memory_space_constraint(a, pltpu.HBM) for a in (x, b, c)])


def whole(a):
    return pl.BlockSpec(a.shape, lambda i: (0,) * len(a.shape))


def split(value, parts):
    found = []
    for _ in range(parts):
        found.append(value.astype(BF16))
        value = value - found[-1].astype(F32)
    groups = []
    for group in range(G):
        lo = group * HEADS
        groups.append(jnp.concatenate([a[:, lo : lo + HEADS] for a in found], axis=1))
    return groups


def spreader(parts):
    head = lax.broadcasted_iota(jnp.int32, (parts * HEADS, COLS), 0) % HEADS
    col = lax.broadcasted_iota(jnp.int32, (parts * HEADS, COLS), 1) // P_SIZE
    return jnp.where(head == col, 1.0, 0.0).astype(BF16)


def by_column(value, matrix, parts):
    rows = jnp.concatenate(split(value, parts), axis=0)
    return jnp.dot(rows, matrix, preferred_element_type=F32)


def steps_body(
    dt_ref,
    decay_ref,
    skip_ref,
    cols_ref,
    rows_ref,
    to_end_ref,
    from_start_ref,
    last_ref,
    skip_cols_ref,
    spread_ref,
):
    raw = dt_ref[...].astype(F32)
    dt = jnp.maximum(raw, 0.0) + jnp.log1p(jnp.exp(-jnp.abs(raw)))
    step = dt * (-jnp.exp(decay_ref[...]))
    row = lax.broadcasted_iota(jnp.int32, (SPAN, SPAN), 0)
    col = lax.broadcasted_iota(jnp.int32, (SPAN, SPAN), 1)
    tri = jnp.where(row >= col, 1.0, 0.0).astype(F32)
    cum = jnp.dot(tri, step, precision=lax.Precision.HIGHEST, preferred_element_type=F32)
    last = cum[SPAN - 1 :, :]
    last_ref[...] = last
    rows_ref[...] = jnp.transpose((cum - jnp.log(dt)) * LOG2E)
    to_end = split(jnp.exp(last - cum) * dt, 2)
    from_start = split(jnp.exp(cum), 2)
    scaled = cum * LOG2E
    for group in range(G):
        lo = group * HEADS
        cols_ref[group] = scaled[:, lo : lo + HEADS]
        to_end_ref[group] = to_end[group]
        from_start_ref[group] = from_start[group]
    skip_cols = by_column(skip_ref[...], spreader(3), 3)
    for group in range(G):
        skip_cols_ref[group] = skip_cols[group : group + 1]
    spread_ref[...] = spreader(2)


def time_steps(dt_input, decay_log, skip_weight):
    given = (dt_input, decay_log.reshape(1, H), skip_weight.reshape(1, H))
    out = [
        jax.ShapeDtypeStruct((G, SPAN, HEADS), F32),
        jax.ShapeDtypeStruct((H, SPAN), F32),
        jax.ShapeDtypeStruct((G, SPAN, 2 * HEADS), BF16),
        jax.ShapeDtypeStruct((G, SPAN, 2 * HEADS), BF16),
        jax.ShapeDtypeStruct((1, H), F32),
        jax.ShapeDtypeStruct((G, 1, COLS), F32),
        jax.ShapeDtypeStruct((2 * HEADS, COLS), BF16),
    ]
    return pl.pallas_call(
        steps_body,
        grid=(1,),
        in_specs=[whole(a) for a in given],
        out_specs=[whole(a) for a in out],
        out_shape=out,
        compiler_params=params(),
        cost_estimate=cost(2.0),
        name="time_steps",
    )(*given)


def convolved(ref, rim_ref, kernel_ref, scratch):
    kernel = kernel_ref[...].astype(F32) * 0.5
    width = ref.shape[1]
    parts = []
    for lo in range(0, width, 128):
        sl = slice(lo, lo + 128)
        scratch[PAD - RIM : PAD, :] = rim_ref[:, sl].astype(F32)
        scratch[PAD : PAD + SPAN, :] = ref[:, sl].astype(F32)
        half = kernel[RIM : RIM + 1, sl] * scratch[PAD : PAD + SPAN, :]
        for tap in range(RIM):
            first = PAD - RIM + tap
            half = half + kernel[tap : tap + 1, sl] * scratch[first : first + SPAN, :]
        parts.append((half + half * jnp.tanh(half)).astype(BF16))
    return parts


def states_body(
    x_ref,
    b_ref,
    c_ref,
    rim_x_ref,
    rim_b_ref,
    rim_c_ref,
    kernel_x_ref,
    kernel_b_ref,
    kernel_c_ref,
    to_end_ref,
    spread_ref,
    flag_ref,
    last_ref,
    values_ref,
    conv_b_ref,
    conv_c_ref,
    keep_ref,
    send_ref,
    mark_ref,
    scratch,
):
    mark_ref[...] = jnp.zeros_like(mark_ref)
    (conv_b,) = convolved(b_ref, rim_b_ref, kernel_b_ref, scratch)
    (conv_c,) = convolved(c_ref, rim_c_ref, kernel_c_ref, scratch)
    conv_b_ref[...] = conv_b
    conv_c_ref[...] = conv_c
    parts = convolved(x_ref, rim_x_ref, kernel_x_ref, scratch)
    for at, part in enumerate(parts):
        values_ref[:, at * 128 : (at + 1) * 128] = part
    gain = jnp.dot(to_end_ref[0], spread_ref[...], preferred_element_type=F32)
    weighted = (values_ref[...].astype(F32) * gain).astype(BF16)
    state = lax.dot_general(
        conv_b, weighted, (((0,), (0,)), ((), ())), preferred_element_type=F32
    ).astype(BF16)
    upper = flag_ref[:1] > 0.5
    at = pl.program_id(0)
    rows = pl.ds(pl.multiple_of(at * HALF, HALF), HALF)
    keep_ref[rows, :] = jnp.where(upper, state[HALF:], state[:HALF])
    send_ref[rows, :] = jnp.where(upper, state[:HALF], state[HALF:])
    if send_ref.shape[0] > keep_ref.shape[0]:
        put_log(send_ref, keep_ref.shape[0], last_ref[...])


def end_states(first, count, x, b, c, rim, conv_weight, to_end, spread, flags, last, after, us=1.0):
    def cols(offset):
        return lambda i: (0, offset + first + i)

    def own(i):
        return (0, i)

    def lead(i):
        return (first + i, 0, 0)

    b_at, c_at = H * P_SIZE // N, H * P_SIZE // N + G
    return pl.pallas_call(
        lambda *refs: states_body(*refs[:13], *refs[13 + len(after) :]),
        grid=(count,),
        in_specs=[
            pl.BlockSpec((SPAN, COLS), cols(0)),
            pl.BlockSpec((SPAN, N), cols(0)),
            pl.BlockSpec((SPAN, N), cols(0)),
            pl.BlockSpec((RIM, COLS), cols(0)),
            pl.BlockSpec((RIM, N), cols(b_at)),
            pl.BlockSpec((RIM, N), cols(c_at)),
            pl.BlockSpec((KERNEL_TAPS, COLS), cols(0)),
            pl.BlockSpec((KERNEL_TAPS, N), cols(b_at)),
            pl.BlockSpec((KERNEL_TAPS, N), cols(c_at)),
            pl.BlockSpec((1, SPAN, 2 * HEADS), lead),
            pl.BlockSpec((2 * HEADS, COLS), lambda i: (0, 0)),
            whole(flags),
            whole(last),
        ]
        + [corner(a) for a in after],
        out_specs=[
            pl.BlockSpec((SPAN, COLS), own),
            pl.BlockSpec((SPAN, N), own),
            pl.BlockSpec((SPAN, N), own),
            pl.BlockSpec((count * HALF, COLS), lambda i: (0, 0)),
            pl.BlockSpec((count * HALF + log_rows(first), COLS), lambda i: (0, 0)),
            MARK,
        ],
        out_shape=[
            jax.ShapeDtypeStruct((SPAN, count * COLS), BF16),
            jax.ShapeDtypeStruct((SPAN, count * N), BF16),
            jax.ShapeDtypeStruct((SPAN, count * N), BF16),
            jax.ShapeDtypeStruct((count * HALF, COLS), BF16),
            jax.ShapeDtypeStruct((count * HALF + log_rows(first), COLS), BF16),
            mark(),
        ],
        scratch_shapes=[pltpu.VMEM((PAD + SPAN, 128), F32)],
        compiler_params=params(),
        cost_estimate=cost(us),
        name="end_states",
    )(x, b, c, rim, rim, rim, conv_weight, conv_weight, conv_weight, to_end, spread, flags, last, *after)


def inside_body(values_ref, b_ref, c_ref, cols_ref, rows_ref, skip_ref, part_ref, mark_ref):
    mark_ref[...] = jnp.zeros_like(mark_ref)
    half = SPAN // 2
    scores = lax.dot_general(
        c_ref[...], b_ref[...], (((1,), (1,)), ((), ())), preferred_element_type=F32
    )
    row = lax.broadcasted_iota(jnp.int32, (half, half), 0)
    col = lax.broadcasted_iota(jnp.int32, (half, half), 1)
    causal = row >= col
    lane = lax.broadcasted_iota(jnp.int32, (half, 2 * P_SIZE), 1)
    first_head = lane < P_SIZE
    cols = cols_ref[0]
    rows = rows_ref[...]
    corner, below, later = scores[:half, :half], scores[half:, :half], scores[half:, half:]
    for pair in range(HEADS // 2):
        upper, lower = [], []
        for head in (2 * pair, 2 * pair + 1):
            at_t = cols[:, head : head + 1]
            at_s = rows[head : head + 1, :]
            e = jnp.exp2(at_t[:half] - at_s[:, :half])
            upper.append(jnp.where(causal, corner * e, 0.0).astype(BF16))
            e = jnp.exp2(at_t[half:] - at_s[:, :half])
            left = (below * e).astype(BF16)
            e = jnp.exp2(at_t[half:] - at_s[:, half:])
            right = jnp.where(causal, later * e, 0.0).astype(BF16)
            lower.append(jnp.concatenate([left, right], axis=1))
        sl = slice(pair * 2 * P_SIZE, (pair + 1) * 2 * P_SIZE)
        values = values_ref[:, sl]
        skip = skip_ref[0, :, sl]
        for lo, mix, depth in ((0, upper, half), (half, lower, SPAN)):
            both = jnp.dot(
                jnp.concatenate(mix, axis=0), values[:depth], preferred_element_type=F32
            )
            inside = jnp.where(first_head, both[:half], both[half:])
            part_ref[lo : lo + half, sl] = inside + skip * values[lo : lo + half].astype(F32)


def inside_block(first, count, values, conv_b, conv_c, cols, rows, skip, after, us=1.0):
    def own(i):
        return (0, i)

    return pl.pallas_call(
        lambda *refs: inside_body(*refs[:6], *refs[6 + len(after) :]),
        grid=(count,),
        in_specs=[
            pl.BlockSpec((SPAN, COLS), own),
            pl.BlockSpec((SPAN, N), own),
            pl.BlockSpec((SPAN, N), own),
            pl.BlockSpec((1, SPAN, HEADS), lambda i: (first + i, 0, 0)),
            pl.BlockSpec((HEADS, SPAN), lambda i: (first + i, 0)),
            pl.BlockSpec((1, 1, COLS), lambda i: (first + i, 0, 0)),
        ]
        + [corner(a) for a in after],
        out_specs=[pl.BlockSpec((SPAN, COLS), own), MARK],
        out_shape=[jax.ShapeDtypeStruct((SPAN, count * COLS), F32), mark()],
        compiler_params=params(),
        cost_estimate=cost(us),
        name="inside_block",
    )(values, conv_b, conv_c, cols, rows, skip, *after)


def carried_body(*refs):
    side_ref, c_ref, part_ref, keep_ref, got_ref, from_start_ref, spread_ref = refs[:7]
    out_ref, mark_ref = refs[-2:]
    mark_ref[...] = jnp.zeros_like(mark_ref)
    upper = side_ref[:1] > 0.5
    keep, got = keep_ref[...], got_ref[...]
    carry = jnp.concatenate(
        [jnp.where(upper, got, keep), jnp.where(upper, keep, got)], axis=0
    )
    gain = jnp.dot(from_start_ref[0], spread_ref[...], preferred_element_type=F32)
    carried = jnp.dot(c_ref[...], carry, preferred_element_type=F32)
    out_ref[...] = (part_ref[...] + carried * gain).astype(BF16)


def with_carry(first, count, side, conv_c, part, keep, got, from_start, spread, out, after, us=1.0):
    def own(i):
        return (0, i)

    given = [] if out is None else [out]
    return pl.pallas_call(
        carried_body,
        grid=(count,),
        in_specs=[
            whole(side),
            pl.BlockSpec((SPAN, N), own),
            pl.BlockSpec((SPAN, COLS), own),
            pl.BlockSpec((HALF, COLS), lambda i: (i, 0)),
            pl.BlockSpec((HALF, COLS), lambda i: (i, 0)),
            pl.BlockSpec((1, SPAN, 2 * HEADS), lambda i: (first + i, 0, 0)),
            pl.BlockSpec((2 * HEADS, COLS), lambda i: (0, 0)),
        ]
        + [pl.BlockSpec(memory_space=pl.ANY)] * len(given)
        + [corner(a) for a in after],
        out_specs=[pl.BlockSpec((SPAN, COLS), lambda i: (0, first + i)), MARK],
        out_shape=[jax.ShapeDtypeStruct((SPAN, WIDE), BF16), mark()],
        input_output_aliases={7: 0} if given else {},
        compiler_params=params(),
        cost_estimate=cost(us),
        name="with_carry",
    )(side, conv_c, part, keep, got, from_start, spread, *given, *after)


def swap(value, axis, pairs):
    return lax.ppermute(value, axis, pairs + [(b, a) for a, b in pairs])


def log_rows(first):
    return TILE if first == 0 else 0


def put_log(ref, at, log):
    ref[at:, :] = jnp.zeros((TILE, COLS), BF16)
    parts = []
    for _ in range(3):
        parts.append(log.astype(BF16).astype(F32))
        log = log - parts[-1]
    rest = jnp.zeros((TILE - len(parts), H), F32)
    ref[at:, :H] = jnp.concatenate(parts + [rest], axis=0).astype(BF16)


def take_log(ref, at):
    rows = ref[at:, :H].astype(F32)
    return rows[0:1] + rows[1:2] + rows[2:3]


Y_PAIRS = [(0, 1), (2, 3), (4, 5), (6, 7)]
Z_PAIRS = [(0, 2), (1, 3), (4, 6), (5, 7)]
MID_PAIRS = [(2, 4), (3, 5)]
FAR_PAIRS = [(0, 4), (1, 5), (2, 6), (3, 7)]

ORDER = (
    [("state", 0, 1.0), ("state", 1, 1.0), ("state", 2, 1.0), ("chip", 0, 1.0)]
    + [("state", 3, 1.0), ("chip", 1, 1.0), ("chips", 0, 1.0), ("chip", 2, 1.0)]
    + [("chips", 1, 1.0), ("link", 0, 1.0), ("chips", 2, 1.0), ("chip", 3, 1.0)]
    + [("inside", 3, 1.0), ("link", 1, 1.0), ("total", 0, 1.0), ("link", 2, 1.0)]
    + [("inside", 0, 1.0), ("chips", 3, 1.0), ("inside", 1, 1.0), ("leave", 0, 1.0)]
    + [("total", 1, 1.0), ("link", 3, 1.0), ("total", 2, 1.0), ("leave", 1, 1.0)]
    + [("out", 0, 1.0), ("total", 3, 1.0), ("leave", 2, 1.0), ("inside", 2, 1.0)]
    + [("out", 1, 1.0), ("leave", 3, 1.0), ("out", 2, 1.0), ("out", 3, 1.0)]
)


def places():
    at, core = lax.axis_index("inner"), lax.axis_index("outer")
    z = at >> 1
    row = lax.broadcasted_iota(jnp.int32, (8, COLS), 0)
    flags = jnp.zeros((8, COLS), F32)
    for number, flag in enumerate(((at & 1) == 1, (z & 1) == 1, z >= 2, core == 1)):
        flags = jnp.where((row == number) & flag, 1.0, flags)
    return flags


def merge(body, arrays, weights, lead, flags, spread, after, outs, us):
    count = min(a.shape[0] for a in arrays) // HALF
    rows = count * HALF
    given = [flags, *arrays]
    out = [jax.ShapeDtypeStruct((rows, COLS), BF16)] * outs
    given += weights
    if lead is not None:
        step, known, wanted, sends = lead
        given += [spread, known]
        if sends:
            out = [jax.ShapeDtypeStruct((rows + TILE, COLS), BF16)]
        out.append(jax.ShapeDtypeStruct((8, H), F32))
        out += [jax.ShapeDtypeStruct((n, 1, COLS), F32) for n in CHUNKS] * wanted
    out.append(mark())

    def run(*refs):
        ins = refs[1 : 1 + len(arrays)]
        scale_refs = refs[1 + len(arrays) : 1 + len(arrays) + len(weights)]
        rest = refs[1 + len(arrays) + len(weights) : len(given)]
        results = refs[len(given) + len(after) :]
        on = [refs[0][at : at + 1] > 0.5 for at in range(4)]
        results[-1][...] = jnp.zeros((8, 128), F32)
        scales = [[r[at] for r in scale_refs] for at in range(count)]
        if lead is not None:
            logs = [take_log(r, rows) if r.shape[0] > rows else None for r in ins]
            found, keeps, onward = step([a[:, :H] for a in on], logs, rest[1][...])
            empty = jnp.zeros((8 - len(keeps), H), F32)
            results[outs][...] = jnp.concatenate(keeps + [empty], axis=0)
            if sends:
                put_log(results[0], rows, onward)
            found = [by_column(row, rest[0][...], 2) for row in found]
            scales = [[f[at : at + 1] for f in found] + scales[at] for at in range(count)]
            at = outs + 1
            for value in found:
                first = 0
                for n in CHUNKS:
                    for group in range(n):
                        results[at][group] = value[first + group : first + group + 1]
                    first += n
                    at += 1
        for at in range(count):
            part = slice(at * HALF, (at + 1) * HALF)
            values = body(on, [r[part, :].astype(F32) for r in ins], scales[at])
            for ref, value in zip(results, values):
                ref[part, :] = value.astype(BF16)

    found = pl.pallas_call(
        run,
        grid=(1,),
        in_specs=[whole(a) for a in given] + [corner(a) for a in after],
        out_specs=[whole(a) for a in out],
        out_shape=out,
        compiler_params=params(),
        cost_estimate=cost(us),
        name=body.__name__,
    )(*given, *after)
    if lead is None:
        return found[:outs], found[-1], None, None
    n = len(CHUNKS)
    scales = [found[outs + 1 + n * at : outs + 1 + n * (at + 1)] for at in range(wanted)]
    return found[:outs], found[-1], found[outs], scales


def add_chip(on, arrays, scales):
    upper, _, _, _ = on
    keep, got = arrays
    return (jnp.where(upper, got, keep) * scales[0] + jnp.where(upper, keep, got),)


def chip_logs(on, logs, known):
    upper, _, _, _ = on
    own, got = known[0:1], logs[1]
    low, high = jnp.where(upper, got, own), jnp.where(upper, own, got)
    return [jnp.exp(high), jnp.exp(low)], [low + high], low + high


def add_chips(on, arrays, scales):
    _, odd, _, _ = on
    chip, got = arrays
    return (jnp.where(odd, got, chip) * scales[0] + jnp.where(odd, chip, got),)


def chips_logs(on, logs, known):
    _, odd, _, _ = on
    own, got = known[0:1], logs[1]
    low, high = jnp.where(odd, got, own), jnp.where(odd, own, got)
    return [jnp.exp(high), jnp.exp(own)], [low + high, low], low + high


def go_on(on, arrays, scales):
    _, _, high, _ = on
    chip, two, got = arrays
    own, other, through = scales
    return (jnp.where(high, got * through + chip, two * own + got * other),)


def go_on_logs(on, logs, known):
    _, _, high, _ = on
    own, low, got = known[0:1], known[1:2], logs[2]
    none = jnp.zeros_like(own)
    weights = [jnp.exp(jnp.where(high, none, got)), jnp.exp(jnp.where(high, own, none))]
    return weights, [got, low], got


def add_all(on, arrays, scales):
    _, odd, high, _ = on
    chip, two, got, far = arrays
    own, other, through = scales[:3]
    at_end = jnp.where(high, far * through + chip, far)
    return (jnp.where(odd != high, two * own + got * other, at_end),)


def enter_logs(on, logs, known):
    _, odd, high, core = on
    other, low, further = known[0:1], known[1:2], logs[4]
    none = jnp.zeros_like(other)
    below = jnp.where(odd, low, none)
    reach = jnp.where(high, jnp.where(odd, further, other), none) + below
    return [jnp.where(core, jnp.exp(reach), none)], [], None


def enter(on, arrays, scales):
    upper, odd, high, _ = on
    keep, got_y, got_z, got, far, before = arrays
    reach, below = scales
    low_side = jnp.where(odd, got_z, jnp.zeros_like(got_z))
    entering = jnp.where(high, jnp.where(odd, far, got), low_side) + before * reach
    above = entering * below + jnp.where(upper, got_y, keep)
    return jnp.where(upper, above, entering), jnp.where(upper, entering, above)


def in_order(x, b, c, rim, conv_weight, steps, flags):
    cols, rows, to_end, from_start, last, skip, spread = steps
    starts = [sum(CHUNKS[:k]) for k in range(len(CHUNKS))]
    done, weights = {}, {}
    known = last
    after = []
    out = None

    def merged(body, k, names, scales, logs, wanted, outs=1, sends=True):
        nonlocal known
        lead = (logs, known, len(wanted), sends) if k == 0 and logs is not None else None
        if lead is None:
            scales = wanted + scales
        found, mark, keeps, new = merge(
            body,
            [done[name, k] for name in names],
            [weights[name][k] for name in scales],
            lead,
            flags,
            spread,
            after,
            outs,
            us,
        )
        if lead is not None:
            known = keeps
            weights.update(zip(wanted, new))
        return found, mark

    for what, k, us in ORDER:
        first, count = starts[k], CHUNKS[k]
        if what == "state":
            found = end_states(
                first, count, x, b, c, rim, conv_weight, to_end, spread, flags, last, after, us
            )
            done["values", k], done["b", k], done["c", k], keep, send, mark = found
            done["keep", k], done["y", k] = keep, swap(send, "inner", Y_PAIRS)
        elif what == "inside":
            given = [done[name, k] for name in ("values", "b", "c")]
            done["inside", k], mark = inside_block(
                first, count, *given, cols, rows, skip, after, us
            )
        elif what == "chip":
            wanted = ["above", "below"]
            if k > 0:
                wanted = ["above"]
            (found,), mark = merged(add_chip, k, ["keep", "y"], [], chip_logs, wanted)
            done["chip", k], done["z", k] = found, swap(found, "inner", Z_PAIRS)
        elif what == "chips":
            wanted = ["high", "through"]
            if k > 0:
                wanted = ["high"]
            (found,), mark = merged(add_chips, k, ["chip", "z"], [], chips_logs, wanted)
            done["chips", k], done["mid", k] = found, swap(found, "inner", MID_PAIRS)
        elif what == "link":
            names = ["chip", "chips", "mid"]
            (found,), mark = merged(
                go_on, k, names, ["through"], go_on_logs, ["own", "other"]
            )
            done["far", k] = swap(found, "inner", Z_PAIRS)
        elif what == "total":
            names = ["chip", "chips", "mid", "far"]
            (found,), mark = merged(
                add_all, k, names, ["own", "other", "through"], None, []
            )
            done["before", k] = swap(found, "outer", [(0, 1)])
        elif what == "leave":
            names = ["keep", "y", "z", "mid", "far", "before"]
            (stay, leave), mark = merged(
                enter, k, names, ["below"], enter_logs, ["reach"], outs=2, sends=False
            )
            done["stay", k], done["back", k] = stay, swap(leave, "inner", Y_PAIRS)
        else:
            given = [done[name, k] for name in ("c", "inside", "stay", "back")]
            out, mark = with_carry(
                first, count, flags, *given, from_start, spread, out, after, us
            )
        after = [mark]
    return out


def combine(earlier, later):
    return (earlier[0] * later[0], later[0][:, None, :] * earlier[1] + later[1])


def enter_by_all_to_all(last, kept, sent):
    size = lax.axis_size("inner")
    upper = (lax.axis_index("inner") & 1) == 1
    wide = 2 * P_SIZE
    pairs = H // 2
    sent = [a[: b.shape[0]] for a, b in zip(sent, kept)]
    keep, send = [jnp.concatenate(a).reshape(G, HALF, COLS) for a in (kept, sent)]
    halves = [jnp.where(upper, send, keep), jnp.where(upper, keep, send)]
    state = jnp.concatenate(halves, axis=1).reshape(G, N, pairs // G, wide)
    state = jnp.swapaxes(state, 1, 2).reshape(pairs, N, wide)
    decay = jnp.repeat(jnp.exp(last[0]), P_SIZE).reshape(pairs, wide)

    def spread(a):
        return lax.all_to_all(a[None], "inner", split_axis=1, concat_axis=0, tiled=True)

    decays, states = spread(decay), spread(state).astype(F32)
    run = (jnp.ones_like(decays[0]), jnp.zeros_like(states[0]))

    def lap(run, item):
        return combine(run, item), run

    total, before = lax.scan(lap, run, (decays, states))
    first = lax.ppermute(total[1].astype(BF16), "outer", [(0, 1)]).astype(F32)
    entering = before[0][:, :, None, :] * first[None] + before[1]
    carry = lax.all_to_all(
        entering.astype(BF16), "inner", split_axis=0, concat_axis=1, tiled=True
    )[0]
    carry = carry.reshape(G, pairs // G, N, wide)
    carry = jnp.swapaxes(carry, 1, 2).reshape(G, N, COLS)
    top, bottom = carry[:, :HALF], carry[:, HALF:]
    stay, got = jnp.where(upper, bottom, top), jnp.where(upper, top, bottom)
    entered = []
    at = 0
    for count in CHUNKS:
        part = [a[at : at + count].reshape(count * HALF, COLS) for a in (stay, got)]
        entered.append(part)
        at += count
    return entered


def one_by_one(x, b, c, rim, conv_weight, steps, flags):
    cols, rows, to_end, from_start, last, skip, spread = steps
    starts = [sum(CHUNKS[:k]) for k in range(len(CHUNKS))]
    states = [
        end_states(
            first, count, x, b, c, rim, conv_weight, to_end, spread, flags, last, []
        )
        for first, count in zip(starts, CHUNKS)
    ]
    entered = enter_by_all_to_all(last, [a[3] for a in states], [a[4] for a in states])
    out = None
    for first, count, state, (keep, got) in zip(starts, CHUNKS, states, entered):
        values, conv_b, conv_c = state[:3]
        part, _ = inside_block(
            first, count, values, conv_b, conv_c, cols, rows, skip, []
        )
        out, _ = with_carry(
            first, count, flags, conv_c, part, keep, got, from_start, spread, out, []
        )
    return out


def shards(x_stream, b_stream, c_stream, dt_input, decay_log, skip_weight, conv_weight):
    devices = lax.axis_size("outer") * lax.axis_size("inner")
    x_stream, dt_input, flags = lax.optimization_barrier((x_stream, dt_input, places()))
    rim = lax.ppermute(
        rim_rows(x_stream, b_stream, c_stream),
        ("outer", "inner"),
        [(i, i + 1) for i in range(devices - 1)],
    )
    steps = time_steps(dt_input, decay_log, skip_weight)
    by_swaps = lax.axis_size("inner") == 8 and lax.axis_size("outer") == 2
    rest = in_order if by_swaps else one_by_one
    return rest(x_stream, b_stream, c_stream, rim, conv_weight, steps, flags)


def solution(mesh):
    return jax.shard_map(
        shards,
        mesh=mesh,
        in_specs=(
            P(("slab", "outer", "inner"), None),
            P(("slab", "outer", "inner"), None),
            P(("slab", "outer", "inner"), None),
            P(("slab", "outer", "inner"), None),
            P("slab"),
            P(),
            P(),
        ),
        out_specs=P(("slab", "outer", "inner"), None),
        check_vma=False,
    )
```

time: 128 us -> 92.5 us (0.72)
  waiting for transfers between devices: 46.2 us -> 15 us
  other arithmetic: 8.68 us -> 0.1 us
  local copies, waits for them, and re-layouts: 6.26 us -> 0.04 us
  starting transfers between devices: 34.9 us -> 41 us
  Pallas kernels: 31.2 us -> 35.8 us
    ppermute x29 -> x25, waiting for transfers between devices: 46.2 us -> 15 us  [the longest x24 14.3 us: swap(): return lax.ppermute(value, axis, pairs + [(b, a) for a, b in pairs])]
    convert_element_type x17 -> x0, other arithmetic: 8.45 us -> none  [the longest x4 3.42 us: enter_by_swaps(): total = (two_chips.astype(F32) * w[3] + others * w[4]).astype(BF16)]
    ppermute x29 -> x25, starting transfers between devices: 34.9 us -> 41 us  [the longest x24 35.8 us: swap(): return lax.ppermute(value, axis, pairs + [(b, a) for a, b in pairs])]
    pallas_call x13 -> x34, Pallas kernels: 31.2 us -> 35.8 us  [the longest x4 10.8 us: end_states(): pl.pallas_call(lambda *refs: states_body(*refs[:13], *refs[13 + len(after...]
    unnamed x26 -> x14, local copies, waits for them, and re-layouts: 3.13 us -> 0.04 us
    slice x3 -> x0, local copies, waits for them, and re-layouts: 2.48 us -> none  [shards(): a[tokens - RIM:]]
  transfers between devices with their start and end apart: 29 -> 25, of which waited for: 16 -> 9; matrix products, arithmetic and copies ran while one was open for 7% -> 0% of each run, Pallas kernels for 20% -> 33%
where the time goes in v1:
time: 92.5 us; the launch traced here: 92.3 us
  starting transfers between devices  41 us (44%)
  Pallas kernels  35.8 us (39%)
  waiting for transfers between devices  15 us (16%)
    ppermute x24, starting transfers between devices, swap(): return lax.ppermute(value, axis, pairs + [(b, a) for a, b in pairs])  35.8 us
    ppermute x24, waiting for transfers between devices, swap(): return lax.ppermute(value, axis, pairs + [(b, a) for a, b in pairs])  14.3 us
    pallas_call x4, Pallas kernels, end_states(): pl.pallas_call(lambda *refs: states_body(*refs[:13], *refs[13 + len(after...  10.8 us
    pallas_call x4, Pallas kernels, inside_block(): pl.pallas_call(lambda *refs: inside_body(*refs[:6], *refs[6 + len(after):...  8.89 us
    pallas_call x4, Pallas kernels, with_carry(): pl.pallas_call(carried_body, grid=(count,), in_specs=[whole(side), pl.Blo...  7.27 us
    pallas_call x20, Pallas kernels, merge(): pl.pallas_call(run, grid=(1,), in_specs=[whole(a) for a in given] + [corn...  6.51 us
    ppermute x1, starting transfers between devices, shards(): lax.ppermute(rim_rows(x_stream, b_stream, c_stream), ('outer', 'inner'),...  5.16 us
  transfers between devices with their start and end apart: 25, of which 9 were waited for; matrix products, arithmetic and copies ran while one was open for 0% of the time, Pallas kernels for 33%

profile of v1, /device:TPU:0, one launch (start us, length us, event | category | flops | bytes accessed | tf_op | source)
XLA Modules:
  0.0 92.3 jit_solution(6853622591620128145)
XLA Ops:
  0.1 1.0 %rim_rows.1 = bf16[3,10240]{1,0:T(4,128)(2,1)S(1)} custom-call(bf16[256,8192]{1,0:T(8,128)(2,1)} %refs_0_.3, bf16[256,1024]{1,0:T(8,128)(2,1)} %refs_1_.7, bf16[256,1024]{1,0:T(8,128)(2,1)} %refs_2_.7), custom_call_target="tpu_custom_call" | custom-call | flops 900000000 | tf_op jit(solution)/shard_map/rim_rows/pallas_call | solution.py:59
  1.2 5.2 %collective-permute-start = (bf16[3,10240]{1,0:T(4,128)(2,1)S(1)}, bf16[3,10240]{1,0:T(4,128)(2,1)S(1)}, u32[]{:S(2)}, u32[]{:S(2)}) collective-permute-start(bf16[3,10240]{1,0:T(4,128)(2,1)S(1)} %rim_rows.1), channel_id=1, source_target_pairs={{0,1},{1,2},{2,3},{3,4},{4,5},{5,6},{6,7},{7,8},{8,9},{9,10},{10,1... | collective-permute-start | bytes 184328 | tf_op jit(solution)/shard_map/ppermute | solution.py:704
  6.4 1.3 %time_steps.1 = (f32[8,256,16]{2,1,0:T(8,128)S(1)}, f32[128,256]{1,0:T(8,128)S(1)}, bf16[8,256,32]{2,1,0:T(8,128)(2,1)S(1)}, bf16[8,256,32]{2,1,0:T(8,128)(2,1)S...) custom-call(bf16[256,128]{1,0:T(8,128)(2,1)S(1)} %copy-done.4, ...), custom_call_target="tpu_custom_call" | custom-call | flops 1800000000 | tf_op jit(solution)/shard_map/time_steps/pallas_call | solution.py:145
  8.4 2.7 %end_states.4 = (bf16[256,2048]{1,0:T(8,128)(2,1)S(1)}, bf16[256,256]{1,0:T(8,128)(2,1)S(1)}, bf16[256,256]{1,0:T(8,128)(2,1)S(1)}, bf16[128,1024]{1,0:T(8,128)(...) custom-call(bf16[256,8192]{1,0:T(8,128)(2,1)S(1)} %copy-done, bf16[256,1024]{1,0:T(8,128)(2,1)S(1)} %copy-done.1, ...), custom_call_target="tpu_custom_call" | custom-call | flops 900000000 | tf_op jit(solution)/shard_map/end_states/pallas_call | solution.py:228
  11.1 2.5 %collective-permute-start.1 = (bf16[144,1024]{1,0:T(8,128)(2,1)S(1)}, bf16[144,1024]{1,0:T(8,128)(2,1)S(1)}, u32[]{:S(2)}, u32[]{:S(2)}) collective-permute-start(bf16[144,1024]{1,0:T(8,128)(2,1)S(1)} %get-tuple-element.133), channel_id=1, source_target_pairs={{0,1},{2,3},{4,5},{6,7},{1,0},{3,2},{5,4},{7,6},{8,9},{10,11},{12,... | collective-permute-start | bytes 884744 | tf_op jit(solution)/shard_map/ppermute | solution.py:374
  13.6 2.7 %end_states.5 = (bf16[256,2048]{1,0:T(8,128)(2,1)S(1)}, bf16[256,256]{1,0:T(8,128)(2,1)S(1)}, bf16[256,256]{1,0:T(8,128)(2,1)S(1)}, bf16[128,1024]{1,0:T(8,128)(...) custom-call(bf16[256,8192]{1,0:T(8,128)(2,1)S(1)} %copy-done, bf16[256,1024]{1,0:T(8,128)(2,1)S(1)} %copy-done.1, ...), custom_call_target="tpu_custom_call" | custom-call | flops 900000000 | tf_op jit(solution)/shard_map/end_states/pallas_call | solution.py:228
  16.4 2.7 %end_states.6 = (bf16[256,2048]{1,0:T(8,128)(2,1)S(1)}, bf16[256,256]{1,0:T(8,128)(2,1)S(1)}, bf16[256,256]{1,0:T(8,128)(2,1)S(1)}, bf16[128,1024]{1,0:T(8,128)(...) custom-call(bf16[256,8192]{1,0:T(8,128)(2,1)S(1)} %copy-done, bf16[256,1024]{1,0:T(8,128)(2,1)S(1)} %copy-done.1, ...), custom_call_target="tpu_custom_call" | custom-call | flops 900000000 | tf_op jit(solution)/shard_map/end_states/pallas_call | solution.py:228
  19.1 1.6 %collective-permute-done.1.refs_2_ = bf16[144,1024]{1,0:T(8,128)(2,1)S(1)} collective-permute-done((bf16[144,1024]{1,0:T(8,128)(2,1)S(1)}, bf16[144,1024]{1,0:T(8,128)(2,1)S(1)}, u32[]{:S(2)}, u32[]{:S(2)}) %collective-permute-start.1) | collective-permute-done | bytes 294944 | tf_op jit(solution)/shard_map/ppermute | solution.py:374
  21.6 3.8 %collective-permute-start.4 = (bf16[144,1024]{1,0:T(8,128)(2,1)S(1)}, bf16[144,1024]{1,0:T(8,128)(2,1)S(1)}, u32[]{:S(2)}, u32[]{:S(2)}) collective-permute-start(bf16[144,1024]{1,0:T(8,128)(2,1)S(1)} %get-tuple-element.150.refs_1_), channel_id=1, source_target_pairs={{0,2},{1,3},{4,6},{5,7},{2,0},{3,1},{6,4},{7,5},{8,10},{9,11},{12,... | collective-permute-start | bytes 884744 | tf_op jit(solution)/shard_map/ppermute | solution.py:374
  26.0 2.7 %end_states.7 = (bf16[256,2048]{1,0:T(8,128)(2,1)S(1)}, bf16[256,256]{1,0:T(8,128)(2,1)S(1)}, bf16[256,256]{1,0:T(8,128)(2,1)S(1)}, bf16[128,1024]{1,0:T(8,128)(...) custom-call(bf16[256,8192]{1,0:T(8,128)(2,1)S(1)} %copy-done, bf16[256,1024]{1,0:T(8,128)(2,1)S(1)} %copy-done.1, ...), custom_call_target="tpu_custom_call" | custom-call | flops 900000000 | tf_op jit(solution)/shard_map/end_states/pallas_call | solution.py:228
  29.0 4.2 %collective-permute-done.4.refs_2_.refs_3_ = bf16[144,1024]{1,0:T(8,128)(2,1)S(1)} collective-permute-done((bf16[144,1024]{1,0:T(8,128)(2,1)S(1)}, bf16[144,1024]{1,0:T(8,128)(2,1)S(1)}, u32[]{:S(2)}, u32[]{:S(2)}) %collective-permute-start.4) | collective-permute-done | bytes 294944 | tf_op jit(solution)/shard_map/ppermute | solution.py:374
  34.9 4.0 %collective-permute-start.6 = (bf16[128,1024]{1,0:T(8,128)(2,1)S(1)}, bf16[128,1024]{1,0:T(8,128)(2,1)S(1)}, u32[]{:S(2)}, u32[]{:S(2)}) collective-permute-start(bf16[128,1024]{1,0:T(8,128)(2,1)S(1)} %get-tuple-element.158.refs_1_), channel_id=1, source_target_pairs={{0,2},{1,3},{4,6},{5,7},{2,0},{3,1},{6,4},{7,5},{8,10},{9,11},{12,... | collective-permute-start | bytes 786440 | tf_op jit(solution)/shard_map/ppermute | solution.py:374
  38.9 1.3 %collective-permute-start.2 = (bf16[128,1024]{1,0:T(8,128)(2,1)S(1)}, bf16[128,1024]{1,0:T(8,128)(2,1)S(1)}, u32[]{:S(2)}, u32[]{:S(2)}) collective-permute-start(bf16[128,1024]{1,0:T(8,128)(2,1)S(1)} %get-tuple-element.145), channel_id=1, source_target_pairs={{0,1},{2,3},{4,5},{6,7},{1,0},{3,2},{5,4},{7,6},{8,9},{10,11},{12,... | collective-permute-start | bytes 786440 | tf_op jit(solution)/shard_map/ppermute | solution.py:374
  41.3 4.7 %collective-permute-start.11 = (bf16[144,1024]{1,0:T(8,128)(2,1)S(1)}, bf16[144,1024]{1,0:T(8,128)(2,1)S(1)}, u32[]{:S(2)}, u32[]{:S(2)}) collective-permute-start(bf16[144,1024]{1,0:T(8,128)(2,1)S(1)} %get-tuple-element.180), channel_id=1, source_target_pairs={{0,2},{1,3},{4,6},{5,7},{2,0},{3,1},{6,4},{7,5},{8,10},{9,11},{12,... | collective-permute-start | bytes 884744 | tf_op jit(solution)/shard_map/ppermute | solution.py:374
  47.0 3.8 %collective-permute-start.9 = (bf16[128,1024]{1,0:T(8,128)(2,1)S(1)}, bf16[128,1024]{1,0:T(8,128)(2,1)S(1)}, u32[]{:S(2)}, u32[]{:S(2)}) collective-permute-start(bf16[128,1024]{1,0:T(8,128)(2,1)S(1)} %get-tuple-element.171.refs_1_), channel_id=1, source_target_pairs={{0,2},{1,3},{4,6},{5,7},{2,0},{3,1},{6,4},{7,5},{8,10},{9,11},{12,... | collective-permute-start | bytes 786440 | tf_op jit(solution)/shard_map/ppermute | solution.py:374
  50.8 2.2 %inside_block.4 = (f32[256,2048]{1,0:T(8,128)S(1)}, f32[8,128]{1,0:T(8,128)S(1)}) custom-call(bf16[256,2048]{1,0:T(8,128)(2,1)S(1)} %get-tuple-element.139.refs_0_, bf16[256,256]{1,0:T(8,128)(2,1)S(1)} %get-tuple-element.140.refs_1_, bf16[256,256]{1,0:T(8,128)(2,1)S(1)} %get-tuple-element.138.refs_2_.refs_1_, f32[8,256,16]{2,1,0:T(8,128)S(1)} %get-tuple-element.141.refs_3_, ...), custom_call_target="tpu_custom_call" | custom-call | flops 900000000 | tf_op jit(solution)/shard_map/inside_block/pallas_call | solution.py:311
  54.5 2.1 %collective-permute-start.19 = (bf16[128,1024]{1,0:T(8,128)(2,1)S(1)}, bf16[128,1024]{1,0:T(8,128)(2,1)S(1)}, u32[]{:S(2)}, u32[]{:S(2)}) collective-permute-start(bf16[128,1024]{1,0:T(8,128)(2,1)S(1)} %get-tuple-element.215), channel_id=1, source_target_pairs={{0,2},{1,3},{4,6},{5,7},{2,0},{3,1},{6,4},{7,5},{8,10},{9,11},{12,... | collective-permute-start | bytes 786440 | tf_op jit(solution)/shard_map/ppermute | solution.py:374
  56.6 2.2 %inside_block.5 = (f32[256,2048]{1,0:T(8,128)S(1)}, f32[8,128]{1,0:T(8,128)S(1)}) custom-call(bf16[256,2048]{1,0:T(8,128)(2,1)S(1)} %get-tuple-element.173.refs_0_, bf16[256,256]{1,0:T(8,128)(2,1)S(1)} %get-tuple-element.174.refs_1_, bf16[256,256]{1,0:T(8,128)(2,1)S(1)} %get-tuple-element.175.refs_2_.refs_1_, f32[8,256,16]{2,1,0:T(8,128)S(1)} %get-tuple-element.141.refs_3_, ...), custom_call_target="tpu_custom_call" | custom-call | flops 900000000 | tf_op jit(solution)/shard_map/inside_block/pallas_call | solution.py:311
  60.6 2.2 %inside_block.6 = (f32[256,2048]{1,0:T(8,128)S(1)}, f32[8,128]{1,0:T(8,128)S(1)}) custom-call(bf16[256,2048]{1,0:T(8,128)(2,1)S(1)} %get-tuple-element.200.refs_0_, bf16[256,256]{1,0:T(8,128)(2,1)S(1)} %get-tuple-element.201.refs_1_, bf16[256,256]{1,0:T(8,128)(2,1)S(1)} %get-tuple-element.202.refs_2_.refs_1_, f32[8,256,16]{2,1,0:T(8,128)S(1)} %get-tuple-element.141.refs_3_, ...), custom_call_target="tpu_custom_call" | custom-call | flops 900000000 | tf_op jit(solution)/shard_map/inside_block/pallas_call | solution.py:311
  62.9 1.2 %enter.4 = (bf16[128,1024]{1,0:T(8,128)(2,1)S(1)}, bf16[128,1024]{1,0:T(8,128)(2,1)S(1)}, f32[8,128]{1,0:T(8,128)}, f32[2,1,1024]{2,1,0:T(1,128)}, f32[2,1,1024]...) custom-call(f32[8,1024]{1,0:T(8,128)S(1)} %select_select_fusion.refs_11_.refs_0_, ...), custom_call_target="tpu_custom_call" | custom-call | flops 900000000 | tf_op jit(solution)/shard_map/enter/pallas_call | solution.py:469
  65.8 4.0 %collective-permute-start.16 = (bf16[128,1024]{1,0:T(8,128)(2,1)S(1)}, bf16[128,1024]{1,0:T(8,128)(2,1)S(1)}, u32[]{:S(2)}, u32[]{:S(2)}) collective-permute-start(bf16[128,1024]{1,0:T(8,128)(2,1)S(1)} %get-tuple-element.207), channel_id=1, source_target_pairs={{0,2},{1,3},{4,6},{5,7},{2,0},{3,1},{6,4},{7,5},{8,10},{9,11},{12,... | collective-permute-start | bytes 786440 | tf_op jit(solution)/shard_map/ppermute | solution.py:374
  70.5 1.6 %collective-permute-start.21 = (bf16[128,1024]{1,0:T(8,128)(2,1)S(1)}, bf16[128,1024]{1,0:T(8,128)(2,1)S(1)}, u32[]{:S(2)}, u32[]{:S(2)}) collective-permute-start(bf16[128,1024]{1,0:T(8,128)(2,1)S(1)} %get-tuple-element.225), channel_id=1, source_target_pairs={{0,1},{2,3},{4,5},{6,7},{1,0},{3,2},{5,4},{7,6},{8,9},{10,11},{12,... | collective-permute-start | bytes 786440 | tf_op jit(solution)/shard_map/ppermute | solution.py:374
  72.0 1.4 %collective-permute-done.17.refs_4_ = bf16[128,1024]{1,0:T(8,128)(2,1)S(1)} collective-permute-done((bf16[128,1024]{1,0:T(8,128)(2,1)S(1)}, bf16[128,1024]{1,0:T(8,128)(2,1)S(1)}, u32[]{:S(2)}, u32[]{:S(2)}) %collective-permute-start.17) | collective-permute-done | bytes 262176 | tf_op jit(solution)/shard_map/ppermute | solution.py:374
  73.5 1.8 %with_carry.4 = (bf16[256,8192]{1,0:T(8,128)(2,1)}, f32[8,128]{1,0:T(8,128)S(1)}) custom-call(f32[8,1024]{1,0:T(8,128)S(1)} %select_select_fusion.refs_11_.refs_0_, bf16[256,256]{1,0:T(8,128)(2,1)S(1)} %get-tuple-element.175.refs_2_.refs_1_, f32[256,2048]{1,0:T(8,128)S(1)} %get-tuple-element.208.refs_2_, bf16[128,1024]{1,0:T(8,128)(2,1)S(1)} %get-tuple-element.209.refs_3_, ...), custom_call_target="tpu_custom_call" | custom-call | flops 900000000 | tf_op jit(solution)/shard_map/with_carry/pallas_call | solution.py:350
  75.9 1.3 %collective-permute-start.24 = (bf16[128,1024]{1,0:T(8,128)(2,1)S(1)}, bf16[128,1024]{1,0:T(8,128)(2,1)S(1)}, u32[]{:S(2)}, u32[]{:S(2)}) collective-permute-start(bf16[128,1024]{1,0:T(8,128)(2,1)S(1)} %get-tuple-element.241), channel_id=1, source_target_pairs={{0,1},{2,3},{4,5},{6,7},{1,0},{3,2},{5,4},{7,6},{8,9},{10,11},{12,... | collective-permute-start | bytes 786440 | tf_op jit(solution)/shard_map/ppermute | solution.py:374
  77.2 2.2 %inside_block.7 = (f32[256,2048]{1,0:T(8,128)S(1)}, f32[8,128]{1,0:T(8,128)S(1)}) custom-call(bf16[256,2048]{1,0:T(8,128)(2,1)S(1)} %get-tuple-element.227.refs_0_, bf16[256,256]{1,0:T(8,128)(2,1)S(1)} %get-tuple-element.228.refs_1_, bf16[256,256]{1,0:T(8,128)(2,1)S(1)} %get-tuple-element.229.refs_2_.refs_1_, f32[8,256,16]{2,1,0:T(8,128)S(1)} %get-tuple-element.141.refs_3_, ...), custom_call_target="tpu_custom_call" | custom-call | flops 900000000 | tf_op jit(solution)/shard_map/inside_block/pallas_call | solution.py:311
  79.5 1.8 %with_carry.5 = (bf16[256,8192]{1,0:T(8,128)(2,1)}, f32[8,128]{1,0:T(8,128)S(1)}) custom-call(f32[8,1024]{1,0:T(8,128)S(1)} %select_select_fusion.refs_11_.refs_0_, bf16[256,256]{1,0:T(8,128)(2,1)S(1)} %get-tuple-element.202.refs_2_.refs_1_, f32[256,2048]{1,0:T(8,128)S(1)} %get-tuple-element.223.refs_2_, ...), custom_call_target="tpu_custom_call", output_to_operand_aliasing={{0}: (7, {})} | custom-call | flops 900000000 | tf_op jit(solution)/shard_map/with_carry/pallas_call | solution.py:350
  81.7 1.7 %collective-permute-start.23 = (bf16[128,1024]{1,0:T(8,128)(2,1)S(1)}, bf16[128,1024]{1,0:T(8,128)(2,1)S(1)}, u32[]{:S(2)}, u32[]{:S(2)}) collective-permute-start(bf16[128,1024]{1,0:T(8,128)(2,1)S(1)} %get-tuple-element.238), channel_id=1, source_target_pairs={{0,1},{2,3},{4,5},{6,7},{1,0},{3,2},{5,4},{7,6},{8,9},{10,11},{12,... | collective-permute-start | bytes 786440 | tf_op jit(solution)/shard_map/ppermute | solution.py:374
  83.4 1.8 %collective-permute-done.24.refs_4_ = bf16[128,1024]{1,0:T(8,128)(2,1)S(1)} collective-permute-done((bf16[128,1024]{1,0:T(8,128)(2,1)S(1)}, bf16[128,1024]{1,0:T(8,128)(2,1)S(1)}, u32[]{:S(2)}, u32[]{:S(2)}) %collective-permute-start.24) | collective-permute-done | bytes 262176 | tf_op jit(solution)/shard_map/ppermute | solution.py:374
  85.1 1.8 %with_carry.6 = (bf16[256,8192]{1,0:T(8,128)(2,1)}, f32[8,128]{1,0:T(8,128)S(1)}) custom-call(f32[8,1024]{1,0:T(8,128)S(1)} %select_select_fusion.refs_11_.refs_0_, bf16[256,256]{1,0:T(8,128)(2,1)S(1)} %get-tuple-element.229.refs_2_.refs_1_, f32[256,2048]{1,0:T(8,128)S(1)} %get-tuple-element.239.refs_2_, ...), custom_call_target="tpu_custom_call", output_to_operand_aliasing={{0}: (7, {})} | custom-call | flops 900000000 | tf_op jit(solution)/shard_map/with_carry/pallas_call | solution.py:350
  87.0 3.5 %collective-permute-done.23.refs_4_ = bf16[128,1024]{1,0:T(8,128)(2,1)S(1)} collective-permute-done((bf16[128,1024]{1,0:T(8,128)(2,1)S(1)}, bf16[128,1024]{1,0:T(8,128)(2,1)S(1)}, u32[]{:S(2)}, u32[]{:S(2)}) %collective-permute-start.23) | collective-permute-done | bytes 262176 | tf_op jit(solution)/shard_map/ppermute | solution.py:374
  90.5 1.8 %with_carry.7 = (bf16[256,8192]{1,0:T(8,128)(2,1)}, f32[8,128]{1,0:T(8,128)}) custom-call(f32[8,1024]{1,0:T(8,128)S(1)} %select_select_fusion.refs_11_.refs_0_, bf16[256,256]{1,0:T(8,128)(2,1)S(1)} %get-tuple-element.138.refs_2_.refs_1_, f32[256,2048]{1,0:T(8,128)S(1)} %get-tuple-element.170.refs_2_, ...), custom_call_target="tpu_custom_call", output_to_operand_aliasing={{0}: (7, {})} | custom-call | flops 900000000 | tf_op jit(solution)/shard_map/with_carry/pallas_call | solution.py:350
  (70 shorter events, 13.1 us)
Async XLA Ops:
  0.0 6.4 %copy-start.4 = (bf16[256,128]{1,0:T(8,128)(2,1)S(1)}, bf16[256,128]{1,0:T(8,128)(2,1)}, u32[]{:S(2)}) copy-start(bf16[256,128]{1,0:T(8,128)(2,1)} %dt_ref) | copy-start | bytes 196612
  0.0 6.4 %copy-start.6 = (f32[128]{0:T(128)S(1)}, f32[128]{0:T(128)}, u32[]{:S(2)}) copy-start(f32[128]{0:T(128)} %param.12) | copy-start | bytes 1540
  0.0 6.4 %copy-start.5 = (f32[128]{0:T(128)S(1)}, f32[128]{0:T(128)}, u32[]{:S(2)}) copy-start(f32[128]{0:T(128)} %param.11) | copy-start | bytes 1540
  1.1 7.3 %copy-start = (bf16[256,8192]{1,0:T(8,128)(2,1)S(1)}, bf16[256,8192]{1,0:T(8,128)(2,1)}, u32[]{:S(2)}) copy-start(bf16[256,8192]{1,0:T(8,128)(2,1)} %refs_0_.3) | copy-start | bytes 12582916
  1.1 7.2 %copy-start.1 = (bf16[256,1024]{1,0:T(8,128)(2,1)S(1)}, bf16[256,1024]{1,0:T(8,128)(2,1)}, u32[]{:S(2)}) copy-start(bf16[256,1024]{1,0:T(8,128)(2,1)} %refs_1_.7) | copy-start | bytes 1572868
  1.2 7.2 %copy-start.2 = (bf16[256,1024]{1,0:T(8,128)(2,1)S(1)}, bf16[256,1024]{1,0:T(8,128)(2,1)}, u32[]{:S(2)}) copy-start(bf16[256,1024]{1,0:T(8,128)(2,1)} %refs_2_.7) | copy-start | bytes 1572868
  1.2 7.2 %copy-start.3 = (bf16[4,10240]{1,0:T(4,128)(2,1)S(1)}, bf16[4,10240]{1,0:T(4,128)(2,1)}, u32[]{:S(2)}) copy-start(bf16[4,10240]{1,0:T(4,128)(2,1)} %refs_8_.7) | copy-start | bytes 245764
  1.2 7.2 %collective-permute-start = (bf16[3,10240]{1,0:T(4,128)(2,1)S(1)}, bf16[3,10240]{1,0:T(4,128)(2,1)S(1)}, u32[]{:S(2)}, u32[]{:S(2)}) collective-permute-start(bf16[3,10240]{1,0:T(4,128)(2,1)S(1)} %rim_rows.1), channel_id=1, source_target_pairs={{0,1},{1,2},{2,3},{3,4},{4,5},{5,6},{6,7},{7,8},{8,9},{9,10},{10,1... | collective-permute-start | bytes 184328 | tf_op jit(solution)/shard_map/ppermute | solution.py:704
  11.1 9.6 %collective-permute-start.1 = (bf16[144,1024]{1,0:T(8,128)(2,1)S(1)}, bf16[144,1024]{1,0:T(8,128)(2,1)S(1)}, u32[]{:S(2)}, u32[]{:S(2)}) collective-permute-start(bf16[144,1024]{1,0:T(8,128)(2,1)S(1)} %get-tuple-element.133), channel_id=1, source_target_pairs={{0,1},{2,3},{4,5},{6,7},{1,0},{3,2},{5,4},{7,6},{8,9},{10,11},{12,... | collective-permute-start | bytes 884744 | tf_op jit(solution)/shard_map/ppermute | solution.py:374
  16.3 12.4 %collective-permute-start.5 = (bf16[128,1024]{1,0:T(8,128)(2,1)S(1)}, bf16[128,1024]{1,0:T(8,128)(2,1)S(1)}, u32[]{:S(2)}, u32[]{:S(2)}) collective-permute-start(bf16[128,1024]{1,0:T(8,128)(2,1)S(1)} %get-tuple-element.153), channel_id=1, source_target_pairs={{0,1},{2,3},{4,5},{6,7},{1,0},{3,2},{5,4},{7,6},{8,9},{10,11},{12,... | collective-permute-start | bytes 786440 | tf_op jit(solution)/shard_map/ppermute | solution.py:374
  21.6 11.6 %collective-permute-start.4 = (bf16[144,1024]{1,0:T(8,128)(2,1)S(1)}, bf16[144,1024]{1,0:T(8,128)(2,1)S(1)}, u32[]{:S(2)}, u32[]{:S(2)}) collective-permute-start(bf16[144,1024]{1,0:T(8,128)(2,1)S(1)} %get-tuple-element.150.refs_1_), channel_id=1, source_target_pairs={{0,2},{1,3},{4,6},{5,7},{2,0},{3,1},{6,4},{7,5},{8,10},{9,11},{12,... | collective-permute-start | bytes 884744 | tf_op jit(solution)/shard_map/ppermute | solution.py:374
  25.4 9.4 %collective-permute-start.3 = (bf16[128,1024]{1,0:T(8,128)(2,1)S(1)}, bf16[128,1024]{1,0:T(8,128)(2,1)S(1)}, u32[]{:S(2)}, u32[]{:S(2)}) collective-permute-start(bf16[128,1024]{1,0:T(8,128)(2,1)S(1)} %get-tuple-element.148), channel_id=1, source_target_pairs={{0,1},{2,3},{4,5},{6,7},{1,0},{3,2},{5,4},{7,6},{8,9},{10,11},{12,... | collective-permute-start | bytes 786440 | tf_op jit(solution)/shard_map/ppermute | solution.py:374
  28.9 11.3 %collective-permute-start.8 = (bf16[128,1024]{1,0:T(8,128)(2,1)S(1)}, bf16[128,1024]{1,0:T(8,128)(2,1)S(1)}, u32[]{:S(2)}, u32[]{:S(2)}) collective-permute-start(bf16[128,1024]{1,0:T(8,128)(2,1)S(1)} %get-tuple-element.163.refs_1_), channel_id=1, source_target_pairs={{0,2},{1,3},{4,6},{5,7},{2,0},{3,1},{6,4},{7,5},{8,10},{9,11},{12,... | collective-permute-start | bytes 786440 | tf_op jit(solution)/shard_map/ppermute | solution.py:374
  34.1 6.9 %collective-permute-start.7 = (bf16[144,1024]{1,0:T(8,128)(2,1)S(1)}, bf16[144,1024]{1,0:T(8,128)(2,1)S(1)}, u32[]{:S(2)}, u32[]{:S(2)}) collective-permute-start(bf16[144,1024]{1,0:T(8,128)(2,1)S(1)} %get-tuple-element.160.refs_2_), channel_id=1, source_target_pairs={{2,4},{3,5},{4,2},{5,3},{10,12},{11,13},{12,10},{13,11},{18,20},{1... | collective-permute-start | bytes 884744 | tf_op jit(solution)/shard_map/ppermute | solution.py:374
  34.9 11.2 %collective-permute-start.6 = (bf16[128,1024]{1,0:T(8,128)(2,1)S(1)}, bf16[128,1024]{1,0:T(8,128)(2,1)S(1)}, u32[]{:S(2)}, u32[]{:S(2)}) collective-permute-start(bf16[128,1024]{1,0:T(8,128)(2,1)S(1)} %get-tuple-element.158.refs_1_), channel_id=1, source_target_pairs={{0,2},{1,3},{4,6},{5,7},{2,0},{3,1},{6,4},{7,5},{8,10},{9,11},{12,... | collective-permute-start | bytes 786440 | tf_op jit(solution)/shard_map/ppermute | solution.py:374
  38.9 8.1 %collective-permute-start.2 = (bf16[128,1024]{1,0:T(8,128)(2,1)S(1)}, bf16[128,1024]{1,0:T(8,128)(2,1)S(1)}, u32[]{:S(2)}, u32[]{:S(2)}) collective-permute-start(bf16[128,1024]{1,0:T(8,128)(2,1)S(1)} %get-tuple-element.145), channel_id=1, source_target_pairs={{0,1},{2,3},{4,5},{6,7},{1,0},{3,2},{5,4},{7,6},{8,9},{10,11},{12,... | collective-permute-start | bytes 786440 | tf_op jit(solution)/shard_map/ppermute | solution.py:374
  40.2 12.8 %collective-permute-start.12 = (bf16[128,1024]{1,0:T(8,128)(2,1)S(1)}, bf16[128,1024]{1,0:T(8,128)(2,1)S(1)}, u32[]{:S(2)}, u32[]{:S(2)}) collective-permute-start(bf16[128,1024]{1,0:T(8,128)(2,1)S(1)} %get-tuple-element.183.refs_2_), channel_id=1, source_target_pairs={{2,4},{3,5},{4,2},{5,3},{10,12},{11,13},{12,10},{13,11},{18,20},{1... | collective-permute-start | bytes 786440 | tf_op jit(solution)/shard_map/ppermute | solution.py:374
  41.3 12.7 %collective-permute-start.11 = (bf16[144,1024]{1,0:T(8,128)(2,1)S(1)}, bf16[144,1024]{1,0:T(8,128)(2,1)S(1)}, u32[]{:S(2)}, u32[]{:S(2)}) collective-permute-start(bf16[144,1024]{1,0:T(8,128)(2,1)S(1)} %get-tuple-element.180), channel_id=1, source_target_pairs={{0,2},{1,3},{4,6},{5,7},{2,0},{3,1},{6,4},{7,5},{8,10},{9,11},{12,... | collective-permute-start | bytes 884744 | tf_op jit(solution)/shard_map/ppermute | solution.py:374
  46.2 8.1 %collective-permute-start.10 = (bf16[128,1024]{1,0:T(8,128)(2,1)S(1)}, bf16[128,1024]{1,0:T(8,128)(2,1)S(1)}, u32[]{:S(2)}, u32[]{:S(2)}) collective-permute-start(bf16[128,1024]{1,0:T(8,128)(2,1)S(1)} %get-tuple-element.176.refs_2_), channel_id=1, source_target_pairs={{2,4},{3,5},{4,2},{5,3},{10,12},{11,13},{12,10},{13,11},{18,20},{1... | collective-permute-start | bytes 786440 | tf_op jit(solution)/shard_map/ppermute | solution.py:374
  47.0 12.6 %collective-permute-start.9 = (bf16[128,1024]{1,0:T(8,128)(2,1)S(1)}, bf16[128,1024]{1,0:T(8,128)(2,1)S(1)}, u32[]{:S(2)}, u32[]{:S(2)}) collective-permute-start(bf16[128,1024]{1,0:T(8,128)(2,1)S(1)} %get-tuple-element.171.refs_1_), channel_id=1, source_target_pairs={{0,2},{1,3},{4,6},{5,7},{2,0},{3,1},{6,4},{7,5},{8,10},{9,11},{12,... | collective-permute-start | bytes 786440 | tf_op jit(solution)/shard_map/ppermute | solution.py:374
  53.3 11.2 %collective-permute-start.14 = (bf16[128,1024]{1,0:T(8,128)(2,1)S(1)}, bf16[128,1024]{1,0:T(8,128)(2,1)S(1)}, u32[]{:S(2)}, u32[]{:S(2)}) collective-permute-start(bf16[128,1024]{1,0:T(8,128)(2,1)S(1)} %get-tuple-element.196), channel_id=1, source_target_pairs={{0,2},{1,3},{4,6},{5,7},{2,0},{3,1},{6,4},{7,5},{8,10},{9,11},{12,... | collective-permute-start | bytes 786440 | tf_op jit(solution)/shard_map/ppermute | solution.py:374
  54.2 8.6 %collective-permute-start.15 = (bf16[128,1024]{1,0:T(8,128)(2,1)S(1)}, bf16[128,1024]{1,0:T(8,128)(2,1)S(1)}, u32[]{:S(2)}, u32[]{:S(2)}) collective-permute-start(bf16[128,1024]{1,0:T(8,128)(2,1)S(1)} %get-tuple-element.197), channel_id=1, source_target_pairs={{0,8},{8,0},{1,9},{9,1},{2,10},{10,2},{3,11},{11,3},{4,12},{12,4},... | collective-permute-start | bytes 786440 | tf_op jit(solution)/shard_map/ppermute | solution.py:374
  54.5 15.3 %collective-permute-start.19 = (bf16[128,1024]{1,0:T(8,128)(2,1)S(1)}, bf16[128,1024]{1,0:T(8,128)(2,1)S(1)}, u32[]{:S(2)}, u32[]{:S(2)}) collective-permute-start(bf16[128,1024]{1,0:T(8,128)(2,1)S(1)} %get-tuple-element.215), channel_id=1, source_target_pairs={{0,2},{1,3},{4,6},{5,7},{2,0},{3,1},{6,4},{7,5},{8,10},{9,11},{12,... | collective-permute-start | bytes 786440 | tf_op jit(solution)/shard_map/ppermute | solution.py:374
  59.8 5.9 %collective-permute-start.13 = (bf16[128,1024]{1,0:T(8,128)(2,1)S(1)}, bf16[128,1024]{1,0:T(8,128)(2,1)S(1)}, u32[]{:S(2)}, u32[]{:S(2)}) collective-permute-start(bf16[128,1024]{1,0:T(8,128)(2,1)S(1)} %get-tuple-element.192.refs_2_), channel_id=1, source_target_pairs={{2,4},{3,5},{4,2},{5,3},{10,12},{11,13},{12,10},{13,11},{18,20},{1... | collective-permute-start | bytes 786440 | tf_op jit(solution)/shard_map/ppermute | solution.py:374
  64.6 5.5 %collective-permute-start.18 = (bf16[128,1024]{1,0:T(8,128)(2,1)S(1)}, bf16[128,1024]{1,0:T(8,128)(2,1)S(1)}, u32[]{:S(2)}, u32[]{:S(2)}) collective-permute-start(bf16[128,1024]{1,0:T(8,128)(2,1)S(1)} %get-tuple-element.212), channel_id=1, source_target_pairs={{0,8},{8,0},{1,9},{9,1},{2,10},{10,2},{3,11},{11,3},{4,12},{12,4},... | collective-permute-start | bytes 786440 | tf_op jit(solution)/shard_map/ppermute | solution.py:374
  64.7 8.7 %collective-permute-start.17 = (bf16[128,1024]{1,0:T(8,128)(2,1)S(1)}, bf16[128,1024]{1,0:T(8,128)(2,1)S(1)}, u32[]{:S(2)}, u32[]{:S(2)}) collective-permute-start(bf16[128,1024]{1,0:T(8,128)(2,1)S(1)} %get-tuple-element.210), channel_id=1, source_target_pairs={{0,1},{2,3},{4,5},{6,7},{1,0},{3,2},{5,4},{7,6},{8,9},{10,11},{12,... | collective-permute-start | bytes 786440 | tf_op jit(solution)/shard_map/ppermute | solution.py:374
  65.8 9.4 %collective-permute-start.16 = (bf16[128,1024]{1,0:T(8,128)(2,1)S(1)}, bf16[128,1024]{1,0:T(8,128)(2,1)S(1)}, u32[]{:S(2)}, u32[]{:S(2)}) collective-permute-start(bf16[128,1024]{1,0:T(8,128)(2,1)S(1)} %get-tuple-element.207), channel_id=1, source_target_pairs={{0,2},{1,3},{4,6},{5,7},{2,0},{3,1},{6,4},{7,5},{8,10},{9,11},{12,... | collective-permute-start | bytes 786440 | tf_op jit(solution)/shard_map/ppermute | solution.py:374
  70.1 5.5 %collective-permute-start.22 = (bf16[128,1024]{1,0:T(8,128)(2,1)S(1)}, bf16[128,1024]{1,0:T(8,128)(2,1)S(1)}, u32[]{:S(2)}, u32[]{:S(2)}) collective-permute-start(bf16[128,1024]{1,0:T(8,128)(2,1)S(1)} %get-tuple-element.230), channel_id=1, source_target_pairs={{0,8},{8,0},{1,9},{9,1},{2,10},{10,2},{3,11},{11,3},{4,12},{12,4},... | collective-permute-start | bytes 786440 | tf_op jit(solution)/shard_map/ppermute | solution.py:374
  70.5 9.0 %collective-permute-start.21 = (bf16[128,1024]{1,0:T(8,128)(2,1)S(1)}, bf16[128,1024]{1,0:T(8,128)(2,1)S(1)}, u32[]{:S(2)}, u32[]{:S(2)}) collective-permute-start(bf16[128,1024]{1,0:T(8,128)(2,1)S(1)} %get-tuple-element.225), channel_id=1, source_target_pairs={{0,1},{2,3},{4,5},{6,7},{1,0},{3,2},{5,4},{7,6},{8,9},{10,11},{12,... | collective-permute-start | bytes 786440 | tf_op jit(solution)/shard_map/ppermute | solution.py:374
  75.5 5.8 %collective-permute-start.20 = (bf16[128,1024]{1,0:T(8,128)(2,1)S(1)}, bf16[128,1024]{1,0:T(8,128)(2,1)S(1)}, u32[]{:S(2)}, u32[]{:S(2)}) collective-permute-start(bf16[128,1024]{1,0:T(8,128)(2,1)S(1)} %get-tuple-element.220), channel_id=1, source_target_pairs={{0,8},{8,0},{1,9},{9,1},{2,10},{10,2},{3,11},{11,3},{4,12},{12,4},... | collective-permute-start | bytes 786440 | tf_op jit(solution)/shard_map/ppermute | solution.py:374
  75.9 9.2 %collective-permute-start.24 = (bf16[128,1024]{1,0:T(8,128)(2,1)S(1)}, bf16[128,1024]{1,0:T(8,128)(2,1)S(1)}, u32[]{:S(2)}, u32[]{:S(2)}) collective-permute-start(bf16[128,1024]{1,0:T(8,128)(2,1)S(1)} %get-tuple-element.241), channel_id=1, source_target_pairs={{0,1},{2,3},{4,5},{6,7},{1,0},{3,2},{5,4},{7,6},{8,9},{10,11},{12,... | collective-permute-start | bytes 786440 | tf_op jit(solution)/shard_map/ppermute | solution.py:374
  81.7 8.8 %collective-permute-start.23 = (bf16[128,1024]{1,0:T(8,128)(2,1)S(1)}, bf16[128,1024]{1,0:T(8,128)(2,1)S(1)}, u32[]{:S(2)}, u32[]{:S(2)}) collective-permute-start(bf16[128,1024]{1,0:T(8,128)(2,1)S(1)} %get-tuple-element.238), channel_id=1, source_target_pairs={{0,1},{2,3},{4,5},{6,7},{1,0},{3,2},{5,4},{7,6},{8,9},{10,11},{12,... | collective-permute-start | bytes 786440 | tf_op jit(solution)/shard_map/ppermute | solution.py:374

commit v2 on v1

--- a/solution.py
+++ b/solution.py
@@ -31,7 +31,7 @@
 
 
 def cost(us, moved=0):
-    return pl.CostEstimate(flops=int(us * 9e8), bytes_accessed=moved, transcendentals=0)
+    return pl.CostEstimate(flops=int(us * 6e8), bytes_accessed=moved, transcendentals=0)
 
 
 def mark():
@@ -154,59 +154,21 @@
     )(*given)
 
 
-def convolved(ref, rim_ref, kernel_ref, scratch):
-    kernel = kernel_ref[...].astype(F32) * 0.5
-    width = ref.shape[1]
-    parts = []
-    for lo in range(0, width, 128):
-        sl = slice(lo, lo + 128)
-        scratch[PAD - RIM : PAD, :] = rim_ref[:, sl].astype(F32)
-        scratch[PAD : PAD + SPAN, :] = ref[:, sl].astype(F32)
-        half = kernel[RIM : RIM + 1, sl] * scratch[PAD : PAD + SPAN, :]
-        for tap in range(RIM):
-            first = PAD - RIM + tap
-            half = half + kernel[tap : tap + 1, sl] * scratch[first : first + SPAN, :]
-        parts.append((half + half * jnp.tanh(half)).astype(BF16))
-    return parts
-
-
-def states_body(
-    x_ref,
-    b_ref,
-    c_ref,
-    rim_x_ref,
-    rim_b_ref,
-    rim_c_ref,
-    kernel_x_ref,
-    kernel_b_ref,
-    kernel_c_ref,
-    to_end_ref,
-    spread_ref,
-    flag_ref,
-    last_ref,
-    values_ref,
-    conv_b_ref,
-    conv_c_ref,
-    keep_ref,
-    send_ref,
-    mark_ref,
-    scratch,
-):
-    mark_ref[...] = jnp.zeros_like(mark_ref)
-    (conv_b,) = convolved(b_ref, rim_b_ref, kernel_b_ref, scratch)
-    (conv_c,) = convolved(c_ref, rim_c_ref, kernel_c_ref, scratch)
-    conv_b_ref[...] = conv_b
-    conv_c_ref[...] = conv_c
-    parts = convolved(x_ref, rim_x_ref, kernel_x_ref, scratch)
-    for at, part in enumerate(parts):
-        values_ref[:, at * 128 : (at + 1) * 128] = part
-    gain = jnp.dot(to_end_ref[0], spread_ref[...], preferred_element_type=F32)
-    weighted = (values_ref[...].astype(F32) * gain).astype(BF16)
-    state = lax.dot_general(
-        conv_b, weighted, (((0,), (0,)), ((), ())), preferred_element_type=F32
-    ).astype(BF16)
+def convolved(now, rim, kernel, scratch):
+    kernel = kernel.astype(F32) * 0.5
+    tokens = now.shape[0]
+    now = now.astype(F32)
+    scratch[PAD - RIM : PAD, :] = rim.astype(F32)
+    scratch[PAD : PAD + tokens, :] = now
+    half = kernel[RIM : RIM + 1] * now
+    for tap in range(RIM):
+        first = PAD - RIM + tap
+        half = half + kernel[tap : tap + 1] * scratch[first : first + tokens, :]
+    return (half + half * jnp.tanh(half)).astype(BF16)
+
+
+def give_state(state, at, flag_ref, last_ref, keep_ref, send_ref):
     upper = flag_ref[:1] > 0.5
-    at = pl.program_id(0)
     rows = pl.ds(pl.multiple_of(at * HALF, HALF), HALF)
     keep_ref[rows, :] = jnp.where(upper, state[HALF:], state[:HALF])
     send_ref[rows, :] = jnp.where(upper, state[:HALF], state[HALF:])
@@ -214,57 +176,158 @@
         put_log(send_ref, keep_ref.shape[0], last_ref[...])
 
 
-def end_states(first, count, x, b, c, rim, conv_weight, to_end, spread, flags, last, after, us=1.0):
+def states_body(skipped, given, outs, scratch):
+    x_ref, b_ref, c_ref, kernel_x_ref, kernel_b_ref, kernel_c_ref, to_end_ref, spread_ref = given[:8]
+    values_ref, conv_b_ref, conv_c_ref = outs[:3]
+    rims = given[8:11] if not skipped else [None] * 3
+    tokens = x_ref.shape[0]
+
+    def conv(ref, rim_ref, kernel_ref, lo, turn):
+        sl = slice(lo, lo + 128)
+        rim = jnp.zeros((RIM, 128), F32) if rim_ref is None else rim_ref[:, sl]
+        return convolved(ref[:, sl], rim, kernel_ref[:, sl], scratch.at[turn])
+
+    conv_b = conv(b_ref, rims[1], kernel_b_ref, 0, 0)
+    conv_b_ref[...] = conv_b
+    conv_c_ref[...] = conv(c_ref, rims[2], kernel_c_ref, 0, 1)
+    gain = jnp.dot(to_end_ref[0], spread_ref[...], preferred_element_type=F32)
+    weighted = []
+    for at in range(x_ref.shape[1] // 128):
+        sl = slice(at * 128, (at + 1) * 128)
+        part = conv(x_ref, rims[0], kernel_x_ref, at * 128, at % 2)
+        values_ref[:, sl] = part
+        weighted.append((part.astype(F32) * gain[:, sl]).astype(BF16))
+    weighted = jnp.concatenate(weighted, axis=1)
+    return lax.dot_general(
+        conv_b[skipped:tokens],
+        weighted[skipped:tokens],
+        (((0,), (0,)), ((), ())),
+        preferred_element_type=F32,
+    )
+
+
+B_AT, C_AT = H * P_SIZE // N, H * P_SIZE // N + G
+
+
+def conv_specs(first, tokens):
     def cols(offset):
         return lambda i: (0, offset + first + i)
 
-    def own(i):
-        return (0, i)
-
-    def lead(i):
-        return (first + i, 0, 0)
-
-    b_at, c_at = H * P_SIZE // N, H * P_SIZE // N + G
+    return [
+        pl.BlockSpec((tokens, COLS), cols(0)),
+        pl.BlockSpec((tokens, N), cols(0)),
+        pl.BlockSpec((tokens, N), cols(0)),
+        pl.BlockSpec((KERNEL_TAPS, COLS), cols(0)),
+        pl.BlockSpec((KERNEL_TAPS, N), cols(B_AT)),
+        pl.BlockSpec((KERNEL_TAPS, N), cols(C_AT)),
+        pl.BlockSpec((1, tokens, 2 * HEADS), lambda i: (first + i, 0, 0)),
+        pl.BlockSpec((2 * HEADS, COLS), lambda i: (0, 0)),
+    ]
+
+
+def rim_specs(first):
+    def cols(offset):
+        return lambda i: (0, offset + first + i)
+
+    return [
+        pl.BlockSpec((RIM, COLS), cols(0)),
+        pl.BlockSpec((RIM, N), cols(B_AT)),
+        pl.BlockSpec((RIM, N), cols(C_AT)),
+    ]
+
+
+def value_specs(tokens):
+    return [pl.BlockSpec((tokens, width), lambda i: (0, i)) for width in (COLS, N, N)]
+
+
+def value_shapes(count):
+    return [jax.ShapeDtypeStruct((SPAN, count * width), BF16) for width in (COLS, N, N)]
+
+
+def state_outs(first, count):
+    rows = count * HALF
+    shapes = [(rows, COLS), (rows + log_rows(first), COLS)]
+    shapes = [jax.ShapeDtypeStruct(a, BF16) for a in shapes]
+    return shapes + [mark()], [whole(a) for a in shapes] + [MARK]
+
+
+def early_states(first, count, x, b, c, conv_weight, to_end, spread, after):
+    def body(*refs):
+        outs = refs[8 + len(after) :]
+        outs[3][0] = states_body(TILE, refs[:8], outs, outs[-1])
+        outs[4][...] = jnp.zeros_like(outs[4])
+
     return pl.pallas_call(
-        lambda *refs: states_body(*refs[:13], *refs[13 + len(after) :]),
+        body,
         grid=(count,),
-        in_specs=[
-            pl.BlockSpec((SPAN, COLS), cols(0)),
-            pl.BlockSpec((SPAN, N), cols(0)),
-            pl.BlockSpec((SPAN, N), cols(0)),
-            pl.BlockSpec((RIM, COLS), cols(0)),
-            pl.BlockSpec((RIM, N), cols(b_at)),
-            pl.BlockSpec((RIM, N), cols(c_at)),
-            pl.BlockSpec((KERNEL_TAPS, COLS), cols(0)),
-            pl.BlockSpec((KERNEL_TAPS, N), cols(b_at)),
-            pl.BlockSpec((KERNEL_TAPS, N), cols(c_at)),
-            pl.BlockSpec((1, SPAN, 2 * HEADS), lead),
-            pl.BlockSpec((2 * HEADS, COLS), lambda i: (0, 0)),
-            whole(flags),
-            whole(last),
-        ]
+        in_specs=conv_specs(first, SPAN) + [corner(a) for a in after],
+        out_specs=value_specs(SPAN) + [pl.BlockSpec((1, N, COLS), lambda i: (i, 0, 0)), MARK],
+        out_shape=value_shapes(count)
+        + [jax.ShapeDtypeStruct((count, N, COLS), F32), mark()],
+        scratch_shapes=[pltpu.VMEM((2, PAD + SPAN, 128), F32)],
+        compiler_params=params(),
+        cost_estimate=cost(1.0),
+        name="early_states",
+    )(x, b, c, conv_weight, conv_weight, conv_weight, to_end, spread, *after)
+
+
+def late_states(first, count, early, x, b, c, rim, conv_weight, to_end, spread, flags, last, us):
+    values, conv_b, conv_c, partial, token = early
+
+    def body(*refs):
+        flag_ref, last_ref, partial_ref = refs[11:14]
+        outs = refs[18:]
+        state = states_body(0, refs[:11], outs, outs[-1]) + partial_ref[0]
+        give_state(state.astype(BF16), pl.program_id(0), flag_ref, last_ref, *outs[3:5])
+        outs[5][...] = jnp.zeros_like(outs[5])
+
+    shapes, specs = state_outs(first, count)
+    return pl.pallas_call(
+        body,
+        grid=(count,),
+        in_specs=conv_specs(first, TILE)
+        + rim_specs(first)
+        + [whole(flags), whole(last), pl.BlockSpec((1, N, COLS), lambda i: (i, 0, 0))]
+        + [pl.BlockSpec(memory_space=pl.ANY)] * 3
+        + [corner(token)],
+        out_specs=value_specs(TILE) + specs,
+        out_shape=value_shapes(count) + shapes,
+        input_output_aliases={14: 0, 15: 1, 16: 2},
+        scratch_shapes=[pltpu.VMEM((2, PAD + SPAN, 128), F32)],
+        compiler_params=params(),
+        cost_estimate=cost(us),
+        name="late_states",
+    )(
+        x, b, c, conv_weight, conv_weight, conv_weight, to_end, spread, rim, rim, rim,
+        flags, last, partial, values, conv_b, conv_c, token,
+    )
+
+
+def end_states(first, count, x, b, c, rim, conv_weight, to_end, spread, flags, last, after, us=1.0):
+    def body(*refs):
+        outs = refs[13 + len(after) :]
+        state = states_body(0, refs[:11], outs, outs[-1])
+        give_state(state.astype(BF16), pl.program_id(0), *refs[11:13], *outs[3:5])
+        outs[5][...] = jnp.zeros_like(outs[5])
+
+    shapes, specs = state_outs(first, count)
+    return pl.pallas_call(
+        body,
+        grid=(count,),
+        in_specs=conv_specs(first, SPAN)
+        + rim_specs(first)
+        + [whole(flags), whole(last)]
         + [corner(a) for a in after],
-        out_specs=[
-            pl.BlockSpec((SPAN, COLS), own),
-            pl.BlockSpec((SPAN, N), own),
-            pl.BlockSpec((SPAN, N), own),
-            pl.BlockSpec((count * HALF, COLS), lambda i: (0, 0)),
-            pl.BlockSpec((count * HALF + log_rows(first), COLS), lambda i: (0, 0)),
-            MARK,
-        ],
-        out_shape=[
-            jax.ShapeDtypeStruct((SPAN, count * COLS), BF16),
-            jax.ShapeDtypeStruct((SPAN, count * N), BF16),
-            jax.ShapeDtypeStruct((SPAN, count * N), BF16),
-            jax.ShapeDtypeStruct((count * HALF, COLS), BF16),
-            jax.ShapeDtypeStruct((count * HALF + log_rows(first), COLS), BF16),
-            mark(),
-        ],
-        scratch_shapes=[pltpu.VMEM((PAD + SPAN, 128), F32)],
+        out_specs=value_specs(SPAN) + specs,
+        out_shape=value_shapes(count) + shapes,
+        scratch_shapes=[pltpu.VMEM((2, PAD + SPAN, 128), F32)],
         compiler_params=params(),
         cost_estimate=cost(us),
         name="end_states",
-    )(x, b, c, rim, rim, rim, conv_weight, conv_weight, conv_weight, to_end, spread, flags, last, *after)
+    )(
+        x, b, c, conv_weight, conv_weight, conv_weight, to_end, spread, rim, rim, rim,
+        flags, last, *after,
+    )
 
 
 def inside_body(values_ref, b_ref, c_ref, cols_ref, rows_ref, skip_ref, part_ref, mark_ref):
@@ -399,13 +462,13 @@
 FAR_PAIRS = [(0, 4), (1, 5), (2, 6), (3, 7)]
 
 ORDER = (
-    [("state", 0, 1.0), ("state", 1, 1.0), ("state", 2, 1.0), ("chip", 0, 1.0)]
+    [("early", 0, 1.0), ("state", 0, 1.0), ("state", 1, 1.0), ("state", 2, 1.0), ("chip", 0, 1.0)]
     + [("state", 3, 1.0), ("chip", 1, 1.0), ("chips", 0, 1.0), ("chip", 2, 1.0)]
-    + [("chips", 1, 1.0), ("link", 0, 1.0), ("chips", 2, 1.0), ("chip", 3, 1.0)]
-    + [("inside", 3, 1.0), ("link", 1, 1.0), ("total", 0, 1.0), ("link", 2, 1.0)]
-    + [("inside", 0, 1.0), ("chips", 3, 1.0), ("inside", 1, 1.0), ("leave", 0, 1.0)]
-    + [("total", 1, 1.0), ("link", 3, 1.0), ("total", 2, 1.0), ("leave", 1, 1.0)]
-    + [("out", 0, 1.0), ("total", 3, 1.0), ("leave", 2, 1.0), ("inside", 2, 1.0)]
+    + [("chips", 1, 1.0), ("chip", 3, 1.0), ("link", 0, 1.0), ("chips", 2, 1.0)]
+    + [("inside", 0, 1.0), ("inside", 1, 1.0), ("link", 1, 1.0), ("chips", 3, 1.0)]
+    + [("inside", 3, 1.0), ("total", 0, 1.0), ("link", 2, 1.0), ("link", 3, 1.0)]
+    + [("total", 1, 1.0), ("leave", 0, 1.0), ("inside", 2, 1.0), ("total", 2, 1.0)]
+    + [("leave", 1, 1.0), ("out", 0, 1.0), ("total", 3, 1.0), ("leave", 2, 1.0)]
     + [("out", 1, 1.0), ("leave", 3, 1.0), ("out", 2, 1.0), ("out", 3, 1.0)]
 )
 
@@ -427,12 +490,13 @@
     out = [jax.ShapeDtypeStruct((rows, COLS), BF16)] * outs
     given += weights
     if lead is not None:
-        step, known, wanted, sends = lead
+        step, known, used, keeps, sends = lead
+        asked = [(n, own or at > 0) for own in used for at, n in enumerate(CHUNKS)]
         given += [spread, known]
         if sends:
             out = [jax.ShapeDtypeStruct((rows + TILE, COLS), BF16)]
-        out.append(jax.ShapeDtypeStruct((8, H), F32))
-        out += [jax.ShapeDtypeStruct((n, 1, COLS), F32) for n in CHUNKS] * wanted
+        out += [jax.ShapeDtypeStruct((8, H), F32)] * keeps
+        out += [jax.ShapeDtypeStruct((n, 1, COLS), F32) for n, given_out in asked if given_out]
     out.append(mark())
 
     def run(*refs):
@@ -445,21 +509,24 @@
         scales = [[r[at] for r in scale_refs] for at in range(count)]
         if lead is not None:
             logs = [take_log(r, rows) if r.shape[0] > rows else None for r in ins]
-            found, keeps, onward = step([a[:, :H] for a in on], logs, rest[1][...])
-            empty = jnp.zeros((8 - len(keeps), H), F32)
-            results[outs][...] = jnp.concatenate(keeps + [empty], axis=0)
+            found, kept, onward = step([a[:, :H] for a in on], logs, rest[1][...])
+            if keeps:
+                empty = jnp.zeros((8 - len(kept), H), F32)
+                results[outs][...] = jnp.concatenate(kept + [empty], axis=0)
             if sends:
                 put_log(results[0], rows, onward)
             found = [by_column(row, rest[0][...], 2) for row in found]
             scales = [[f[at : at + 1] for f in found] + scales[at] for at in range(count)]
-            at = outs + 1
-            for value in found:
-                first = 0
-                for n in CHUNKS:
+            at = outs + keeps
+            first = 0
+            for number, (n, given_out) in enumerate(asked):
+                value = found[number // len(CHUNKS)]
+                first = 0 if number % len(CHUNKS) == 0 else first
+                if given_out:
                     for group in range(n):
                         results[at][group] = value[first + group : first + group + 1]
-                    first += n
                     at += 1
+                first += n
         for at in range(count):
             part = slice(at * HALF, (at + 1) * HALF)
             values = body(on, [r[part, :].astype(F32) for r in ins], scales[at])
@@ -478,9 +545,11 @@
     )(*given, *after)
     if lead is None:
         return found[:outs], found[-1], None, None
+    new = list(found[outs + keeps : -1])
+    scales = [new.pop(0) if given_out else None for _, given_out in asked]
     n = len(CHUNKS)
-    scales = [found[outs + 1 + n * at : outs + 1 + n * (at + 1)] for at in range(wanted)]
-    return found[:outs], found[-1], found[outs], scales
+    scales = [scales[n * at : n * (at + 1)] for at in range(len(used))]
+    return found[:outs], found[-1], found[outs] if keeps else None, scales
 
 
 def add_chip(on, arrays, scales):
@@ -561,7 +630,10 @@
 
     def merged(body, k, names, scales, logs, wanted, outs=1, sends=True):
         nonlocal known
-        lead = (logs, known, len(wanted), sends) if k == 0 and logs is not None else None
+        lead = None
+        if k == 0 and logs is not None:
+            used = [name not in ("above", "high", "reach") for name in wanted]
+            lead = (logs, known, used, int(sends), sends)
         if lead is None:
             scales = wanted + scales
         found, mark, keeps, new = merge(
@@ -582,10 +654,15 @@
 
     for what, k, us in ORDER:
         first, count = starts[k], CHUNKS[k]
-        if what == "state":
-            found = end_states(
-                first, count, x, b, c, rim, conv_weight, to_end, spread, flags, last, after, us
-            )
+        if what == "early":
+            early = early_states(first, count, x, b, c, conv_weight, to_end, spread, after)
+            done["early", k], mark = early, early[-1]
+        elif what == "state":
+            given = (x, b, c, rim, conv_weight, to_end, spread, flags, last)
+            if ("early", k) in done:
+                found = late_states(first, count, done["early", k], *given, us)
+            else:
+                found = end_states(first, count, *given, after, us)
             done["values", k], done["b", k], done["c", k], keep, send, mark = found
             done["keep", k], done["y", k] = keep, swap(send, "inner", Y_PAIRS)
         elif what == "inside":

time: 92.5 us -> 89 us (0.962)
  starting transfers between devices: 41 us -> 37.3 us
  waiting for transfers between devices: 15 us -> 17.1 us
  Pallas kernels: 35.8 us -> 33.8 us
    ppermute x24, starting transfers between devices: 35.8 us -> 32.3 us  [swap(): return lax.ppermute(value, axis, pairs + [(b, a) for a, b in pairs])]
    ppermute x24, waiting for transfers between devices: 14.3 us -> 17.1 us  [swap(): return lax.ppermute(value, axis, pairs + [(b, a) for a, b in pairs])]
    pallas_call x20, Pallas kernels: 6.51 us -> 4.73 us  [merge(): pl.pallas_call(run, grid=(1,), in_specs=[whole(a) for a in given] + [corn...]
    pallas_call x4 -> x5, Pallas kernels: 10.8 us -> 10.5 us  [the longest x3 7.32 us: end_states(): pl.pallas_call(body, grid=(count,), in_specs=conv_specs(first, SPAN) + ri...]
  transfers between devices with their start and end apart: 25 -> 25, of which waited for: 9 -> 12; matrix products, arithmetic and copies ran while one was open for 0% -> 0% of each run, Pallas kernels for 33% -> 34%
where the time goes in v2:
time: 89 us; the launch traced here: 88.8 us
  starting transfers between devices  37.3 us (42%)
  Pallas kernels  33.8 us (38%)
  waiting for transfers between devices  17.1 us (19%)
    ppermute x24, starting transfers between devices, swap(): return lax.ppermute(value, axis, pairs + [(b, a) for a, b in pairs])  32.3 us
    ppermute x24, waiting for transfers between devices, swap(): return lax.ppermute(value, axis, pairs + [(b, a) for a, b in pairs])  17.1 us
    pallas_call x4, Pallas kernels, inside_block(): pl.pallas_call(lambda *refs: inside_body(*refs[:6], *refs[6 + len(after):...  8.92 us
    pallas_call x3, Pallas kernels, end_states(): pl.pallas_call(body, grid=(count,), in_specs=conv_specs(first, SPAN) + ri...  7.32 us
    pallas_call x4, Pallas kernels, with_carry(): pl.pallas_call(carried_body, grid=(count,), in_specs=[whole(side), pl.Blo...  7.23 us
    ppermute x1, starting transfers between devices, shards(): lax.ppermute(rim_rows(x_stream, b_stream, c_stream), ('outer', 'inner'),...  5.02 us
    pallas_call x20, Pallas kernels, merge(): pl.pallas_call(run, grid=(1,), in_specs=[whole(a) for a in given] + [corn...  4.73 us
    pallas_call x1, Pallas kernels, early_states(): pl.pallas_call(body, grid=(count,), in_specs=conv_specs(first, SPAN) + [c...  2.4 us
  transfers between devices with their start and end apart: 25, of which 12 were waited for; matrix products, arithmetic and copies ran while one was open for 0% of the time, Pallas kernels for 34%

profile of v2, /device:TPU:0, one launch (start us, length us, event | category | flops | bytes accessed | tf_op | source)
XLA Modules:
  0.0 88.8 jit_solution(17382539975289063288)
XLA Ops:
  1.3 5.0 %collective-permute-start = (bf16[3,10240]{1,0:T(4,128)(2,1)S(1)}, bf16[3,10240]{1,0:T(4,128)(2,1)S(1)}, u32[]{:S(2)}, u32[]{:S(2)}) collective-permute-start(bf16[3,10240]{1,0:T(4,128)(2,1)S(1)} %rim_rows.1), channel_id=1, source_target_pairs={{0,1},{1,2},{2,3},{3,4},{4,5},{5,6},{6,7},{7,8},{8,9},{9,10},{10,1... | collective-permute-start | bytes 184328 | tf_op jit(solution)/shard_map/ppermute | solution.py:781
  6.4 1.3 %time_steps.1 = (f32[8,256,16]{2,1,0:T(8,128)S(1)}, f32[128,256]{1,0:T(8,128)S(1)}, bf16[8,256,32]{2,1,0:T(8,128)(2,1)S(1)}, bf16[8,256,32]{2,1,0:T(8,128)(2,1)S...) custom-call(bf16[256,128]{1,0:T(8,128)(2,1)S(1)} %copy-done.4, ...), custom_call_target="tpu_custom_call" | custom-call | flops 1200000000 | tf_op jit(solution)/shard_map/time_steps/pallas_call | solution.py:145
  7.7 2.4 %early_states.1 = (bf16[256,2048]{1,0:T(8,128)(2,1)S(1)}, bf16[256,256]{1,0:T(8,128)(2,1)S(1)}, bf16[256,256]{1,0:T(8,128)(2,1)S(1)}, f32[2,128,1024]{2,1,0:T(8,128)S(1)}, f32[8,128]{1,0:T(8,128)S(1)}) custom-call(bf16[256,8192]{1,0:T(8,128)(2,1)S(1)} %copy-done, bf16[256,1024]{1,0:T(8,128)(2,1)S(1)} %copy-done.1, bf16[256,1024]{1,0:T(8,128)(2,1)S(1)} %copy-done.2, ...), custom_call_target="tpu_custom_call" | custom-call | flops 600000000 | tf_op jit(solution)/shard_map/early_states/pallas_call | solution.py:260
  10.9 1.6 %collective-permute-start.1 = (bf16[144,1024]{1,0:T(8,128)(2,1)S(1)}, bf16[144,1024]{1,0:T(8,128)(2,1)S(1)}, u32[]{:S(2)}, u32[]{:S(2)}) collective-permute-start(bf16[144,1024]{1,0:T(8,128)(2,1)S(1)} %get-tuple-element.143), channel_id=1, source_target_pairs={{0,1},{2,3},{4,5},{6,7},{1,0},{3,2},{5,4},{7,6},{8,9},{10,11},{12,... | collective-permute-start | bytes 884744 | tf_op jit(solution)/shard_map/ppermute | solution.py:437
  12.5 2.4 %end_states.3 = (bf16[256,2048]{1,0:T(8,128)(2,1)S(1)}, bf16[256,256]{1,0:T(8,128)(2,1)S(1)}, bf16[256,256]{1,0:T(8,128)(2,1)S(1)}, bf16[128,1024]{1,0:T(8,128)(...) custom-call(bf16[256,8192]{1,0:T(8,128)(2,1)S(1)} %copy-done, bf16[256,1024]{1,0:T(8,128)(2,1)S(1)} %copy-done.1, ...), custom_call_target="tpu_custom_call" | custom-call | flops 600000000 | tf_op jit(solution)/shard_map/end_states/pallas_call | solution.py:314
  15.5 2.4 %end_states.4 = (bf16[256,2048]{1,0:T(8,128)(2,1)S(1)}, bf16[256,256]{1,0:T(8,128)(2,1)S(1)}, bf16[256,256]{1,0:T(8,128)(2,1)S(1)}, bf16[128,1024]{1,0:T(8,128)(...) custom-call(bf16[256,8192]{1,0:T(8,128)(2,1)S(1)} %copy-done, bf16[256,1024]{1,0:T(8,128)(2,1)S(1)} %copy-done.1, ...), custom_call_target="tpu_custom_call" | custom-call | flops 600000000 | tf_op jit(solution)/shard_map/end_states/pallas_call | solution.py:314
  18.0 2.5 %collective-permute-done.1.refs_2_ = bf16[144,1024]{1,0:T(8,128)(2,1)S(1)} collective-permute-done((bf16[144,1024]{1,0:T(8,128)(2,1)S(1)}, bf16[144,1024]{1,0:T(8,128)(2,1)S(1)}, u32[]{:S(2)}, u32[]{:S(2)}) %collective-permute-start.1) | collective-permute-done | bytes 294944 | tf_op jit(solution)/shard_map/ppermute | solution.py:437
  20.8 2.1 %collective-permute-start.5 = (bf16[144,1024]{1,0:T(8,128)(2,1)S(1)}, bf16[144,1024]{1,0:T(8,128)(2,1)S(1)}, u32[]{:S(2)}, u32[]{:S(2)}) collective-permute-start(bf16[144,1024]{1,0:T(8,128)(2,1)S(1)} %get-tuple-element.162.refs_1_), channel_id=1, source_target_pairs={{0,2},{1,3},{4,6},{5,7},{2,0},{3,1},{6,4},{7,5},{8,10},{9,11},{12,... | collective-permute-start | bytes 884744 | tf_op jit(solution)/shard_map/ppermute | solution.py:437
  22.9 1.5 %collective-permute-start.6 = (bf16[128,1024]{1,0:T(8,128)(2,1)S(1)}, bf16[128,1024]{1,0:T(8,128)(2,1)S(1)}, u32[]{:S(2)}, u32[]{:S(2)}) collective-permute-start(bf16[128,1024]{1,0:T(8,128)(2,1)S(1)} %get-tuple-element.167), channel_id=1, source_target_pairs={{0,1},{2,3},{4,5},{6,7},{1,0},{3,2},{5,4},{7,6},{8,9},{10,11},{12,... | collective-permute-start | bytes 786440 | tf_op jit(solution)/shard_map/ppermute | solution.py:437
  24.4 2.4 %end_states.5 = (bf16[256,2048]{1,0:T(8,128)(2,1)S(1)}, bf16[256,256]{1,0:T(8,128)(2,1)S(1)}, bf16[256,256]{1,0:T(8,128)(2,1)S(1)}, bf16[128,1024]{1,0:T(8,128)(...) custom-call(bf16[256,8192]{1,0:T(8,128)(2,1)S(1)} %copy-done, bf16[256,1024]{1,0:T(8,128)(2,1)S(1)} %copy-done.1, ...), custom_call_target="tpu_custom_call" | custom-call | flops 600000000 | tf_op jit(solution)/shard_map/end_states/pallas_call | solution.py:314
  27.4 2.4 %collective-permute-start.2 = (bf16[128,1024]{1,0:T(8,128)(2,1)S(1)}, bf16[128,1024]{1,0:T(8,128)(2,1)S(1)}, u32[]{:S(2)}, u32[]{:S(2)}) collective-permute-start(bf16[128,1024]{1,0:T(8,128)(2,1)S(1)} %get-tuple-element.155), channel_id=1, source_target_pairs={{0,1},{2,3},{4,5},{6,7},{1,0},{3,2},{5,4},{7,6},{8,9},{10,11},{12,... | collective-permute-start | bytes 786440 | tf_op jit(solution)/shard_map/ppermute | solution.py:437
  32.2 2.8 %collective-permute-start.10 = (bf16[128,1024]{1,0:T(8,128)(2,1)S(1)}, bf16[128,1024]{1,0:T(8,128)(2,1)S(1)}, u32[]{:S(2)}, u32[]{:S(2)}) collective-permute-start(bf16[128,1024]{1,0:T(8,128)(2,1)S(1)} %get-tuple-element.188.refs_1_), channel_id=1, source_target_pairs={{0,2},{1,3},{4,6},{5,7},{2,0},{3,1},{6,4},{7,5},{8,10},{9,11},{12,... | collective-permute-start | bytes 786440 | tf_op jit(solution)/shard_map/ppermute | solution.py:437
  35.0 1.3 %collective-permute-done.4.refs_2_.refs_3_ = bf16[128,1024]{1,0:T(8,128)(2,1)S(1)} collective-permute-done((bf16[128,1024]{1,0:T(8,128)(2,1)S(1)}, bf16[128,1024]{1,0:T(8,128)(2,1)S(1)}, u32[]{:S(2)}, u32[]{:S(2)}) %collective-permute-start.4) | collective-permute-done | bytes 262176 | tf_op jit(solution)/shard_map/ppermute | solution.py:437
  37.8 2.2 %collective-permute-start.7 = (bf16[128,1024]{1,0:T(8,128)(2,1)S(1)}, bf16[128,1024]{1,0:T(8,128)(2,1)S(1)}, u32[]{:S(2)}, u32[]{:S(2)}) collective-permute-start(bf16[128,1024]{1,0:T(8,128)(2,1)S(1)} %get-tuple-element.172.refs_1_), channel_id=1, source_target_pairs={{0,2},{1,3},{4,6},{5,7},{2,0},{3,1},{6,4},{7,5},{8,10},{9,11},{12,... | collective-permute-start | bytes 786440 | tf_op jit(solution)/shard_map/ppermute | solution.py:437
  40.4 2.2 %collective-permute-start.13 = (bf16[144,1024]{1,0:T(8,128)(2,1)S(1)}, bf16[144,1024]{1,0:T(8,128)(2,1)S(1)}, u32[]{:S(2)}, u32[]{:S(2)}) collective-permute-start(bf16[144,1024]{1,0:T(8,128)(2,1)S(1)} %get-tuple-element.205), channel_id=1, source_target_pairs={{0,2},{1,3},{4,6},{5,7},{2,0},{3,1},{6,4},{7,5},{8,10},{9,11},{12,... | collective-permute-start | bytes 884744 | tf_op jit(solution)/shard_map/ppermute | solution.py:437
  43.5 2.2 %inside_block.4 = (f32[256,2048]{1,0:T(8,128)S(1)}, f32[8,128]{1,0:T(8,128)S(1)}) custom-call(bf16[256,2048]{1,0:T(8,128)(2,1)S(1)} %get-tuple-element.185.refs_0_, bf16[256,256]{1,0:T(8,128)(2,1)S(1)} %get-tuple-element.186.refs_1_, bf16[256,256]{1,0:T(8,128)(2,1)S(1)} %get-tuple-element.187.refs_2_.refs_1_, f32[8,256,16]{2,1,0:T(8,128)S(1)} %get-tuple-element.151.refs_3_, ...), custom_call_target="tpu_custom_call" | custom-call | flops 600000000 | tf_op jit(solution)/shard_map/inside_block/pallas_call | solution.py:374
  45.7 2.2 %inside_block.5 = (f32[256,2048]{1,0:T(8,128)S(1)}, f32[8,128]{1,0:T(8,128)S(1)}) custom-call(bf16[256,2048]{1,0:T(8,128)(2,1)S(1)} %get-tuple-element.182.refs_0_, bf16[256,256]{1,0:T(8,128)(2,1)S(1)} %get-tuple-element.183.refs_1_, bf16[256,256]{1,0:T(8,128)(2,1)S(1)} %get-tuple-element.184.refs_2_.refs_1_, f32[8,256,16]{2,1,0:T(8,128)S(1)} %get-tuple-element.151.refs_3_, ...), custom_call_target="tpu_custom_call" | custom-call | flops 600000000 | tf_op jit(solution)/shard_map/inside_block/pallas_call | solution.py:374
  49.2 5.3 %collective-permute-start.16 = (bf16[128,1024]{1,0:T(8,128)(2,1)S(1)}, bf16[128,1024]{1,0:T(8,128)(2,1)S(1)}, u32[]{:S(2)}, u32[]{:S(2)}) collective-permute-start(bf16[128,1024]{1,0:T(8,128)(2,1)S(1)} %get-tuple-element.216), channel_id=1, source_target_pairs={{0,2},{1,3},{4,6},{5,7},{2,0},{3,1},{6,4},{7,5},{8,10},{9,11},{12,... | collective-permute-start | bytes 786440 | tf_op jit(solution)/shard_map/ppermute | solution.py:437
  54.5 2.2 %inside_block.6 = (f32[256,2048]{1,0:T(8,128)S(1)}, f32[8,128]{1,0:T(8,128)S(1)}) custom-call(bf16[256,2048]{1,0:T(8,128)(2,1)S(1)} %get-tuple-element.149.refs_0_, bf16[256,256]{1,0:T(8,128)(2,1)S(1)} %get-tuple-element.150.refs_1_, bf16[256,256]{1,0:T(8,128)(2,1)S(1)} %get-tuple-element.148.refs_2_.refs_1_, f32[8,256,16]{2,1,0:T(8,128)S(1)} %get-tuple-element.151.refs_3_, ...), custom_call_target="tpu_custom_call" | custom-call | flops 600000000 | tf_op jit(solution)/shard_map/inside_block/pallas_call | solution.py:374
  57.5 2.0 %collective-permute-done.16.refs_4_.refs_5_ = bf16[128,1024]{1,0:T(8,128)(2,1)S(1)} collective-permute-done((bf16[128,1024]{1,0:T(8,128)(2,1)S(1)}, bf16[128,1024]{1,0:T(8,128)(2,1)S(1)}, u32[]{:S(2)}, u32[]{:S(2)}) %collective-permute-start.16) | collective-permute-done | bytes 262176 | tf_op jit(solution)/shard_map/ppermute | solution.py:437
  61.3 2.2 %collective-permute-start.14 = (bf16[128,1024]{1,0:T(8,128)(2,1)S(1)}, bf16[128,1024]{1,0:T(8,128)(2,1)S(1)}, u32[]{:S(2)}, u32[]{:S(2)}) collective-permute-start(bf16[128,1024]{1,0:T(8,128)(2,1)S(1)} %get-tuple-element.211), channel_id=1, source_target_pairs={{0,2},{1,3},{4,6},{5,7},{2,0},{3,1},{6,4},{7,5},{8,10},{9,11},{12,... | collective-permute-start | bytes 786440 | tf_op jit(solution)/shard_map/ppermute | solution.py:437
  63.5 2.2 %inside_block.7 = (f32[256,2048]{1,0:T(8,128)S(1)}, f32[8,128]{1,0:T(8,128)S(1)}) custom-call(bf16[256,2048]{1,0:T(8,128)(2,1)S(1)} %get-tuple-element.226.refs_0_, bf16[256,256]{1,0:T(8,128)(2,1)S(1)} %get-tuple-element.227.refs_1_, bf16[256,256]{1,0:T(8,128)(2,1)S(1)} %get-tuple-element.228.refs_2_.refs_1_, f32[8,256,16]{2,1,0:T(8,128)S(1)} %get-tuple-element.151.refs_3_, ...), custom_call_target="tpu_custom_call" | custom-call | flops 600000000 | tf_op jit(solution)/shard_map/inside_block/pallas_call | solution.py:374
  67.0 1.6 %collective-permute-start.21 = (bf16[128,1024]{1,0:T(8,128)(2,1)S(1)}, bf16[128,1024]{1,0:T(8,128)(2,1)S(1)}, u32[]{:S(2)}, u32[]{:S(2)}) collective-permute-start(bf16[128,1024]{1,0:T(8,128)(2,1)S(1)} %get-tuple-element.239), channel_id=1, source_target_pairs={{0,1},{2,3},{4,5},{6,7},{1,0},{3,2},{5,4},{7,6},{8,9},{10,11},{12,... | collective-permute-start | bytes 786440 | tf_op jit(solution)/shard_map/ppermute | solution.py:437
  69.1 1.8 %with_carry.4 = (bf16[256,8192]{1,0:T(8,128)(2,1)}, f32[8,128]{1,0:T(8,128)S(1)}) custom-call(f32[8,1024]{1,0:T(8,128)S(1)} %select_select_fusion.refs_11_.refs_0_, bf16[256,256]{1,0:T(8,128)(2,1)S(1)} %get-tuple-element.187.refs_2_.refs_1_, f32[256,2048]{1,0:T(8,128)S(1)} %get-tuple-element.212.refs_2_, bf16[128,1024]{1,0:T(8,128)(2,1)S(1)} %get-tuple-element.219.refs_3_, ...), custom_call_target="tpu_custom_call" | custom-call | flops 600000000 | tf_op jit(solution)/shard_map/with_carry/pallas_call | solution.py:413
  72.2 1.6 %collective-permute-start.24 = (bf16[128,1024]{1,0:T(8,128)(2,1)S(1)}, bf16[128,1024]{1,0:T(8,128)(2,1)S(1)}, u32[]{:S(2)}, u32[]{:S(2)}) collective-permute-start(bf16[128,1024]{1,0:T(8,128)(2,1)S(1)} %get-tuple-element.251), channel_id=1, source_target_pairs={{0,1},{2,3},{4,5},{6,7},{1,0},{3,2},{5,4},{7,6},{8,9},{10,11},{12,... | collective-permute-start | bytes 786440 | tf_op jit(solution)/shard_map/ppermute | solution.py:437
  73.8 2.3 %collective-permute-done.21.refs_4_ = bf16[128,1024]{1,0:T(8,128)(2,1)S(1)} collective-permute-done((bf16[128,1024]{1,0:T(8,128)(2,1)S(1)}, bf16[128,1024]{1,0:T(8,128)(2,1)S(1)}, u32[]{:S(2)}, u32[]{:S(2)}) %collective-permute-start.21) | collective-permute-done | bytes 262176 | tf_op jit(solution)/shard_map/ppermute | solution.py:437
  76.1 1.8 %with_carry.5 = (bf16[256,8192]{1,0:T(8,128)(2,1)}, f32[8,128]{1,0:T(8,128)S(1)}) custom-call(f32[8,1024]{1,0:T(8,128)S(1)} %select_select_fusion.refs_11_.refs_0_, bf16[256,256]{1,0:T(8,128)(2,1)S(1)} %get-tuple-element.184.refs_2_.refs_1_, f32[256,2048]{1,0:T(8,128)S(1)} %get-tuple-element.237.refs_2_, ...), custom_call_target="tpu_custom_call", output_to_operand_aliasing={{0}: (7, {})} | custom-call | flops 600000000 | tf_op jit(solution)/shard_map/with_carry/pallas_call | solution.py:413
  78.3 1.6 %collective-permute-start.23 = (bf16[128,1024]{1,0:T(8,128)(2,1)S(1)}, bf16[128,1024]{1,0:T(8,128)(2,1)S(1)}, u32[]{:S(2)}, u32[]{:S(2)}) collective-permute-start(bf16[128,1024]{1,0:T(8,128)(2,1)S(1)} %get-tuple-element.248), channel_id=1, source_target_pairs={{0,1},{2,3},{4,5},{6,7},{1,0},{3,2},{5,4},{7,6},{8,9},{10,11},{12,... | collective-permute-start | bytes 786440 | tf_op jit(solution)/shard_map/ppermute | solution.py:437
  79.9 1.9 %collective-permute-done.24.refs_4_ = bf16[128,1024]{1,0:T(8,128)(2,1)S(1)} collective-permute-done((bf16[128,1024]{1,0:T(8,128)(2,1)S(1)}, bf16[128,1024]{1,0:T(8,128)(2,1)S(1)}, u32[]{:S(2)}, u32[]{:S(2)}) %collective-permute-start.24) | collective-permute-done | bytes 262176 | tf_op jit(solution)/shard_map/ppermute | solution.py:437
  81.7 1.8 %with_carry.6 = (bf16[256,8192]{1,0:T(8,128)(2,1)}, f32[8,128]{1,0:T(8,128)S(1)}) custom-call(f32[8,1024]{1,0:T(8,128)S(1)} %select_select_fusion.refs_11_.refs_0_, bf16[256,256]{1,0:T(8,128)(2,1)S(1)} %get-tuple-element.228.refs_2_.refs_1_, f32[256,2048]{1,0:T(8,128)S(1)} %get-tuple-element.249.refs_2_, ...), custom_call_target="tpu_custom_call", output_to_operand_aliasing={{0}: (7, {})} | custom-call | flops 600000000 | tf_op jit(solution)/shard_map/with_carry/pallas_call | solution.py:413
  83.6 3.5 %collective-permute-done.23.refs_4_ = bf16[128,1024]{1,0:T(8,128)(2,1)S(1)} collective-permute-done((bf16[128,1024]{1,0:T(8,128)(2,1)S(1)}, bf16[128,1024]{1,0:T(8,128)(2,1)S(1)}, u32[]{:S(2)}, u32[]{:S(2)}) %collective-permute-start.23) | collective-permute-done | bytes 262176 | tf_op jit(solution)/shard_map/ppermute | solution.py:437
  87.0 1.8 %with_carry.7 = (bf16[256,8192]{1,0:T(8,128)(2,1)}, f32[8,128]{1,0:T(8,128)}) custom-call(f32[8,1024]{1,0:T(8,128)S(1)} %select_select_fusion.refs_11_.refs_0_, bf16[256,256]{1,0:T(8,128)(2,1)S(1)} %get-tuple-element.148.refs_2_.refs_1_, f32[256,2048]{1,0:T(8,128)S(1)} %get-tuple-element.196.refs_2_, ...), custom_call_target="tpu_custom_call", output_to_operand_aliasing={{0}: (7, {})} | custom-call | flops 600000000 | tf_op jit(solution)/shard_map/with_carry/pallas_call | solution.py:413
  (71 shorter events, 15.7 us)
Async XLA Ops:
  0.0 6.4 %copy-start.4 = (bf16[256,128]{1,0:T(8,128)(2,1)S(1)}, bf16[256,128]{1,0:T(8,128)(2,1)}, u32[]{:S(2)}) copy-start(bf16[256,128]{1,0:T(8,128)(2,1)} %dt_ref) | copy-start | bytes 196612
  0.0 6.4 %copy-start.6 = (f32[128]{0:T(128)S(1)}, f32[128]{0:T(128)}, u32[]{:S(2)}) copy-start(f32[128]{0:T(128)} %param.12) | copy-start | bytes 1540
  0.0 6.4 %copy-start.5 = (f32[128]{0:T(128)S(1)}, f32[128]{0:T(128)}, u32[]{:S(2)}) copy-start(f32[128]{0:T(128)} %param.11) | copy-start | bytes 1540
  0.1 7.5 %copy-start = (bf16[256,8192]{1,0:T(8,128)(2,1)S(1)}, bf16[256,8192]{1,0:T(8,128)(2,1)}, u32[]{:S(2)}) copy-start(bf16[256,8192]{1,0:T(8,128)(2,1)} %refs_0_.4) | copy-start | bytes 12582916
  0.1 7.5 %copy-start.1 = (bf16[256,1024]{1,0:T(8,128)(2,1)S(1)}, bf16[256,1024]{1,0:T(8,128)(2,1)}, u32[]{:S(2)}) copy-start(bf16[256,1024]{1,0:T(8,128)(2,1)} %refs_1_.9) | copy-start | bytes 1572868
  0.1 7.5 %copy-start.2 = (bf16[256,1024]{1,0:T(8,128)(2,1)S(1)}, bf16[256,1024]{1,0:T(8,128)(2,1)}, u32[]{:S(2)}) copy-start(bf16[256,1024]{1,0:T(8,128)(2,1)} %refs_2_.9) | copy-start | bytes 1572868
  0.1 7.5 %copy-start.3 = (bf16[4,10240]{1,0:T(4,128)(2,1)S(1)}, bf16[4,10240]{1,0:T(4,128)(2,1)}, u32[]{:S(2)}) copy-start(bf16[4,10240]{1,0:T(4,128)(2,1)} %refs_5_.9) | copy-start | bytes 245764
  1.3 8.8 %collective-permute-start = (bf16[3,10240]{1,0:T(4,128)(2,1)S(1)}, bf16[3,10240]{1,0:T(4,128)(2,1)S(1)}, u32[]{:S(2)}, u32[]{:S(2)}) collective-permute-start(bf16[3,10240]{1,0:T(4,128)(2,1)S(1)} %rim_rows.1), channel_id=1, source_target_pairs={{0,1},{1,2},{2,3},{3,4},{4,5},{5,6},{6,7},{7,8},{8,9},{9,10},{10,1... | collective-permute-start | bytes 184328 | tf_op jit(solution)/shard_map/ppermute | solution.py:781
  10.9 9.5 %collective-permute-start.1 = (bf16[144,1024]{1,0:T(8,128)(2,1)S(1)}, bf16[144,1024]{1,0:T(8,128)(2,1)S(1)}, u32[]{:S(2)}, u32[]{:S(2)}) collective-permute-start(bf16[144,1024]{1,0:T(8,128)(2,1)S(1)} %get-tuple-element.143), channel_id=1, source_target_pairs={{0,1},{2,3},{4,5},{6,7},{1,0},{3,2},{5,4},{7,6},{8,9},{10,11},{12,... | collective-permute-start | bytes 884744 | tf_op jit(solution)/shard_map/ppermute | solution.py:437
  14.9 11.9 %collective-permute-start.3 = (bf16[128,1024]{1,0:T(8,128)(2,1)S(1)}, bf16[128,1024]{1,0:T(8,128)(2,1)S(1)}, u32[]{:S(2)}, u32[]{:S(2)}) collective-permute-start(bf16[128,1024]{1,0:T(8,128)(2,1)S(1)} %get-tuple-element.158), channel_id=1, source_target_pairs={{0,1},{2,3},{4,5},{6,7},{1,0},{3,2},{5,4},{7,6},{8,9},{10,11},{12,... | collective-permute-start | bytes 786440 | tf_op jit(solution)/shard_map/ppermute | solution.py:437
  20.8 10.0 %collective-permute-start.5 = (bf16[144,1024]{1,0:T(8,128)(2,1)S(1)}, bf16[144,1024]{1,0:T(8,128)(2,1)S(1)}, u32[]{:S(2)}, u32[]{:S(2)}) collective-permute-start(bf16[144,1024]{1,0:T(8,128)(2,1)S(1)} %get-tuple-element.162.refs_1_), channel_id=1, source_target_pairs={{0,2},{1,3},{4,6},{5,7},{2,0},{3,1},{6,4},{7,5},{8,10},{9,11},{12,... | collective-permute-start | bytes 884744 | tf_op jit(solution)/shard_map/ppermute | solution.py:437
  22.9 9.2 %collective-permute-start.6 = (bf16[128,1024]{1,0:T(8,128)(2,1)S(1)}, bf16[128,1024]{1,0:T(8,128)(2,1)S(1)}, u32[]{:S(2)}, u32[]{:S(2)}) collective-permute-start(bf16[128,1024]{1,0:T(8,128)(2,1)S(1)} %get-tuple-element.167), channel_id=1, source_target_pairs={{0,1},{2,3},{4,5},{6,7},{1,0},{3,2},{5,4},{7,6},{8,9},{10,11},{12,... | collective-permute-start | bytes 786440 | tf_op jit(solution)/shard_map/ppermute | solution.py:437
  27.0 9.4 %collective-permute-start.4 = (bf16[128,1024]{1,0:T(8,128)(2,1)S(1)}, bf16[128,1024]{1,0:T(8,128)(2,1)S(1)}, u32[]{:S(2)}, u32[]{:S(2)}) collective-permute-start(bf16[128,1024]{1,0:T(8,128)(2,1)S(1)} %get-tuple-element.161.refs_1_), channel_id=1, source_target_pairs={{0,2},{1,3},{4,6},{5,7},{2,0},{3,1},{6,4},{7,5},{8,10},{9,11},{12,... | collective-permute-start | bytes 786440 | tf_op jit(solution)/shard_map/ppermute | solution.py:437
  27.4 10.3 %collective-permute-start.2 = (bf16[128,1024]{1,0:T(8,128)(2,1)S(1)}, bf16[128,1024]{1,0:T(8,128)(2,1)S(1)}, u32[]{:S(2)}, u32[]{:S(2)}) collective-permute-start(bf16[128,1024]{1,0:T(8,128)(2,1)S(1)} %get-tuple-element.155), channel_id=1, source_target_pairs={{0,1},{2,3},{4,5},{6,7},{1,0},{3,2},{5,4},{7,6},{8,9},{10,11},{12,... | collective-permute-start | bytes 786440 | tf_op jit(solution)/shard_map/ppermute | solution.py:437
  31.0 9.0 %collective-permute-start.9 = (bf16[144,1024]{1,0:T(8,128)(2,1)S(1)}, bf16[144,1024]{1,0:T(8,128)(2,1)S(1)}, u32[]{:S(2)}, u32[]{:S(2)}) collective-permute-start(bf16[144,1024]{1,0:T(8,128)(2,1)S(1)} %get-tuple-element.175.refs_2_), channel_id=1, source_target_pairs={{2,4},{3,5},{4,2},{5,3},{10,12},{11,13},{12,10},{13,11},{18,20},{1... | collective-permute-start | bytes 884744 | tf_op jit(solution)/shard_map/ppermute | solution.py:437
  32.2 10.4 %collective-permute-start.10 = (bf16[128,1024]{1,0:T(8,128)(2,1)S(1)}, bf16[128,1024]{1,0:T(8,128)(2,1)S(1)}, u32[]{:S(2)}, u32[]{:S(2)}) collective-permute-start(bf16[128,1024]{1,0:T(8,128)(2,1)S(1)} %get-tuple-element.188.refs_1_), channel_id=1, source_target_pairs={{0,2},{1,3},{4,6},{5,7},{2,0},{3,1},{6,4},{7,5},{8,10},{9,11},{12,... | collective-permute-start | bytes 786440 | tf_op jit(solution)/shard_map/ppermute | solution.py:437
  36.5 11.5 %collective-permute-start.8 = (bf16[128,1024]{1,0:T(8,128)(2,1)S(1)}, bf16[128,1024]{1,0:T(8,128)(2,1)S(1)}, u32[]{:S(2)}, u32[]{:S(2)}) collective-permute-start(bf16[128,1024]{1,0:T(8,128)(2,1)S(1)} %get-tuple-element.174.refs_2_), channel_id=1, source_target_pairs={{2,4},{3,5},{4,2},{5,3},{10,12},{11,13},{12,10},{13,11},{18,20},{1... | collective-permute-start | bytes 786440 | tf_op jit(solution)/shard_map/ppermute | solution.py:437
  37.8 10.3 %collective-permute-start.7 = (bf16[128,1024]{1,0:T(8,128)(2,1)S(1)}, bf16[128,1024]{1,0:T(8,128)(2,1)S(1)}, u32[]{:S(2)}, u32[]{:S(2)}) collective-permute-start(bf16[128,1024]{1,0:T(8,128)(2,1)S(1)} %get-tuple-element.172.refs_1_), channel_id=1, source_target_pairs={{0,2},{1,3},{4,6},{5,7},{2,0},{3,1},{6,4},{7,5},{8,10},{9,11},{12,... | collective-permute-start | bytes 786440 | tf_op jit(solution)/shard_map/ppermute | solution.py:437
  40.4 16.2 %collective-permute-start.13 = (bf16[144,1024]{1,0:T(8,128)(2,1)S(1)}, bf16[144,1024]{1,0:T(8,128)(2,1)S(1)}, u32[]{:S(2)}, u32[]{:S(2)}) collective-permute-start(bf16[144,1024]{1,0:T(8,128)(2,1)S(1)} %get-tuple-element.205), channel_id=1, source_target_pairs={{0,2},{1,3},{4,6},{5,7},{2,0},{3,1},{6,4},{7,5},{8,10},{9,11},{12,... | collective-permute-start | bytes 884744 | tf_op jit(solution)/shard_map/ppermute | solution.py:437
  42.8 14.2 %collective-permute-start.12 = (bf16[128,1024]{1,0:T(8,128)(2,1)S(1)}, bf16[128,1024]{1,0:T(8,128)(2,1)S(1)}, u32[]{:S(2)}, u32[]{:S(2)}) collective-permute-start(bf16[128,1024]{1,0:T(8,128)(2,1)S(1)} %get-tuple-element.201.refs_2_), channel_id=1, source_target_pairs={{2,4},{3,5},{4,2},{5,3},{10,12},{11,13},{12,10},{13,11},{18,20},{1... | collective-permute-start | bytes 786440 | tf_op jit(solution)/shard_map/ppermute | solution.py:437
  48.3 9.0 %collective-permute-start.11 = (bf16[128,1024]{1,0:T(8,128)(2,1)S(1)}, bf16[128,1024]{1,0:T(8,128)(2,1)S(1)}, u32[]{:S(2)}, u32[]{:S(2)}) collective-permute-start(bf16[128,1024]{1,0:T(8,128)(2,1)S(1)} %get-tuple-element.197.refs_2_), channel_id=1, source_target_pairs={{2,4},{3,5},{4,2},{5,3},{10,12},{11,13},{12,10},{13,11},{18,20},{1... | collective-permute-start | bytes 786440 | tf_op jit(solution)/shard_map/ppermute | solution.py:437
  49.2 10.3 %collective-permute-start.16 = (bf16[128,1024]{1,0:T(8,128)(2,1)S(1)}, bf16[128,1024]{1,0:T(8,128)(2,1)S(1)}, u32[]{:S(2)}, u32[]{:S(2)}) collective-permute-start(bf16[128,1024]{1,0:T(8,128)(2,1)S(1)} %get-tuple-element.216), channel_id=1, source_target_pairs={{0,2},{1,3},{4,6},{5,7},{2,0},{3,1},{6,4},{7,5},{8,10},{9,11},{12,... | collective-permute-start | bytes 786440 | tf_op jit(solution)/shard_map/ppermute | solution.py:437
  56.9 2.8 %collective-permute-start.15 = (bf16[128,1024]{1,0:T(8,128)(2,1)S(1)}, bf16[128,1024]{1,0:T(8,128)(2,1)S(1)}, u32[]{:S(2)}, u32[]{:S(2)}) collective-permute-start(bf16[128,1024]{1,0:T(8,128)(2,1)S(1)} %get-tuple-element.213), channel_id=1, source_target_pairs={{0,8},{8,0},{1,9},{9,1},{2,10},{10,2},{3,11},{11,3},{4,12},{12,4},... | collective-permute-start | bytes 786440 | tf_op jit(solution)/shard_map/ppermute | solution.py:437
  57.2 9.2 %collective-permute-start.19 = (bf16[128,1024]{1,0:T(8,128)(2,1)S(1)}, bf16[128,1024]{1,0:T(8,128)(2,1)S(1)}, u32[]{:S(2)}, u32[]{:S(2)}) collective-permute-start(bf16[128,1024]{1,0:T(8,128)(2,1)S(1)} %get-tuple-element.225), channel_id=1, source_target_pairs={{0,2},{1,3},{4,6},{5,7},{2,0},{3,1},{6,4},{7,5},{8,10},{9,11},{12,... | collective-permute-start | bytes 786440 | tf_op jit(solution)/shard_map/ppermute | solution.py:437
  59.7 7.0 %collective-permute-start.18 = (bf16[128,1024]{1,0:T(8,128)(2,1)S(1)}, bf16[128,1024]{1,0:T(8,128)(2,1)S(1)}, u32[]{:S(2)}, u32[]{:S(2)}) collective-permute-start(bf16[128,1024]{1,0:T(8,128)(2,1)S(1)} %get-tuple-element.222), channel_id=1, source_target_pairs={{0,8},{8,0},{1,9},{9,1},{2,10},{10,2},{3,11},{11,3},{4,12},{12,4},... | collective-permute-start | bytes 786440 | tf_op jit(solution)/shard_map/ppermute | solution.py:437
  60.4 8.8 %collective-permute-start.17 = (bf16[128,1024]{1,0:T(8,128)(2,1)S(1)}, bf16[128,1024]{1,0:T(8,128)(2,1)S(1)}, u32[]{:S(2)}, u32[]{:S(2)}) collective-permute-start(bf16[128,1024]{1,0:T(8,128)(2,1)S(1)} %get-tuple-element.220), channel_id=1, source_target_pairs={{0,1},{2,3},{4,5},{6,7},{1,0},{3,2},{5,4},{7,6},{8,9},{10,11},{12,... | collective-permute-start | bytes 786440 | tf_op jit(solution)/shard_map/ppermute | solution.py:437
  61.3 10.3 %collective-permute-start.14 = (bf16[128,1024]{1,0:T(8,128)(2,1)S(1)}, bf16[128,1024]{1,0:T(8,128)(2,1)S(1)}, u32[]{:S(2)}, u32[]{:S(2)}) collective-permute-start(bf16[128,1024]{1,0:T(8,128)(2,1)S(1)} %get-tuple-element.211), channel_id=1, source_target_pairs={{0,2},{1,3},{4,6},{5,7},{2,0},{3,1},{6,4},{7,5},{8,10},{9,11},{12,... | collective-permute-start | bytes 786440 | tf_op jit(solution)/shard_map/ppermute | solution.py:437
  66.6 5.3 %collective-permute-start.22 = (bf16[128,1024]{1,0:T(8,128)(2,1)S(1)}, bf16[128,1024]{1,0:T(8,128)(2,1)S(1)}, u32[]{:S(2)}, u32[]{:S(2)}) collective-permute-start(bf16[128,1024]{1,0:T(8,128)(2,1)S(1)} %get-tuple-element.241), channel_id=1, source_target_pairs={{0,8},{8,0},{1,9},{9,1},{2,10},{10,2},{3,11},{11,3},{4,12},{12,4},... | collective-permute-start | bytes 786440 | tf_op jit(solution)/shard_map/ppermute | solution.py:437
  67.0 9.1 %collective-permute-start.21 = (bf16[128,1024]{1,0:T(8,128)(2,1)S(1)}, bf16[128,1024]{1,0:T(8,128)(2,1)S(1)}, u32[]{:S(2)}, u32[]{:S(2)}) collective-permute-start(bf16[128,1024]{1,0:T(8,128)(2,1)S(1)} %get-tuple-element.239), channel_id=1, source_target_pairs={{0,1},{2,3},{4,5},{6,7},{1,0},{3,2},{5,4},{7,6},{8,9},{10,11},{12,... | collective-permute-start | bytes 786440 | tf_op jit(solution)/shard_map/ppermute | solution.py:437
  71.8 6.1 %collective-permute-start.20 = (bf16[128,1024]{1,0:T(8,128)(2,1)S(1)}, bf16[128,1024]{1,0:T(8,128)(2,1)S(1)}, u32[]{:S(2)}, u32[]{:S(2)}) collective-permute-start(bf16[128,1024]{1,0:T(8,128)(2,1)S(1)} %get-tuple-element.234), channel_id=1, source_target_pairs={{0,8},{8,0},{1,9},{9,1},{2,10},{10,2},{3,11},{11,3},{4,12},{12,4},... | collective-permute-start | bytes 786440 | tf_op jit(solution)/shard_map/ppermute | solution.py:437
  72.2 9.5 %collective-permute-start.24 = (bf16[128,1024]{1,0:T(8,128)(2,1)S(1)}, bf16[128,1024]{1,0:T(8,128)(2,1)S(1)}, u32[]{:S(2)}, u32[]{:S(2)}) collective-permute-start(bf16[128,1024]{1,0:T(8,128)(2,1)S(1)} %get-tuple-element.251), channel_id=1, source_target_pairs={{0,1},{2,3},{4,5},{6,7},{1,0},{3,2},{5,4},{7,6},{8,9},{10,11},{12,... | collective-permute-start | bytes 786440 | tf_op jit(solution)/shard_map/ppermute | solution.py:437
  78.3 8.7 %collective-permute-start.23 = (bf16[128,1024]{1,0:T(8,128)(2,1)S(1)}, bf16[128,1024]{1,0:T(8,128)(2,1)S(1)}, u32[]{:S(2)}, u32[]{:S(2)}) collective-permute-start(bf16[128,1024]{1,0:T(8,128)(2,1)S(1)} %get-tuple-element.248), channel_id=1, source_target_pairs={{0,1},{2,3},{4,5},{6,7},{1,0},{3,2},{5,4},{7,6},{8,9},{10,11},{12,... | collective-permute-start | bytes 786440 | tf_op jit(solution)/shard_map/ppermute | solution.py:437

commit v3 on v2

--- a/solution.py
+++ b/solution.py
@@ -464,12 +464,12 @@
 ORDER = (
     [("early", 0, 1.0), ("state", 0, 1.0), ("state", 1, 1.0), ("state", 2, 1.0), ("chip", 0, 1.0)]
     + [("state", 3, 1.0), ("chip", 1, 1.0), ("chips", 0, 1.0), ("chip", 2, 1.0)]
-    + [("chips", 1, 1.0), ("chip", 3, 1.0), ("link", 0, 1.0), ("chips", 2, 1.0)]
-    + [("inside", 0, 1.0), ("inside", 1, 1.0), ("link", 1, 1.0), ("chips", 3, 1.0)]
-    + [("inside", 3, 1.0), ("total", 0, 1.0), ("link", 2, 1.0), ("link", 3, 1.0)]
-    + [("total", 1, 1.0), ("leave", 0, 1.0), ("inside", 2, 1.0), ("total", 2, 1.0)]
-    + [("leave", 1, 1.0), ("out", 0, 1.0), ("total", 3, 1.0), ("leave", 2, 1.0)]
-    + [("out", 1, 1.0), ("leave", 3, 1.0), ("out", 2, 1.0), ("out", 3, 1.0)]
+    + [("chips", 1, 1.0), ("chip", 3, 1.0), ("inside", 0, 1.0), ("link", 0, 1.0)]
+    + [("chips", 2, 1.0), ("link", 1, 1.0), ("chips", 3, 1.0), ("inside", 1, 1.0)]
+    + [("total", 0, 1.0), ("link", 2, 1.0), ("link", 3, 1.0), ("total", 1, 1.0)]
+    + [("leave", 0, 1.0), ("total", 2, 1.0), ("leave", 1, 1.0), ("out", 0, 1.0)]
+    + [("total", 3, 1.0), ("leave", 2, 1.0), ("out", 1, 1.0), ("leave", 3, 1.0)]
+    + [("inside", 2, 1.0), ("inside", 3, 1.0), ("out", 2, 1.0), ("out", 3, 1.0)]
 )
 
 

time: 89 us -> 88.1 us (0.990)
  starting transfers between devices: 37.3 us -> 28.6 us
  waiting for transfers between devices: 17.1 us -> 24.9 us
    ppermute x24, starting transfers between devices: 32.3 us -> 23.5 us  [swap(): return lax.ppermute(value, axis, pairs + [(b, a) for a, b in pairs])]
    ppermute x24, waiting for transfers between devices: 17.1 us -> 24.9 us  [swap(): return lax.ppermute(value, axis, pairs + [(b, a) for a, b in pairs])]
  transfers between devices with their start and end apart: 25 -> 25, of which waited for: 12 -> 11; matrix products, arithmetic and copies ran while one was open for 0% -> 0% of each run, Pallas kernels for 34% -> 34%
where the time goes in v3:
time: 88.1 us; the launch traced here: 87.9 us
  Pallas kernels  33.9 us (38%)
  starting transfers between devices  28.6 us (32%)
  waiting for transfers between devices  24.9 us (28%)
    ppermute x24, waiting for transfers between devices, swap(): return lax.ppermute(value, axis, pairs + [(b, a) for a, b in pairs])  24.9 us
    ppermute x24, starting transfers between devices, swap(): return lax.ppermute(value, axis, pairs + [(b, a) for a, b in pairs])  23.5 us
    pallas_call x4, Pallas kernels, inside_block(): pl.pallas_call(lambda *refs: inside_body(*refs[:6], *refs[6 + len(after):...  8.9 us
    pallas_call x3, Pallas kernels, end_states(): pl.pallas_call(body, grid=(count,), in_specs=conv_specs(first, SPAN) + ri...  7.32 us
    pallas_call x4, Pallas kernels, with_carry(): pl.pallas_call(carried_body, grid=(count,), in_specs=[whole(side), pl.Blo...  7.27 us
    ppermute x1, starting transfers between devices, shards(): lax.ppermute(rim_rows(x_stream, b_stream, c_stream), ('outer', 'inner'),...  5.02 us
    pallas_call x20, Pallas kernels, merge(): pl.pallas_call(run, grid=(1,), in_specs=[whole(a) for a in given] + [corn...  4.74 us
    pallas_call x1, Pallas kernels, early_states(): pl.pallas_call(body, grid=(count,), in_specs=conv_specs(first, SPAN) + [c...  2.4 us
  transfers between devices with their start and end apart: 25, of which 11 were waited for; matrix products, arithmetic and copies ran while one was open for 0% of the time, Pallas kernels for 34%

profile of v3, /device:TPU:0, one launch (start us, length us, event | category | flops | bytes accessed | tf_op | source)
XLA Modules:
  0.0 87.9 jit_solution(9846024546226196850)
XLA Ops:
  0.2 1.2 %rim_rows.1 = bf16[3,10240]{1,0:T(4,128)(2,1)S(1)} custom-call(bf16[256,8192]{1,0:T(8,128)(2,1)} %refs_0_.4, bf16[256,1024]{1,0:T(8,128)(2,1)} %refs_1_.9, bf16[256,1024]{1,0:T(8,128)(2,1)} %refs_2_.9), custom_call_target="tpu_custom_call" | custom-call | flops 600000000 | tf_op jit(solution)/shard_map/rim_rows/pallas_call | solution.py:59
  1.3 5.0 %collective-permute-start = (bf16[3,10240]{1,0:T(4,128)(2,1)S(1)}, bf16[3,10240]{1,0:T(4,128)(2,1)S(1)}, u32[]{:S(2)}, u32[]{:S(2)}) collective-permute-start(bf16[3,10240]{1,0:T(4,128)(2,1)S(1)} %rim_rows.1), channel_id=1, source_target_pairs={{0,1},{1,2},{2,3},{3,4},{4,5},{5,6},{6,7},{7,8},{8,9},{9,10},{10,1... | collective-permute-start | bytes 184328 | tf_op jit(solution)/shard_map/ppermute | solution.py:781
  6.4 1.3 %time_steps.1 = (f32[8,256,16]{2,1,0:T(8,128)S(1)}, f32[128,256]{1,0:T(8,128)S(1)}, bf16[8,256,32]{2,1,0:T(8,128)(2,1)S(1)}, bf16[8,256,32]{2,1,0:T(8,128)(2,1)S...) custom-call(bf16[256,128]{1,0:T(8,128)(2,1)S(1)} %copy-done.4, ...), custom_call_target="tpu_custom_call" | custom-call | flops 1200000000 | tf_op jit(solution)/shard_map/time_steps/pallas_call | solution.py:145
  7.7 2.4 %early_states.1 = (bf16[256,2048]{1,0:T(8,128)(2,1)S(1)}, bf16[256,256]{1,0:T(8,128)(2,1)S(1)}, bf16[256,256]{1,0:T(8,128)(2,1)S(1)}, f32[2,128,1024]{2,1,0:T(8,128)S(1)}, f32[8,128]{1,0:T(8,128)S(1)}) custom-call(bf16[256,8192]{1,0:T(8,128)(2,1)S(1)} %copy-done, bf16[256,1024]{1,0:T(8,128)(2,1)S(1)} %copy-done.1, bf16[256,1024]{1,0:T(8,128)(2,1)S(1)} %copy-done.2, ...), custom_call_target="tpu_custom_call" | custom-call | flops 600000000 | tf_op jit(solution)/shard_map/early_states/pallas_call | solution.py:260
  10.9 1.6 %collective-permute-start.1 = (bf16[144,1024]{1,0:T(8,128)(2,1)S(1)}, bf16[144,1024]{1,0:T(8,128)(2,1)S(1)}, u32[]{:S(2)}, u32[]{:S(2)}) collective-permute-start(bf16[144,1024]{1,0:T(8,128)(2,1)S(1)} %get-tuple-element.143), channel_id=1, source_target_pairs={{0,1},{2,3},{4,5},{6,7},{1,0},{3,2},{5,4},{7,6},{8,9},{10,11},{12,... | collective-permute-start | bytes 884744 | tf_op jit(solution)/shard_map/ppermute | solution.py:437
  12.5 2.4 %end_states.3 = (bf16[256,2048]{1,0:T(8,128)(2,1)S(1)}, bf16[256,256]{1,0:T(8,128)(2,1)S(1)}, bf16[256,256]{1,0:T(8,128)(2,1)S(1)}, bf16[128,1024]{1,0:T(8,128)(...) custom-call(bf16[256,8192]{1,0:T(8,128)(2,1)S(1)} %copy-done, bf16[256,1024]{1,0:T(8,128)(2,1)S(1)} %copy-done.1, ...), custom_call_target="tpu_custom_call" | custom-call | flops 600000000 | tf_op jit(solution)/shard_map/end_states/pallas_call | solution.py:314
  15.5 2.4 %end_states.4 = (bf16[256,2048]{1,0:T(8,128)(2,1)S(1)}, bf16[256,256]{1,0:T(8,128)(2,1)S(1)}, bf16[256,256]{1,0:T(8,128)(2,1)S(1)}, bf16[128,1024]{1,0:T(8,128)(...) custom-call(bf16[256,8192]{1,0:T(8,128)(2,1)S(1)} %copy-done, bf16[256,1024]{1,0:T(8,128)(2,1)S(1)} %copy-done.1, ...), custom_call_target="tpu_custom_call" | custom-call | flops 600000000 | tf_op jit(solution)/shard_map/end_states/pallas_call | solution.py:314
  18.0 2.5 %collective-permute-done.1.refs_2_ = bf16[144,1024]{1,0:T(8,128)(2,1)S(1)} collective-permute-done((bf16[144,1024]{1,0:T(8,128)(2,1)S(1)}, bf16[144,1024]{1,0:T(8,128)(2,1)S(1)}, u32[]{:S(2)}, u32[]{:S(2)}) %collective-permute-start.1) | collective-permute-done | bytes 294944 | tf_op jit(solution)/shard_map/ppermute | solution.py:437
  20.8 2.1 %collective-permute-start.5 = (bf16[144,1024]{1,0:T(8,128)(2,1)S(1)}, bf16[144,1024]{1,0:T(8,128)(2,1)S(1)}, u32[]{:S(2)}, u32[]{:S(2)}) collective-permute-start(bf16[144,1024]{1,0:T(8,128)(2,1)S(1)} %get-tuple-element.165.refs_1_), channel_id=1, source_target_pairs={{0,2},{1,3},{4,6},{5,7},{2,0},{3,1},{6,4},{7,5},{8,10},{9,11},{12,... | collective-permute-start | bytes 884744 | tf_op jit(solution)/shard_map/ppermute | solution.py:437
  22.9 1.5 %collective-permute-start.6 = (bf16[128,1024]{1,0:T(8,128)(2,1)S(1)}, bf16[128,1024]{1,0:T(8,128)(2,1)S(1)}, u32[]{:S(2)}, u32[]{:S(2)}) collective-permute-start(bf16[128,1024]{1,0:T(8,128)(2,1)S(1)} %get-tuple-element.170), channel_id=1, source_target_pairs={{0,1},{2,3},{4,5},{6,7},{1,0},{3,2},{5,4},{7,6},{8,9},{10,11},{12,... | collective-permute-start | bytes 786440 | tf_op jit(solution)/shard_map/ppermute | solution.py:437
  24.4 2.4 %end_states.5 = (bf16[256,2048]{1,0:T(8,128)(2,1)S(1)}, bf16[256,256]{1,0:T(8,128)(2,1)S(1)}, bf16[256,256]{1,0:T(8,128)(2,1)S(1)}, bf16[128,1024]{1,0:T(8,128)(...) custom-call(bf16[256,8192]{1,0:T(8,128)(2,1)S(1)} %copy-done, bf16[256,1024]{1,0:T(8,128)(2,1)S(1)} %copy-done.1, ...), custom_call_target="tpu_custom_call" | custom-call | flops 600000000 | tf_op jit(solution)/shard_map/end_states/pallas_call | solution.py:314
  27.4 2.4 %collective-permute-start.2 = (bf16[128,1024]{1,0:T(8,128)(2,1)S(1)}, bf16[128,1024]{1,0:T(8,128)(2,1)S(1)}, u32[]{:S(2)}, u32[]{:S(2)}) collective-permute-start(bf16[128,1024]{1,0:T(8,128)(2,1)S(1)} %get-tuple-element.158), channel_id=1, source_target_pairs={{0,1},{2,3},{4,5},{6,7},{1,0},{3,2},{5,4},{7,6},{8,9},{10,11},{12,... | collective-permute-start | bytes 786440 | tf_op jit(solution)/shard_map/ppermute | solution.py:437
  29.8 0.9 %collective-permute-done.5.refs_2_.refs_3_ = bf16[144,1024]{1,0:T(8,128)(2,1)S(1)} collective-permute-done((bf16[144,1024]{1,0:T(8,128)(2,1)S(1)}, bf16[144,1024]{1,0:T(8,128)(2,1)S(1)}, u32[]{:S(2)}, u32[]{:S(2)}) %collective-permute-start.5) | collective-permute-done | bytes 294944 | tf_op jit(solution)/shard_map/ppermute | solution.py:437
  32.2 2.8 %collective-permute-start.10 = (bf16[128,1024]{1,0:T(8,128)(2,1)S(1)}, bf16[128,1024]{1,0:T(8,128)(2,1)S(1)}, u32[]{:S(2)}, u32[]{:S(2)}) collective-permute-start(bf16[128,1024]{1,0:T(8,128)(2,1)S(1)} %get-tuple-element.189.refs_1_), channel_id=1, source_target_pairs={{0,2},{1,3},{4,6},{5,7},{2,0},{3,1},{6,4},{7,5},{8,10},{9,11},{12,... | collective-permute-start | bytes 786440 | tf_op jit(solution)/shard_map/ppermute | solution.py:437
  35.0 1.3 %collective-permute-done.4.refs_2_.refs_3_ = bf16[128,1024]{1,0:T(8,128)(2,1)S(1)} collective-permute-done((bf16[128,1024]{1,0:T(8,128)(2,1)S(1)}, bf16[128,1024]{1,0:T(8,128)(2,1)S(1)}, u32[]{:S(2)}, u32[]{:S(2)}) %collective-permute-start.4) | collective-permute-done | bytes 262176 | tf_op jit(solution)/shard_map/ppermute | solution.py:437
  37.8 2.2 %collective-permute-start.7 = (bf16[128,1024]{1,0:T(8,128)(2,1)S(1)}, bf16[128,1024]{1,0:T(8,128)(2,1)S(1)}, u32[]{:S(2)}, u32[]{:S(2)}) collective-permute-start(bf16[128,1024]{1,0:T(8,128)(2,1)S(1)} %get-tuple-element.175.refs_1_), channel_id=1, source_target_pairs={{0,2},{1,3},{4,6},{5,7},{2,0},{3,1},{6,4},{7,5},{8,10},{9,11},{12,... | collective-permute-start | bytes 786440 | tf_op jit(solution)/shard_map/ppermute | solution.py:437
  40.0 2.2 %inside_block.4 = (f32[256,2048]{1,0:T(8,128)S(1)}, f32[8,128]{1,0:T(8,128)S(1)}) custom-call(bf16[256,2048]{1,0:T(8,128)(2,1)S(1)} %get-tuple-element.181.refs_0_, bf16[256,256]{1,0:T(8,128)(2,1)S(1)} %get-tuple-element.182.refs_1_, bf16[256,256]{1,0:T(8,128)(2,1)S(1)} %get-tuple-element.183.refs_2_.refs_1_, f32[8,256,16]{2,1,0:T(8,128)S(1)} %get-tuple-element.151.refs_3_, ...), custom_call_target="tpu_custom_call" | custom-call | flops 600000000 | tf_op jit(solution)/shard_map/inside_block/pallas_call | solution.py:374
  43.8 4.1 %collective-permute-done.7.refs_2_.refs_3_ = bf16[128,1024]{1,0:T(8,128)(2,1)S(1)} collective-permute-done((bf16[128,1024]{1,0:T(8,128)(2,1)S(1)}, bf16[128,1024]{1,0:T(8,128)(2,1)S(1)}, u32[]{:S(2)}, u32[]{:S(2)}) %collective-permute-start.7) | collective-permute-done | bytes 262176 | tf_op jit(solution)/shard_map/ppermute | solution.py:437
  48.9 4.7 %collective-permute-start.16 = (bf16[128,1024]{1,0:T(8,128)(2,1)S(1)}, bf16[128,1024]{1,0:T(8,128)(2,1)S(1)}, u32[]{:S(2)}, u32[]{:S(2)}) collective-permute-start(bf16[128,1024]{1,0:T(8,128)(2,1)S(1)} %get-tuple-element.217), channel_id=1, source_target_pairs={{0,2},{1,3},{4,6},{5,7},{2,0},{3,1},{6,4},{7,5},{8,10},{9,11},{12,... | collective-permute-start | bytes 786440 | tf_op jit(solution)/shard_map/ppermute | solution.py:437
  53.6 2.2 %inside_block.5 = (f32[256,2048]{1,0:T(8,128)S(1)}, f32[8,128]{1,0:T(8,128)S(1)}) custom-call(bf16[256,2048]{1,0:T(8,128)(2,1)S(1)} %get-tuple-element.205.refs_0_, bf16[256,256]{1,0:T(8,128)(2,1)S(1)} %get-tuple-element.206.refs_1_, bf16[256,256]{1,0:T(8,128)(2,1)S(1)} %get-tuple-element.207.refs_2_.refs_1_, f32[8,256,16]{2,1,0:T(8,128)S(1)} %get-tuple-element.151.refs_3_, ...), custom_call_target="tpu_custom_call" | custom-call | flops 600000000 | tf_op jit(solution)/shard_map/inside_block/pallas_call | solution.py:374
  56.6 2.9 %collective-permute-done.16.refs_4_.refs_5_ = bf16[128,1024]{1,0:T(8,128)(2,1)S(1)} collective-permute-done((bf16[128,1024]{1,0:T(8,128)(2,1)S(1)}, bf16[128,1024]{1,0:T(8,128)(2,1)S(1)}, u32[]{:S(2)}, u32[]{:S(2)}) %collective-permute-start.16) | collective-permute-done | bytes 262176 | tf_op jit(solution)/shard_map/ppermute | solution.py:437
  60.4 1.0 %collective-permute-start.14 = (bf16[128,1024]{1,0:T(8,128)(2,1)S(1)}, bf16[128,1024]{1,0:T(8,128)(2,1)S(1)}, u32[]{:S(2)}, u32[]{:S(2)}) collective-permute-start(bf16[128,1024]{1,0:T(8,128)(2,1)S(1)} %get-tuple-element.212), channel_id=1, source_target_pairs={{0,2},{1,3},{4,6},{5,7},{2,0},{3,1},{6,4},{7,5},{8,10},{9,11},{12,... | collective-permute-start | bytes 786440 | tf_op jit(solution)/shard_map/ppermute | solution.py:437
  61.5 4.0 %collective-permute-done.19.refs_4_.refs_5_ = bf16[128,1024]{1,0:T(8,128)(2,1)S(1)} collective-permute-done((bf16[128,1024]{1,0:T(8,128)(2,1)S(1)}, bf16[128,1024]{1,0:T(8,128)(2,1)S(1)}, u32[]{:S(2)}, u32[]{:S(2)}) %collective-permute-start.19) | collective-permute-done | bytes 262176 | tf_op jit(solution)/shard_map/ppermute | solution.py:437
  66.2 2.9 %collective-permute-done.17.refs_4_ = bf16[128,1024]{1,0:T(8,128)(2,1)S(1)} collective-permute-done((bf16[128,1024]{1,0:T(8,128)(2,1)S(1)}, bf16[128,1024]{1,0:T(8,128)(2,1)S(1)}, u32[]{:S(2)}, u32[]{:S(2)}) %collective-permute-start.17) | collective-permute-done | bytes 262176 | tf_op jit(solution)/shard_map/ppermute | solution.py:437
  69.1 1.8 %with_carry.4 = (bf16[256,8192]{1,0:T(8,128)(2,1)}, f32[8,128]{1,0:T(8,128)S(1)}) custom-call(f32[8,1024]{1,0:T(8,128)S(1)} %select_select_fusion.refs_11_.refs_0_, bf16[256,256]{1,0:T(8,128)(2,1)S(1)} %get-tuple-element.183.refs_2_.refs_1_, f32[256,2048]{1,0:T(8,128)S(1)} %get-tuple-element.213.refs_2_, bf16[128,1024]{1,0:T(8,128)(2,1)S(1)} %get-tuple-element.220.refs_3_, ...), custom_call_target="tpu_custom_call" | custom-call | flops 600000000 | tf_op jit(solution)/shard_map/with_carry/pallas_call | solution.py:413
  71.9 3.1 %collective-permute-done.21.refs_4_ = bf16[128,1024]{1,0:T(8,128)(2,1)S(1)} collective-permute-done((bf16[128,1024]{1,0:T(8,128)(2,1)S(1)}, bf16[128,1024]{1,0:T(8,128)(2,1)S(1)}, u32[]{:S(2)}, u32[]{:S(2)}) %collective-permute-start.21) | collective-permute-done | bytes 262176 | tf_op jit(solution)/shard_map/ppermute | solution.py:437
  75.0 1.8 %with_carry.5 = (bf16[256,8192]{1,0:T(8,128)(2,1)}, f32[8,128]{1,0:T(8,128)S(1)}) custom-call(f32[8,1024]{1,0:T(8,128)S(1)} %select_select_fusion.refs_11_.refs_0_, bf16[256,256]{1,0:T(8,128)(2,1)S(1)} %get-tuple-element.207.refs_2_.refs_1_, f32[256,2048]{1,0:T(8,128)S(1)} %get-tuple-element.234.refs_2_, ...), custom_call_target="tpu_custom_call", output_to_operand_aliasing={{0}: (7, {})} | custom-call | flops 600000000 | tf_op jit(solution)/shard_map/with_carry/pallas_call | solution.py:413
  77.5 2.2 %inside_block.6 = (f32[256,2048]{1,0:T(8,128)S(1)}, f32[8,128]{1,0:T(8,128)S(1)}) custom-call(bf16[256,2048]{1,0:T(8,128)(2,1)S(1)} %get-tuple-element.154.refs_0_, bf16[256,256]{1,0:T(8,128)(2,1)S(1)} %get-tuple-element.155.refs_1_, bf16[256,256]{1,0:T(8,128)(2,1)S(1)} %get-tuple-element.156.refs_2_.refs_1_, f32[8,256,16]{2,1,0:T(8,128)S(1)} %get-tuple-element.151.refs_3_, ...), custom_call_target="tpu_custom_call" | custom-call | flops 600000000 | tf_op jit(solution)/shard_map/inside_block/pallas_call | solution.py:374
  79.8 2.2 %inside_block.7 = (f32[256,2048]{1,0:T(8,128)S(1)}, f32[8,128]{1,0:T(8,128)S(1)}) custom-call(bf16[256,2048]{1,0:T(8,128)(2,1)S(1)} %get-tuple-element.149.refs_0_, bf16[256,256]{1,0:T(8,128)(2,1)S(1)} %get-tuple-element.150.refs_1_, bf16[256,256]{1,0:T(8,128)(2,1)S(1)} %get-tuple-element.148.refs_2_.refs_1_, f32[8,256,16]{2,1,0:T(8,128)S(1)} %get-tuple-element.151.refs_3_, ...), custom_call_target="tpu_custom_call" | custom-call | flops 600000000 | tf_op jit(solution)/shard_map/inside_block/pallas_call | solution.py:374
  82.0 1.8 %with_carry.6 = (bf16[256,8192]{1,0:T(8,128)(2,1)}, f32[8,128]{1,0:T(8,128)S(1)}) custom-call(f32[8,1024]{1,0:T(8,128)S(1)} %select_select_fusion.refs_11_.refs_0_, bf16[256,256]{1,0:T(8,128)(2,1)S(1)} %get-tuple-element.156.refs_2_.refs_1_, f32[256,2048]{1,0:T(8,128)S(1)} %get-tuple-element.249.refs_2_, ...), custom_call_target="tpu_custom_call", output_to_operand_aliasing={{0}: (7, {})} | custom-call | flops 600000000 | tf_op jit(solution)/shard_map/with_carry/pallas_call | solution.py:413
  83.8 2.3 %collective-permute-done.23.refs_4_ = bf16[128,1024]{1,0:T(8,128)(2,1)S(1)} collective-permute-done((bf16[128,1024]{1,0:T(8,128)(2,1)S(1)}, bf16[128,1024]{1,0:T(8,128)(2,1)S(1)}, u32[]{:S(2)}, u32[]{:S(2)}) %collective-permute-start.23) | collective-permute-done | bytes 262176 | tf_op jit(solution)/shard_map/ppermute | solution.py:437
  86.1 1.8 %with_carry.7 = (bf16[256,8192]{1,0:T(8,128)(2,1)}, f32[8,128]{1,0:T(8,128)}) custom-call(f32[8,1024]{1,0:T(8,128)S(1)} %select_select_fusion.refs_11_.refs_0_, bf16[256,256]{1,0:T(8,128)(2,1)S(1)} %get-tuple-element.148.refs_2_.refs_1_, f32[256,2048]{1,0:T(8,128)S(1)} %get-tuple-element.246.refs_2_, ...), custom_call_target="tpu_custom_call", output_to_operand_aliasing={{0}: (7, {})} | custom-call | flops 600000000 | tf_op jit(solution)/shard_map/with_carry/pallas_call | solution.py:413
  (71 shorter events, 11.9 us)
Async XLA Ops:
  0.0 6.4 %copy-start.4 = (bf16[256,128]{1,0:T(8,128)(2,1)S(1)}, bf16[256,128]{1,0:T(8,128)(2,1)}, u32[]{:S(2)}) copy-start(bf16[256,128]{1,0:T(8,128)(2,1)} %dt_ref) | copy-start | bytes 196612
  0.0 6.4 %copy-start.6 = (f32[128]{0:T(128)S(1)}, f32[128]{0:T(128)}, u32[]{:S(2)}) copy-start(f32[128]{0:T(128)} %param.12) | copy-start | bytes 1540
  0.0 6.4 %copy-start.5 = (f32[128]{0:T(128)S(1)}, f32[128]{0:T(128)}, u32[]{:S(2)}) copy-start(f32[128]{0:T(128)} %param.11) | copy-start | bytes 1540
  0.1 7.5 %copy-start = (bf16[256,8192]{1,0:T(8,128)(2,1)S(1)}, bf16[256,8192]{1,0:T(8,128)(2,1)}, u32[]{:S(2)}) copy-start(bf16[256,8192]{1,0:T(8,128)(2,1)} %refs_0_.4) | copy-start | bytes 12582916
  0.1 7.5 %copy-start.1 = (bf16[256,1024]{1,0:T(8,128)(2,1)S(1)}, bf16[256,1024]{1,0:T(8,128)(2,1)}, u32[]{:S(2)}) copy-start(bf16[256,1024]{1,0:T(8,128)(2,1)} %refs_1_.9) | copy-start | bytes 1572868
  0.1 7.5 %copy-start.2 = (bf16[256,1024]{1,0:T(8,128)(2,1)S(1)}, bf16[256,1024]{1,0:T(8,128)(2,1)}, u32[]{:S(2)}) copy-start(bf16[256,1024]{1,0:T(8,128)(2,1)} %refs_2_.9) | copy-start | bytes 1572868
  0.1 7.5 %copy-start.3 = (bf16[4,10240]{1,0:T(4,128)(2,1)S(1)}, bf16[4,10240]{1,0:T(4,128)(2,1)}, u32[]{:S(2)}) copy-start(bf16[4,10240]{1,0:T(4,128)(2,1)} %refs_5_.9) | copy-start | bytes 245764
  1.3 8.8 %collective-permute-start = (bf16[3,10240]{1,0:T(4,128)(2,1)S(1)}, bf16[3,10240]{1,0:T(4,128)(2,1)S(1)}, u32[]{:S(2)}, u32[]{:S(2)}) collective-permute-start(bf16[3,10240]{1,0:T(4,128)(2,1)S(1)} %rim_rows.1), channel_id=1, source_target_pairs={{0,1},{1,2},{2,3},{3,4},{4,5},{5,6},{6,7},{7,8},{8,9},{9,10},{10,1... | collective-permute-start | bytes 184328 | tf_op jit(solution)/shard_map/ppermute | solution.py:781
  10.9 9.5 %collective-permute-start.1 = (bf16[144,1024]{1,0:T(8,128)(2,1)S(1)}, bf16[144,1024]{1,0:T(8,128)(2,1)S(1)}, u32[]{:S(2)}, u32[]{:S(2)}) collective-permute-start(bf16[144,1024]{1,0:T(8,128)(2,1)S(1)} %get-tuple-element.143), channel_id=1, source_target_pairs={{0,1},{2,3},{4,5},{6,7},{1,0},{3,2},{5,4},{7,6},{8,9},{10,11},{12,... | collective-permute-start | bytes 884744 | tf_op jit(solution)/shard_map/ppermute | solution.py:437
  14.9 11.9 %collective-permute-start.3 = (bf16[128,1024]{1,0:T(8,128)(2,1)S(1)}, bf16[128,1024]{1,0:T(8,128)(2,1)S(1)}, u32[]{:S(2)}, u32[]{:S(2)}) collective-permute-start(bf16[128,1024]{1,0:T(8,128)(2,1)S(1)} %get-tuple-element.161), channel_id=1, source_target_pairs={{0,1},{2,3},{4,5},{6,7},{1,0},{3,2},{5,4},{7,6},{8,9},{10,11},{12,... | collective-permute-start | bytes 786440 | tf_op jit(solution)/shard_map/ppermute | solution.py:437
  20.8 10.0 %collective-permute-start.5 = (bf16[144,1024]{1,0:T(8,128)(2,1)S(1)}, bf16[144,1024]{1,0:T(8,128)(2,1)S(1)}, u32[]{:S(2)}, u32[]{:S(2)}) collective-permute-start(bf16[144,1024]{1,0:T(8,128)(2,1)S(1)} %get-tuple-element.165.refs_1_), channel_id=1, source_target_pairs={{0,2},{1,3},{4,6},{5,7},{2,0},{3,1},{6,4},{7,5},{8,10},{9,11},{12,... | collective-permute-start | bytes 884744 | tf_op jit(solution)/shard_map/ppermute | solution.py:437
  22.9 9.2 %collective-permute-start.6 = (bf16[128,1024]{1,0:T(8,128)(2,1)S(1)}, bf16[128,1024]{1,0:T(8,128)(2,1)S(1)}, u32[]{:S(2)}, u32[]{:S(2)}) collective-permute-start(bf16[128,1024]{1,0:T(8,128)(2,1)S(1)} %get-tuple-element.170), channel_id=1, source_target_pairs={{0,1},{2,3},{4,5},{6,7},{1,0},{3,2},{5,4},{7,6},{8,9},{10,11},{12,... | collective-permute-start | bytes 786440 | tf_op jit(solution)/shard_map/ppermute | solution.py:437
  27.0 9.4 %collective-permute-start.4 = (bf16[128,1024]{1,0:T(8,128)(2,1)S(1)}, bf16[128,1024]{1,0:T(8,128)(2,1)S(1)}, u32[]{:S(2)}, u32[]{:S(2)}) collective-permute-start(bf16[128,1024]{1,0:T(8,128)(2,1)S(1)} %get-tuple-element.164.refs_1_), channel_id=1, source_target_pairs={{0,2},{1,3},{4,6},{5,7},{2,0},{3,1},{6,4},{7,5},{8,10},{9,11},{12,... | collective-permute-start | bytes 786440 | tf_op jit(solution)/shard_map/ppermute | solution.py:437
  27.4 10.3 %collective-permute-start.2 = (bf16[128,1024]{1,0:T(8,128)(2,1)S(1)}, bf16[128,1024]{1,0:T(8,128)(2,1)S(1)}, u32[]{:S(2)}, u32[]{:S(2)}) collective-permute-start(bf16[128,1024]{1,0:T(8,128)(2,1)S(1)} %get-tuple-element.158), channel_id=1, source_target_pairs={{0,1},{2,3},{4,5},{6,7},{1,0},{3,2},{5,4},{7,6},{8,9},{10,11},{12,... | collective-permute-start | bytes 786440 | tf_op jit(solution)/shard_map/ppermute | solution.py:437
  31.0 11.2 %collective-permute-start.9 = (bf16[144,1024]{1,0:T(8,128)(2,1)S(1)}, bf16[144,1024]{1,0:T(8,128)(2,1)S(1)}, u32[]{:S(2)}, u32[]{:S(2)}) collective-permute-start(bf16[144,1024]{1,0:T(8,128)(2,1)S(1)} %get-tuple-element.178.refs_2_), channel_id=1, source_target_pairs={{2,4},{3,5},{4,2},{5,3},{10,12},{11,13},{12,10},{13,11},{18,20},{1... | collective-permute-start | bytes 884744 | tf_op jit(solution)/shard_map/ppermute | solution.py:437
  32.2 10.5 %collective-permute-start.10 = (bf16[128,1024]{1,0:T(8,128)(2,1)S(1)}, bf16[128,1024]{1,0:T(8,128)(2,1)S(1)}, u32[]{:S(2)}, u32[]{:S(2)}) collective-permute-start(bf16[128,1024]{1,0:T(8,128)(2,1)S(1)} %get-tuple-element.189.refs_1_), channel_id=1, source_target_pairs={{0,2},{1,3},{4,6},{5,7},{2,0},{3,1},{6,4},{7,5},{8,10},{9,11},{12,... | collective-permute-start | bytes 786440 | tf_op jit(solution)/shard_map/ppermute | solution.py:437
  36.5 7.1 %collective-permute-start.8 = (bf16[128,1024]{1,0:T(8,128)(2,1)S(1)}, bf16[128,1024]{1,0:T(8,128)(2,1)S(1)}, u32[]{:S(2)}, u32[]{:S(2)}) collective-permute-start(bf16[128,1024]{1,0:T(8,128)(2,1)S(1)} %get-tuple-element.177.refs_2_), channel_id=1, source_target_pairs={{2,4},{3,5},{4,2},{5,3},{10,12},{11,13},{12,10},{13,11},{18,20},{1... | collective-permute-start | bytes 786440 | tf_op jit(solution)/shard_map/ppermute | solution.py:437
  37.8 10.0 %collective-permute-start.7 = (bf16[128,1024]{1,0:T(8,128)(2,1)S(1)}, bf16[128,1024]{1,0:T(8,128)(2,1)S(1)}, u32[]{:S(2)}, u32[]{:S(2)}) collective-permute-start(bf16[128,1024]{1,0:T(8,128)(2,1)S(1)} %get-tuple-element.175.refs_1_), channel_id=1, source_target_pairs={{0,2},{1,3},{4,6},{5,7},{2,0},{3,1},{6,4},{7,5},{8,10},{9,11},{12,... | collective-permute-start | bytes 786440 | tf_op jit(solution)/shard_map/ppermute | solution.py:437
  42.7 13.1 %collective-permute-start.13 = (bf16[144,1024]{1,0:T(8,128)(2,1)S(1)}, bf16[144,1024]{1,0:T(8,128)(2,1)S(1)}, u32[]{:S(2)}, u32[]{:S(2)}) collective-permute-start(bf16[144,1024]{1,0:T(8,128)(2,1)S(1)} %get-tuple-element.202), channel_id=1, source_target_pairs={{0,2},{1,3},{4,6},{5,7},{2,0},{3,1},{6,4},{7,5},{8,10},{9,11},{12,... | collective-permute-start | bytes 884744 | tf_op jit(solution)/shard_map/ppermute | solution.py:437
  42.9 13.2 %collective-permute-start.12 = (bf16[128,1024]{1,0:T(8,128)(2,1)S(1)}, bf16[128,1024]{1,0:T(8,128)(2,1)S(1)}, u32[]{:S(2)}, u32[]{:S(2)}) collective-permute-start(bf16[128,1024]{1,0:T(8,128)(2,1)S(1)} %get-tuple-element.198.refs_2_), channel_id=1, source_target_pairs={{2,4},{3,5},{4,2},{5,3},{10,12},{11,13},{12,10},{13,11},{18,20},{1... | collective-permute-start | bytes 786440 | tf_op jit(solution)/shard_map/ppermute | solution.py:437
  48.0 8.4 %collective-permute-start.11 = (bf16[128,1024]{1,0:T(8,128)(2,1)S(1)}, bf16[128,1024]{1,0:T(8,128)(2,1)S(1)}, u32[]{:S(2)}, u32[]{:S(2)}) collective-permute-start(bf16[128,1024]{1,0:T(8,128)(2,1)S(1)} %get-tuple-element.194.refs_2_), channel_id=1, source_target_pairs={{2,4},{3,5},{4,2},{5,3},{10,12},{11,13},{12,10},{13,11},{18,20},{1... | collective-permute-start | bytes 786440 | tf_op jit(solution)/shard_map/ppermute | solution.py:437
  48.9 10.6 %collective-permute-start.16 = (bf16[128,1024]{1,0:T(8,128)(2,1)S(1)}, bf16[128,1024]{1,0:T(8,128)(2,1)S(1)}, u32[]{:S(2)}, u32[]{:S(2)}) collective-permute-start(bf16[128,1024]{1,0:T(8,128)(2,1)S(1)} %get-tuple-element.217), channel_id=1, source_target_pairs={{0,2},{1,3},{4,6},{5,7},{2,0},{3,1},{6,4},{7,5},{8,10},{9,11},{12,... | collective-permute-start | bytes 786440 | tf_op jit(solution)/shard_map/ppermute | solution.py:437
  56.0 3.7 %collective-permute-start.15 = (bf16[128,1024]{1,0:T(8,128)(2,1)S(1)}, bf16[128,1024]{1,0:T(8,128)(2,1)S(1)}, u32[]{:S(2)}, u32[]{:S(2)}) collective-permute-start(bf16[128,1024]{1,0:T(8,128)(2,1)S(1)} %get-tuple-element.214), channel_id=1, source_target_pairs={{0,8},{8,0},{1,9},{9,1},{2,10},{10,2},{3,11},{11,3},{4,12},{12,4},... | collective-permute-start | bytes 786440 | tf_op jit(solution)/shard_map/ppermute | solution.py:437
  56.3 9.2 %collective-permute-start.19 = (bf16[128,1024]{1,0:T(8,128)(2,1)S(1)}, bf16[128,1024]{1,0:T(8,128)(2,1)S(1)}, u32[]{:S(2)}, u32[]{:S(2)}) collective-permute-start(bf16[128,1024]{1,0:T(8,128)(2,1)S(1)} %get-tuple-element.226), channel_id=1, source_target_pairs={{0,2},{1,3},{4,6},{5,7},{2,0},{3,1},{6,4},{7,5},{8,10},{9,11},{12,... | collective-permute-start | bytes 786440 | tf_op jit(solution)/shard_map/ppermute | solution.py:437
  59.7 6.1 %collective-permute-start.18 = (bf16[128,1024]{1,0:T(8,128)(2,1)S(1)}, bf16[128,1024]{1,0:T(8,128)(2,1)S(1)}, u32[]{:S(2)}, u32[]{:S(2)}) collective-permute-start(bf16[128,1024]{1,0:T(8,128)(2,1)S(1)} %get-tuple-element.223), channel_id=1, source_target_pairs={{0,8},{8,0},{1,9},{9,1},{2,10},{10,2},{3,11},{11,3},{4,12},{12,4},... | collective-permute-start | bytes 786440 | tf_op jit(solution)/shard_map/ppermute | solution.py:437
  60.4 8.8 %collective-permute-start.17 = (bf16[128,1024]{1,0:T(8,128)(2,1)S(1)}, bf16[128,1024]{1,0:T(8,128)(2,1)S(1)}, u32[]{:S(2)}, u32[]{:S(2)}) collective-permute-start(bf16[128,1024]{1,0:T(8,128)(2,1)S(1)} %get-tuple-element.221), channel_id=1, source_target_pairs={{0,1},{2,3},{4,5},{6,7},{1,0},{3,2},{5,4},{7,6},{8,9},{10,11},{12,... | collective-permute-start | bytes 786440 | tf_op jit(solution)/shard_map/ppermute | solution.py:437
  60.4 10.5 %collective-permute-start.14 = (bf16[128,1024]{1,0:T(8,128)(2,1)S(1)}, bf16[128,1024]{1,0:T(8,128)(2,1)S(1)}, u32[]{:S(2)}, u32[]{:S(2)}) collective-permute-start(bf16[128,1024]{1,0:T(8,128)(2,1)S(1)} %get-tuple-element.212), channel_id=1, source_target_pairs={{0,2},{1,3},{4,6},{5,7},{2,0},{3,1},{6,4},{7,5},{8,10},{9,11},{12,... | collective-permute-start | bytes 786440 | tf_op jit(solution)/shard_map/ppermute | solution.py:437
  65.7 5.5 %collective-permute-start.22 = (bf16[128,1024]{1,0:T(8,128)(2,1)S(1)}, bf16[128,1024]{1,0:T(8,128)(2,1)S(1)}, u32[]{:S(2)}, u32[]{:S(2)}) collective-permute-start(bf16[128,1024]{1,0:T(8,128)(2,1)S(1)} %get-tuple-element.238), channel_id=1, source_target_pairs={{0,8},{8,0},{1,9},{9,1},{2,10},{10,2},{3,11},{11,3},{4,12},{12,4},... | collective-permute-start | bytes 786440 | tf_op jit(solution)/shard_map/ppermute | solution.py:437
  66.1 8.9 %collective-permute-start.21 = (bf16[128,1024]{1,0:T(8,128)(2,1)S(1)}, bf16[128,1024]{1,0:T(8,128)(2,1)S(1)}, u32[]{:S(2)}, u32[]{:S(2)}) collective-permute-start(bf16[128,1024]{1,0:T(8,128)(2,1)S(1)} %get-tuple-element.236), channel_id=1, source_target_pairs={{0,1},{2,3},{4,5},{6,7},{1,0},{3,2},{5,4},{7,6},{8,9},{10,11},{12,... | collective-permute-start | bytes 786440 | tf_op jit(solution)/shard_map/ppermute | solution.py:437
  71.1 5.7 %collective-permute-start.20 = (bf16[128,1024]{1,0:T(8,128)(2,1)S(1)}, bf16[128,1024]{1,0:T(8,128)(2,1)S(1)}, u32[]{:S(2)}, u32[]{:S(2)}) collective-permute-start(bf16[128,1024]{1,0:T(8,128)(2,1)S(1)} %get-tuple-element.231), channel_id=1, source_target_pairs={{0,8},{8,0},{1,9},{9,1},{2,10},{10,2},{3,11},{11,3},{4,12},{12,4},... | collective-permute-start | bytes 786440 | tf_op jit(solution)/shard_map/ppermute | solution.py:437
  71.6 10.4 %collective-permute-start.24 = (bf16[128,1024]{1,0:T(8,128)(2,1)S(1)}, bf16[128,1024]{1,0:T(8,128)(2,1)S(1)}, u32[]{:S(2)}, u32[]{:S(2)}) collective-permute-start(bf16[128,1024]{1,0:T(8,128)(2,1)S(1)} %get-tuple-element.251), channel_id=1, source_target_pairs={{0,1},{2,3},{4,5},{6,7},{1,0},{3,2},{5,4},{7,6},{8,9},{10,11},{12,... | collective-permute-start | bytes 786440 | tf_op jit(solution)/shard_map/ppermute | solution.py:437
  77.2 9.0 %collective-permute-start.23 = (bf16[128,1024]{1,0:T(8,128)(2,1)S(1)}, bf16[128,1024]{1,0:T(8,128)(2,1)S(1)}, u32[]{:S(2)}, u32[]{:S(2)}) collective-permute-start(bf16[128,1024]{1,0:T(8,128)(2,1)S(1)} %get-tuple-element.248), channel_id=1, source_target_pairs={{0,1},{2,3},{4,5},{6,7},{1,0},{3,2},{5,4},{7,6},{8,9},{10,11},{12,... | collective-permute-start | bytes 786440 | tf_op jit(solution)/shard_map/ppermute | solution.py:437

commit v4 on v3

--- a/solution.py
+++ b/solution.py
@@ -368,22 +368,38 @@
 
 
 def inside_block(first, count, values, conv_b, conv_c, cols, rows, skip, after, us=1.0):
-    def own(i):
-        return (0, i)
+    assert first % count == 0
+    chunk = first // count
+
+    def body(*refs):
+        values_ref, b_ref, c_ref, cols_ref, rows_ref, skip_ref = refs[:6]
+        part_ref, mark_ref = refs[6 + len(after) :]
+        for at in range(count):
+            wide, state = pl.ds(at * COLS, COLS), pl.ds(at * N, N)
+            inside_body(
+                values_ref.at[:, wide],
+                b_ref.at[:, state],
+                c_ref.at[:, state],
+                cols_ref.at[pl.ds(at, 1)],
+                rows_ref.at[pl.ds(at * HEADS, HEADS)],
+                skip_ref.at[pl.ds(at, 1)],
+                part_ref.at[:, wide],
+                mark_ref,
+            )
 
     return pl.pallas_call(
-        lambda *refs: inside_body(*refs[:6], *refs[6 + len(after) :]),
-        grid=(count,),
+        body,
+        grid=(1,),
         in_specs=[
-            pl.BlockSpec((SPAN, COLS), own),
-            pl.BlockSpec((SPAN, N), own),
-            pl.BlockSpec((SPAN, N), own),
-            pl.BlockSpec((1, SPAN, HEADS), lambda i: (first + i, 0, 0)),
-            pl.BlockSpec((HEADS, SPAN), lambda i: (first + i, 0)),
-            pl.BlockSpec((1, 1, COLS), lambda i: (first + i, 0, 0)),
+            whole(values),
+            whole(conv_b),
+            whole(conv_c),
+            pl.BlockSpec((count, SPAN, HEADS), lambda i: (chunk, 0, 0)),
+            pl.BlockSpec((count * HEADS, SPAN), lambda i: (chunk, 0)),
+            pl.BlockSpec((count, 1, COLS), lambda i: (chunk, 0, 0)),
         ]
         + [corner(a) for a in after],
-        out_specs=[pl.BlockSpec((SPAN, COLS), own), MARK],
+        out_specs=[pl.BlockSpec((SPAN, count * COLS), lambda i: (0, 0)), MARK],
         out_shape=[jax.ShapeDtypeStruct((SPAN, count * COLS), F32), mark()],
         compiler_params=params(),
         cost_estimate=cost(us),

time: 88.1 us -> 88.4 us (level)
  waiting for transfers between devices: 24.9 us -> 26.4 us
  Pallas kernels: 33.9 us -> 32.6 us
    ppermute x24, waiting for transfers between devices: 24.9 us -> 26.4 us  [swap(): return lax.ppermute(value, axis, pairs + [(b, a) for a, b in pairs])]
    pallas_call x4, Pallas kernels: 8.9 us -> 7.6 us  [inside_block(): pl.pallas_call(body, grid=(1,), in_specs=[whole(values), whole(conv_b), w...]
  transfers between devices with their start and end apart: 25 -> 25, of which waited for: 11 -> 11; matrix products, arithmetic and copies ran while one was open for 0% -> 0% of each run, Pallas kernels for 34% -> 33%
where the time goes in v4:
time: 88.4 us; the launch traced here: 88.2 us
  Pallas kernels  32.6 us (37%)
  starting transfers between devices  28.6 us (32%)
  waiting for transfers between devices  26.4 us (30%)
    ppermute x24, waiting for transfers between devices, swap(): return lax.ppermute(value, axis, pairs + [(b, a) for a, b in pairs])  26.4 us
    ppermute x24, starting transfers between devices, swap(): return lax.ppermute(value, axis, pairs + [(b, a) for a, b in pairs])  23.6 us
    pallas_call x4, Pallas kernels, inside_block(): pl.pallas_call(body, grid=(1,), in_specs=[whole(values), whole(conv_b), w...  7.6 us
    pallas_call x3, Pallas kernels, end_states(): pl.pallas_call(body, grid=(count,), in_specs=conv_specs(first, SPAN) + ri...  7.32 us
    pallas_call x4, Pallas kernels, with_carry(): pl.pallas_call(carried_body, grid=(count,), in_specs=[whole(side), pl.Blo...  7.27 us
    ppermute x1, starting transfers between devices, shards(): lax.ppermute(rim_rows(x_stream, b_stream, c_stream), ('outer', 'inner'),...  5.02 us
    pallas_call x20, Pallas kernels, merge(): pl.pallas_call(run, grid=(1,), in_specs=[whole(a) for a in given] + [corn...  4.74 us
    pallas_call x1, Pallas kernels, early_states(): pl.pallas_call(body, grid=(count,), in_specs=conv_specs(first, SPAN) + [c...  2.4 us
  transfers between devices with their start and end apart: 25, of which 11 were waited for; matrix products, arithmetic and copies ran while one was open for 0% of the time, Pallas kernels for 33%

profile of v4, /device:TPU:0, one launch (start us, length us, event | category | flops | bytes accessed | tf_op | source)
XLA Modules:
  0.0 88.2 jit_solution(15250548282451206811)
XLA Ops:
  0.2 1.2 %rim_rows.1 = bf16[3,10240]{1,0:T(4,128)(2,1)S(1)} custom-call(bf16[256,8192]{1,0:T(8,128)(2,1)} %refs_0_.4, bf16[256,1024]{1,0:T(8,128)(2,1)} %refs_1_.9, bf16[256,1024]{1,0:T(8,128)(2,1)} %refs_2_.9), custom_call_target="tpu_custom_call" | custom-call | flops 600000000 | tf_op jit(solution)/shard_map/rim_rows/pallas_call | solution.py:59
  1.3 5.0 %collective-permute-start = (bf16[3,10240]{1,0:T(4,128)(2,1)S(1)}, bf16[3,10240]{1,0:T(4,128)(2,1)S(1)}, u32[]{:S(2)}, u32[]{:S(2)}) collective-permute-start(bf16[3,10240]{1,0:T(4,128)(2,1)S(1)} %rim_rows.1), channel_id=1, source_target_pairs={{0,1},{1,2},{2,3},{3,4},{4,5},{5,6},{6,7},{7,8},{8,9},{9,10},{10,1... | collective-permute-start | bytes 184328 | tf_op jit(solution)/shard_map/ppermute | solution.py:797
  6.4 1.3 %time_steps.1 = (f32[8,256,16]{2,1,0:T(8,128)S(1)}, f32[128,256]{1,0:T(8,128)S(1)}, bf16[8,256,32]{2,1,0:T(8,128)(2,1)S(1)}, bf16[8,256,32]{2,1,0:T(8,128)(2,1)S...) custom-call(bf16[256,128]{1,0:T(8,128)(2,1)S(1)} %copy-done.4, ...), custom_call_target="tpu_custom_call" | custom-call | flops 1200000000 | tf_op jit(solution)/shard_map/time_steps/pallas_call | solution.py:145
  7.7 2.4 %early_states.1 = (bf16[256,2048]{1,0:T(8,128)(2,1)S(1)}, bf16[256,256]{1,0:T(8,128)(2,1)S(1)}, bf16[256,256]{1,0:T(8,128)(2,1)S(1)}, f32[2,128,1024]{2,1,0:T(8,128)S(1)}, f32[8,128]{1,0:T(8,128)S(1)}) custom-call(bf16[256,8192]{1,0:T(8,128)(2,1)S(1)} %copy-done, bf16[256,1024]{1,0:T(8,128)(2,1)S(1)} %copy-done.1, bf16[256,1024]{1,0:T(8,128)(2,1)S(1)} %copy-done.2, ...), custom_call_target="tpu_custom_call" | custom-call | flops 600000000 | tf_op jit(solution)/shard_map/early_states/pallas_call | solution.py:260
  10.9 1.6 %collective-permute-start.1 = (bf16[144,1024]{1,0:T(8,128)(2,1)S(1)}, bf16[144,1024]{1,0:T(8,128)(2,1)S(1)}, u32[]{:S(2)}, u32[]{:S(2)}) collective-permute-start(bf16[144,1024]{1,0:T(8,128)(2,1)S(1)} %get-tuple-element.143), channel_id=1, source_target_pairs={{0,1},{2,3},{4,5},{6,7},{1,0},{3,2},{5,4},{7,6},{8,9},{10,11},{12,... | collective-permute-start | bytes 884744 | tf_op jit(solution)/shard_map/ppermute | solution.py:453
  12.5 2.4 %end_states.3 = (bf16[256,2048]{1,0:T(8,128)(2,1)S(1)}, bf16[256,256]{1,0:T(8,128)(2,1)S(1)}, bf16[256,256]{1,0:T(8,128)(2,1)S(1)}, bf16[128,1024]{1,0:T(8,128)(...) custom-call(bf16[256,8192]{1,0:T(8,128)(2,1)S(1)} %copy-done, bf16[256,1024]{1,0:T(8,128)(2,1)S(1)} %copy-done.1, ...), custom_call_target="tpu_custom_call" | custom-call | flops 600000000 | tf_op jit(solution)/shard_map/end_states/pallas_call | solution.py:314
  15.5 2.4 %end_states.4 = (bf16[256,2048]{1,0:T(8,128)(2,1)S(1)}, bf16[256,256]{1,0:T(8,128)(2,1)S(1)}, bf16[256,256]{1,0:T(8,128)(2,1)S(1)}, bf16[128,1024]{1,0:T(8,128)(...) custom-call(bf16[256,8192]{1,0:T(8,128)(2,1)S(1)} %copy-done, bf16[256,1024]{1,0:T(8,128)(2,1)S(1)} %copy-done.1, ...), custom_call_target="tpu_custom_call" | custom-call | flops 600000000 | tf_op jit(solution)/shard_map/end_states/pallas_call | solution.py:314
  18.0 2.5 %collective-permute-done.1.refs_2_ = bf16[144,1024]{1,0:T(8,128)(2,1)S(1)} collective-permute-done((bf16[144,1024]{1,0:T(8,128)(2,1)S(1)}, bf16[144,1024]{1,0:T(8,128)(2,1)S(1)}, u32[]{:S(2)}, u32[]{:S(2)}) %collective-permute-start.1) | collective-permute-done | bytes 294944 | tf_op jit(solution)/shard_map/ppermute | solution.py:453
  20.8 2.1 %collective-permute-start.5 = (bf16[144,1024]{1,0:T(8,128)(2,1)S(1)}, bf16[144,1024]{1,0:T(8,128)(2,1)S(1)}, u32[]{:S(2)}, u32[]{:S(2)}) collective-permute-start(bf16[144,1024]{1,0:T(8,128)(2,1)S(1)} %get-tuple-element.165.refs_1_), channel_id=1, source_target_pairs={{0,2},{1,3},{4,6},{5,7},{2,0},{3,1},{6,4},{7,5},{8,10},{9,11},{12,... | collective-permute-start | bytes 884744 | tf_op jit(solution)/shard_map/ppermute | solution.py:453
  22.9 1.5 %collective-permute-start.6 = (bf16[128,1024]{1,0:T(8,128)(2,1)S(1)}, bf16[128,1024]{1,0:T(8,128)(2,1)S(1)}, u32[]{:S(2)}, u32[]{:S(2)}) collective-permute-start(bf16[128,1024]{1,0:T(8,128)(2,1)S(1)} %get-tuple-element.170), channel_id=1, source_target_pairs={{0,1},{2,3},{4,5},{6,7},{1,0},{3,2},{5,4},{7,6},{8,9},{10,11},{12,... | collective-permute-start | bytes 786440 | tf_op jit(solution)/shard_map/ppermute | solution.py:453
  24.4 2.4 %end_states.5 = (bf16[256,2048]{1,0:T(8,128)(2,1)S(1)}, bf16[256,256]{1,0:T(8,128)(2,1)S(1)}, bf16[256,256]{1,0:T(8,128)(2,1)S(1)}, bf16[128,1024]{1,0:T(8,128)(...) custom-call(bf16[256,8192]{1,0:T(8,128)(2,1)S(1)} %copy-done, bf16[256,1024]{1,0:T(8,128)(2,1)S(1)} %copy-done.1, ...), custom_call_target="tpu_custom_call" | custom-call | flops 600000000 | tf_op jit(solution)/shard_map/end_states/pallas_call | solution.py:314
  27.4 2.4 %collective-permute-start.2 = (bf16[128,1024]{1,0:T(8,128)(2,1)S(1)}, bf16[128,1024]{1,0:T(8,128)(2,1)S(1)}, u32[]{:S(2)}, u32[]{:S(2)}) collective-permute-start(bf16[128,1024]{1,0:T(8,128)(2,1)S(1)} %get-tuple-element.158), channel_id=1, source_target_pairs={{0,1},{2,3},{4,5},{6,7},{1,0},{3,2},{5,4},{7,6},{8,9},{10,11},{12,... | collective-permute-start | bytes 786440 | tf_op jit(solution)/shard_map/ppermute | solution.py:453
  29.8 0.9 %collective-permute-done.5.refs_2_.refs_3_ = bf16[144,1024]{1,0:T(8,128)(2,1)S(1)} collective-permute-done((bf16[144,1024]{1,0:T(8,128)(2,1)S(1)}, bf16[144,1024]{1,0:T(8,128)(2,1)S(1)}, u32[]{:S(2)}, u32[]{:S(2)}) %collective-permute-start.5) | collective-permute-done | bytes 294944 | tf_op jit(solution)/shard_map/ppermute | solution.py:453
  32.2 2.8 %collective-permute-start.10 = (bf16[128,1024]{1,0:T(8,128)(2,1)S(1)}, bf16[128,1024]{1,0:T(8,128)(2,1)S(1)}, u32[]{:S(2)}, u32[]{:S(2)}) collective-permute-start(bf16[128,1024]{1,0:T(8,128)(2,1)S(1)} %get-tuple-element.189.refs_1_), channel_id=1, source_target_pairs={{0,2},{1,3},{4,6},{5,7},{2,0},{3,1},{6,4},{7,5},{8,10},{9,11},{12,... | collective-permute-start | bytes 786440 | tf_op jit(solution)/shard_map/ppermute | solution.py:453
  35.0 1.3 %collective-permute-done.4.refs_2_.refs_3_ = bf16[128,1024]{1,0:T(8,128)(2,1)S(1)} collective-permute-done((bf16[128,1024]{1,0:T(8,128)(2,1)S(1)}, bf16[128,1024]{1,0:T(8,128)(2,1)S(1)}, u32[]{:S(2)}, u32[]{:S(2)}) %collective-permute-start.4) | collective-permute-done | bytes 262176 | tf_op jit(solution)/shard_map/ppermute | solution.py:453
  37.8 2.2 %collective-permute-start.7 = (bf16[128,1024]{1,0:T(8,128)(2,1)S(1)}, bf16[128,1024]{1,0:T(8,128)(2,1)S(1)}, u32[]{:S(2)}, u32[]{:S(2)}) collective-permute-start(bf16[128,1024]{1,0:T(8,128)(2,1)S(1)} %get-tuple-element.175.refs_1_), channel_id=1, source_target_pairs={{0,2},{1,3},{4,6},{5,7},{2,0},{3,1},{6,4},{7,5},{8,10},{9,11},{12,... | collective-permute-start | bytes 786440 | tf_op jit(solution)/shard_map/ppermute | solution.py:453
  40.0 1.9 %inside_block.4 = (f32[256,2048]{1,0:T(8,128)S(1)}, f32[8,128]{1,0:T(8,128)S(1)}) custom-call(bf16[256,2048]{1,0:T(8,128)(2,1)S(1)} %get-tuple-element.181.refs_0_, bf16[256,256]{1,0:T(8,128)(2,1)S(1)} %get-tuple-element.182.refs_1_, bf16[256,256]{1,0:T(8,128)(2,1)S(1)} %get-tuple-element.183.refs_2_.refs_1_, f32[8,256,16]{2,1,0:T(8,128)S(1)} %get-tuple-element.151.refs_3_, ...), custom_call_target="tpu_custom_call" | custom-call | flops 600000000 | tf_op jit(solution)/shard_map/inside_block/pallas_call | solution.py:390
  43.6 4.2 %collective-permute-done.7.refs_2_.refs_3_ = bf16[128,1024]{1,0:T(8,128)(2,1)S(1)} collective-permute-done((bf16[128,1024]{1,0:T(8,128)(2,1)S(1)}, bf16[128,1024]{1,0:T(8,128)(2,1)S(1)}, u32[]{:S(2)}, u32[]{:S(2)}) %collective-permute-start.7) | collective-permute-done | bytes 262176 | tf_op jit(solution)/shard_map/ppermute | solution.py:453
  48.0 0.9 collective-permute-start.11
  48.9 4.7 %collective-permute-start.16 = (bf16[128,1024]{1,0:T(8,128)(2,1)S(1)}, bf16[128,1024]{1,0:T(8,128)(2,1)S(1)}, u32[]{:S(2)}, u32[]{:S(2)}) collective-permute-start(bf16[128,1024]{1,0:T(8,128)(2,1)S(1)} %get-tuple-element.217), channel_id=1, source_target_pairs={{0,2},{1,3},{4,6},{5,7},{2,0},{3,1},{6,4},{7,5},{8,10},{9,11},{12,... | collective-permute-start | bytes 786440 | tf_op jit(solution)/shard_map/ppermute | solution.py:453
  53.6 1.9 %inside_block.5 = (f32[256,2048]{1,0:T(8,128)S(1)}, f32[8,128]{1,0:T(8,128)S(1)}) custom-call(bf16[256,2048]{1,0:T(8,128)(2,1)S(1)} %get-tuple-element.205.refs_0_, bf16[256,256]{1,0:T(8,128)(2,1)S(1)} %get-tuple-element.206.refs_1_, bf16[256,256]{1,0:T(8,128)(2,1)S(1)} %get-tuple-element.207.refs_2_.refs_1_, f32[8,256,16]{2,1,0:T(8,128)S(1)} %get-tuple-element.151.refs_3_, ...), custom_call_target="tpu_custom_call" | custom-call | flops 600000000 | tf_op jit(solution)/shard_map/inside_block/pallas_call | solution.py:390
  56.3 3.4 %collective-permute-done.16.refs_4_.refs_5_ = bf16[128,1024]{1,0:T(8,128)(2,1)S(1)} collective-permute-done((bf16[128,1024]{1,0:T(8,128)(2,1)S(1)}, bf16[128,1024]{1,0:T(8,128)(2,1)S(1)}, u32[]{:S(2)}, u32[]{:S(2)}) %collective-permute-start.16) | collective-permute-done | bytes 262176 | tf_op jit(solution)/shard_map/ppermute | solution.py:453
  61.5 3.9 %collective-permute-done.19.refs_4_.refs_5_ = bf16[128,1024]{1,0:T(8,128)(2,1)S(1)} collective-permute-done((bf16[128,1024]{1,0:T(8,128)(2,1)S(1)}, bf16[128,1024]{1,0:T(8,128)(2,1)S(1)}, u32[]{:S(2)}, u32[]{:S(2)}) %collective-permute-start.19) | collective-permute-done | bytes 262176 | tf_op jit(solution)/shard_map/ppermute | solution.py:453
  66.1 3.5 %collective-permute-done.17.refs_4_ = bf16[128,1024]{1,0:T(8,128)(2,1)S(1)} collective-permute-done((bf16[128,1024]{1,0:T(8,128)(2,1)S(1)}, bf16[128,1024]{1,0:T(8,128)(2,1)S(1)}, u32[]{:S(2)}, u32[]{:S(2)}) %collective-permute-start.17) | collective-permute-done | bytes 262176 | tf_op jit(solution)/shard_map/ppermute | solution.py:453
  69.5 1.8 %with_carry.4 = (bf16[256,8192]{1,0:T(8,128)(2,1)}, f32[8,128]{1,0:T(8,128)S(1)}) custom-call(f32[8,1024]{1,0:T(8,128)S(1)} %select_select_fusion.refs_11_.refs_0_, bf16[256,256]{1,0:T(8,128)(2,1)S(1)} %get-tuple-element.183.refs_2_.refs_1_, f32[256,2048]{1,0:T(8,128)S(1)} %get-tuple-element.213.refs_2_, bf16[128,1024]{1,0:T(8,128)(2,1)S(1)} %get-tuple-element.220.refs_3_, ...), custom_call_target="tpu_custom_call" | custom-call | flops 600000000 | tf_op jit(solution)/shard_map/with_carry/pallas_call | solution.py:429
  72.4 2.6 %collective-permute-done.21.refs_4_ = bf16[128,1024]{1,0:T(8,128)(2,1)S(1)} collective-permute-done((bf16[128,1024]{1,0:T(8,128)(2,1)S(1)}, bf16[128,1024]{1,0:T(8,128)(2,1)S(1)}, u32[]{:S(2)}, u32[]{:S(2)}) %collective-permute-start.21) | collective-permute-done | bytes 262176 | tf_op jit(solution)/shard_map/ppermute | solution.py:453
  75.0 1.8 %with_carry.5 = (bf16[256,8192]{1,0:T(8,128)(2,1)}, f32[8,128]{1,0:T(8,128)S(1)}) custom-call(f32[8,1024]{1,0:T(8,128)S(1)} %select_select_fusion.refs_11_.refs_0_, bf16[256,256]{1,0:T(8,128)(2,1)S(1)} %get-tuple-element.207.refs_2_.refs_1_, f32[256,2048]{1,0:T(8,128)S(1)} %get-tuple-element.234.refs_2_, ...), custom_call_target="tpu_custom_call", output_to_operand_aliasing={{0}: (7, {})} | custom-call | flops 600000000 | tf_op jit(solution)/shard_map/with_carry/pallas_call | solution.py:429
  77.5 1.9 %inside_block.6 = (f32[256,2048]{1,0:T(8,128)S(1)}, f32[8,128]{1,0:T(8,128)S(1)}) custom-call(bf16[256,2048]{1,0:T(8,128)(2,1)S(1)} %get-tuple-element.154.refs_0_, bf16[256,256]{1,0:T(8,128)(2,1)S(1)} %get-tuple-element.155.refs_1_, bf16[256,256]{1,0:T(8,128)(2,1)S(1)} %get-tuple-element.156.refs_2_.refs_1_, f32[8,256,16]{2,1,0:T(8,128)S(1)} %get-tuple-element.151.refs_3_, ...), custom_call_target="tpu_custom_call" | custom-call | flops 600000000 | tf_op jit(solution)/shard_map/inside_block/pallas_call | solution.py:390
  79.4 1.9 %inside_block.7 = (f32[256,2048]{1,0:T(8,128)S(1)}, f32[8,128]{1,0:T(8,128)S(1)}) custom-call(bf16[256,2048]{1,0:T(8,128)(2,1)S(1)} %get-tuple-element.149.refs_0_, bf16[256,256]{1,0:T(8,128)(2,1)S(1)} %get-tuple-element.150.refs_1_, bf16[256,256]{1,0:T(8,128)(2,1)S(1)} %get-tuple-element.148.refs_2_.refs_1_, f32[8,256,16]{2,1,0:T(8,128)S(1)} %get-tuple-element.151.refs_3_, ...), custom_call_target="tpu_custom_call" | custom-call | flops 600000000 | tf_op jit(solution)/shard_map/inside_block/pallas_call | solution.py:390
  81.3 1.8 %with_carry.6 = (bf16[256,8192]{1,0:T(8,128)(2,1)}, f32[8,128]{1,0:T(8,128)S(1)}) custom-call(f32[8,1024]{1,0:T(8,128)S(1)} %select_select_fusion.refs_11_.refs_0_, bf16[256,256]{1,0:T(8,128)(2,1)S(1)} %get-tuple-element.156.refs_2_.refs_1_, f32[256,2048]{1,0:T(8,128)S(1)} %get-tuple-element.249.refs_2_, ...), custom_call_target="tpu_custom_call", output_to_operand_aliasing={{0}: (7, {})} | custom-call | flops 600000000 | tf_op jit(solution)/shard_map/with_carry/pallas_call | solution.py:429
  83.2 3.2 %collective-permute-done.23.refs_4_ = bf16[128,1024]{1,0:T(8,128)(2,1)S(1)} collective-permute-done((bf16[128,1024]{1,0:T(8,128)(2,1)S(1)}, bf16[128,1024]{1,0:T(8,128)(2,1)S(1)}, u32[]{:S(2)}, u32[]{:S(2)}) %collective-permute-start.23) | collective-permute-done | bytes 262176 | tf_op jit(solution)/shard_map/ppermute | solution.py:453
  86.4 1.8 %with_carry.7 = (bf16[256,8192]{1,0:T(8,128)(2,1)}, f32[8,128]{1,0:T(8,128)}) custom-call(f32[8,1024]{1,0:T(8,128)S(1)} %select_select_fusion.refs_11_.refs_0_, bf16[256,256]{1,0:T(8,128)(2,1)S(1)} %get-tuple-element.148.refs_2_.refs_1_, f32[256,2048]{1,0:T(8,128)S(1)} %get-tuple-element.246.refs_2_, ...), custom_call_target="tpu_custom_call", output_to_operand_aliasing={{0}: (7, {})} | custom-call | flops 600000000 | tf_op jit(solution)/shard_map/with_carry/pallas_call | solution.py:429
  (71 shorter events, 12.1 us)
Async XLA Ops:
  0.0 6.4 %copy-start.4 = (bf16[256,128]{1,0:T(8,128)(2,1)S(1)}, bf16[256,128]{1,0:T(8,128)(2,1)}, u32[]{:S(2)}) copy-start(bf16[256,128]{1,0:T(8,128)(2,1)} %dt_ref) | copy-start | bytes 196612
  0.0 6.4 %copy-start.6 = (f32[128]{0:T(128)S(1)}, f32[128]{0:T(128)}, u32[]{:S(2)}) copy-start(f32[128]{0:T(128)} %param.12) | copy-start | bytes 1540
  0.0 6.4 %copy-start.5 = (f32[128]{0:T(128)S(1)}, f32[128]{0:T(128)}, u32[]{:S(2)}) copy-start(f32[128]{0:T(128)} %param.11) | copy-start | bytes 1540
  0.1 7.5 %copy-start = (bf16[256,8192]{1,0:T(8,128)(2,1)S(1)}, bf16[256,8192]{1,0:T(8,128)(2,1)}, u32[]{:S(2)}) copy-start(bf16[256,8192]{1,0:T(8,128)(2,1)} %refs_0_.4) | copy-start | bytes 12582916
  0.1 7.5 %copy-start.1 = (bf16[256,1024]{1,0:T(8,128)(2,1)S(1)}, bf16[256,1024]{1,0:T(8,128)(2,1)}, u32[]{:S(2)}) copy-start(bf16[256,1024]{1,0:T(8,128)(2,1)} %refs_1_.9) | copy-start | bytes 1572868
  0.1 7.5 %copy-start.2 = (bf16[256,1024]{1,0:T(8,128)(2,1)S(1)}, bf16[256,1024]{1,0:T(8,128)(2,1)}, u32[]{:S(2)}) copy-start(bf16[256,1024]{1,0:T(8,128)(2,1)} %refs_2_.9) | copy-start | bytes 1572868
  0.1 7.5 %copy-start.3 = (bf16[4,10240]{1,0:T(4,128)(2,1)S(1)}, bf16[4,10240]{1,0:T(4,128)(2,1)}, u32[]{:S(2)}) copy-start(bf16[4,10240]{1,0:T(4,128)(2,1)} %refs_5_.9) | copy-start | bytes 245764
  1.3 8.8 %collective-permute-start = (bf16[3,10240]{1,0:T(4,128)(2,1)S(1)}, bf16[3,10240]{1,0:T(4,128)(2,1)S(1)}, u32[]{:S(2)}, u32[]{:S(2)}) collective-permute-start(bf16[3,10240]{1,0:T(4,128)(2,1)S(1)} %rim_rows.1), channel_id=1, source_target_pairs={{0,1},{1,2},{2,3},{3,4},{4,5},{5,6},{6,7},{7,8},{8,9},{9,10},{10,1... | collective-permute-start | bytes 184328 | tf_op jit(solution)/shard_map/ppermute | solution.py:797
  10.9 9.5 %collective-permute-start.1 = (bf16[144,1024]{1,0:T(8,128)(2,1)S(1)}, bf16[144,1024]{1,0:T(8,128)(2,1)S(1)}, u32[]{:S(2)}, u32[]{:S(2)}) collective-permute-start(bf16[144,1024]{1,0:T(8,128)(2,1)S(1)} %get-tuple-element.143), channel_id=1, source_target_pairs={{0,1},{2,3},{4,5},{6,7},{1,0},{3,2},{5,4},{7,6},{8,9},{10,11},{12,... | collective-permute-start | bytes 884744 | tf_op jit(solution)/shard_map/ppermute | solution.py:453
  14.9 11.9 %collective-permute-start.3 = (bf16[128,1024]{1,0:T(8,128)(2,1)S(1)}, bf16[128,1024]{1,0:T(8,128)(2,1)S(1)}, u32[]{:S(2)}, u32[]{:S(2)}) collective-permute-start(bf16[128,1024]{1,0:T(8,128)(2,1)S(1)} %get-tuple-element.161), channel_id=1, source_target_pairs={{0,1},{2,3},{4,5},{6,7},{1,0},{3,2},{5,4},{7,6},{8,9},{10,11},{12,... | collective-permute-start | bytes 786440 | tf_op jit(solution)/shard_map/ppermute | solution.py:453
  20.8 10.0 %collective-permute-start.5 = (bf16[144,1024]{1,0:T(8,128)(2,1)S(1)}, bf16[144,1024]{1,0:T(8,128)(2,1)S(1)}, u32[]{:S(2)}, u32[]{:S(2)}) collective-permute-start(bf16[144,1024]{1,0:T(8,128)(2,1)S(1)} %get-tuple-element.165.refs_1_), channel_id=1, source_target_pairs={{0,2},{1,3},{4,6},{5,7},{2,0},{3,1},{6,4},{7,5},{8,10},{9,11},{12,... | collective-permute-start | bytes 884744 | tf_op jit(solution)/shard_map/ppermute | solution.py:453
  22.9 9.2 %collective-permute-start.6 = (bf16[128,1024]{1,0:T(8,128)(2,1)S(1)}, bf16[128,1024]{1,0:T(8,128)(2,1)S(1)}, u32[]{:S(2)}, u32[]{:S(2)}) collective-permute-start(bf16[128,1024]{1,0:T(8,128)(2,1)S(1)} %get-tuple-element.170), channel_id=1, source_target_pairs={{0,1},{2,3},{4,5},{6,7},{1,0},{3,2},{5,4},{7,6},{8,9},{10,11},{12,... | collective-permute-start | bytes 786440 | tf_op jit(solution)/shard_map/ppermute | solution.py:453
  27.0 9.4 %collective-permute-start.4 = (bf16[128,1024]{1,0:T(8,128)(2,1)S(1)}, bf16[128,1024]{1,0:T(8,128)(2,1)S(1)}, u32[]{:S(2)}, u32[]{:S(2)}) collective-permute-start(bf16[128,1024]{1,0:T(8,128)(2,1)S(1)} %get-tuple-element.164.refs_1_), channel_id=1, source_target_pairs={{0,2},{1,3},{4,6},{5,7},{2,0},{3,1},{6,4},{7,5},{8,10},{9,11},{12,... | collective-permute-start | bytes 786440 | tf_op jit(solution)/shard_map/ppermute | solution.py:453
  27.4 10.3 %collective-permute-start.2 = (bf16[128,1024]{1,0:T(8,128)(2,1)S(1)}, bf16[128,1024]{1,0:T(8,128)(2,1)S(1)}, u32[]{:S(2)}, u32[]{:S(2)}) collective-permute-start(bf16[128,1024]{1,0:T(8,128)(2,1)S(1)} %get-tuple-element.158), channel_id=1, source_target_pairs={{0,1},{2,3},{4,5},{6,7},{1,0},{3,2},{5,4},{7,6},{8,9},{10,11},{12,... | collective-permute-start | bytes 786440 | tf_op jit(solution)/shard_map/ppermute | solution.py:453
  31.0 10.9 %collective-permute-start.9 = (bf16[144,1024]{1,0:T(8,128)(2,1)S(1)}, bf16[144,1024]{1,0:T(8,128)(2,1)S(1)}, u32[]{:S(2)}, u32[]{:S(2)}) collective-permute-start(bf16[144,1024]{1,0:T(8,128)(2,1)S(1)} %get-tuple-element.178.refs_2_), channel_id=1, source_target_pairs={{2,4},{3,5},{4,2},{5,3},{10,12},{11,13},{12,10},{13,11},{18,20},{1... | collective-permute-start | bytes 884744 | tf_op jit(solution)/shard_map/ppermute | solution.py:453
  32.2 10.4 %collective-permute-start.10 = (bf16[128,1024]{1,0:T(8,128)(2,1)S(1)}, bf16[128,1024]{1,0:T(8,128)(2,1)S(1)}, u32[]{:S(2)}, u32[]{:S(2)}) collective-permute-start(bf16[128,1024]{1,0:T(8,128)(2,1)S(1)} %get-tuple-element.189.refs_1_), channel_id=1, source_target_pairs={{0,2},{1,3},{4,6},{5,7},{2,0},{3,1},{6,4},{7,5},{8,10},{9,11},{12,... | collective-permute-start | bytes 786440 | tf_op jit(solution)/shard_map/ppermute | solution.py:453
  36.5 7.0 %collective-permute-start.8 = (bf16[128,1024]{1,0:T(8,128)(2,1)S(1)}, bf16[128,1024]{1,0:T(8,128)(2,1)S(1)}, u32[]{:S(2)}, u32[]{:S(2)}) collective-permute-start(bf16[128,1024]{1,0:T(8,128)(2,1)S(1)} %get-tuple-element.177.refs_2_), channel_id=1, source_target_pairs={{2,4},{3,5},{4,2},{5,3},{10,12},{11,13},{12,10},{13,11},{18,20},{1... | collective-permute-start | bytes 786440 | tf_op jit(solution)/shard_map/ppermute | solution.py:453
  37.8 10.0 %collective-permute-start.7 = (bf16[128,1024]{1,0:T(8,128)(2,1)S(1)}, bf16[128,1024]{1,0:T(8,128)(2,1)S(1)}, u32[]{:S(2)}, u32[]{:S(2)}) collective-permute-start(bf16[128,1024]{1,0:T(8,128)(2,1)S(1)} %get-tuple-element.175.refs_1_), channel_id=1, source_target_pairs={{0,2},{1,3},{4,6},{5,7},{2,0},{3,1},{6,4},{7,5},{8,10},{9,11},{12,... | collective-permute-start | bytes 786440 | tf_op jit(solution)/shard_map/ppermute | solution.py:453
  42.3 13.1 %collective-permute-start.13 = (bf16[144,1024]{1,0:T(8,128)(2,1)S(1)}, bf16[144,1024]{1,0:T(8,128)(2,1)S(1)}, u32[]{:S(2)}, u32[]{:S(2)}) collective-permute-start(bf16[144,1024]{1,0:T(8,128)(2,1)S(1)} %get-tuple-element.202), channel_id=1, source_target_pairs={{0,2},{1,3},{4,6},{5,7},{2,0},{3,1},{6,4},{7,5},{8,10},{9,11},{12,... | collective-permute-start | bytes 884744 | tf_op jit(solution)/shard_map/ppermute | solution.py:453
  42.8 13.0 %collective-permute-start.12 = (bf16[128,1024]{1,0:T(8,128)(2,1)S(1)}, bf16[128,1024]{1,0:T(8,128)(2,1)S(1)}, u32[]{:S(2)}, u32[]{:S(2)}) collective-permute-start(bf16[128,1024]{1,0:T(8,128)(2,1)S(1)} %get-tuple-element.198.refs_2_), channel_id=1, source_target_pairs={{2,4},{3,5},{4,2},{5,3},{10,12},{11,13},{12,10},{13,11},{18,20},{1... | collective-permute-start | bytes 786440 | tf_op jit(solution)/shard_map/ppermute | solution.py:453
  48.0 8.2 %collective-permute-start.11 = (bf16[128,1024]{1,0:T(8,128)(2,1)S(1)}, bf16[128,1024]{1,0:T(8,128)(2,1)S(1)}, u32[]{:S(2)}, u32[]{:S(2)}) collective-permute-start(bf16[128,1024]{1,0:T(8,128)(2,1)S(1)} %get-tuple-element.194.refs_2_), channel_id=1, source_target_pairs={{2,4},{3,5},{4,2},{5,3},{10,12},{11,13},{12,10},{13,11},{18,20},{1... | collective-permute-start | bytes 786440 | tf_op jit(solution)/shard_map/ppermute | solution.py:453
  48.9 10.8 %collective-permute-start.16 = (bf16[128,1024]{1,0:T(8,128)(2,1)S(1)}, bf16[128,1024]{1,0:T(8,128)(2,1)S(1)}, u32[]{:S(2)}, u32[]{:S(2)}) collective-permute-start(bf16[128,1024]{1,0:T(8,128)(2,1)S(1)} %get-tuple-element.217), channel_id=1, source_target_pairs={{0,2},{1,3},{4,6},{5,7},{2,0},{3,1},{6,4},{7,5},{8,10},{9,11},{12,... | collective-permute-start | bytes 786440 | tf_op jit(solution)/shard_map/ppermute | solution.py:453
  55.7 4.3 %collective-permute-start.15 = (bf16[128,1024]{1,0:T(8,128)(2,1)S(1)}, bf16[128,1024]{1,0:T(8,128)(2,1)S(1)}, u32[]{:S(2)}, u32[]{:S(2)}) collective-permute-start(bf16[128,1024]{1,0:T(8,128)(2,1)S(1)} %get-tuple-element.214), channel_id=1, source_target_pairs={{0,8},{8,0},{1,9},{9,1},{2,10},{10,2},{3,11},{11,3},{4,12},{12,4},... | collective-permute-start | bytes 786440 | tf_op jit(solution)/shard_map/ppermute | solution.py:453
  56.0 9.3 %collective-permute-start.19 = (bf16[128,1024]{1,0:T(8,128)(2,1)S(1)}, bf16[128,1024]{1,0:T(8,128)(2,1)S(1)}, u32[]{:S(2)}, u32[]{:S(2)}) collective-permute-start(bf16[128,1024]{1,0:T(8,128)(2,1)S(1)} %get-tuple-element.226), channel_id=1, source_target_pairs={{0,2},{1,3},{4,6},{5,7},{2,0},{3,1},{6,4},{7,5},{8,10},{9,11},{12,... | collective-permute-start | bytes 786440 | tf_op jit(solution)/shard_map/ppermute | solution.py:453
  59.9 5.7 %collective-permute-start.18 = (bf16[128,1024]{1,0:T(8,128)(2,1)S(1)}, bf16[128,1024]{1,0:T(8,128)(2,1)S(1)}, u32[]{:S(2)}, u32[]{:S(2)}) collective-permute-start(bf16[128,1024]{1,0:T(8,128)(2,1)S(1)} %get-tuple-element.223), channel_id=1, source_target_pairs={{0,8},{8,0},{1,9},{9,1},{2,10},{10,2},{3,11},{11,3},{4,12},{12,4},... | collective-permute-start | bytes 786440 | tf_op jit(solution)/shard_map/ppermute | solution.py:453
  60.6 8.9 %collective-permute-start.17 = (bf16[128,1024]{1,0:T(8,128)(2,1)S(1)}, bf16[128,1024]{1,0:T(8,128)(2,1)S(1)}, u32[]{:S(2)}, u32[]{:S(2)}) collective-permute-start(bf16[128,1024]{1,0:T(8,128)(2,1)S(1)} %get-tuple-element.221), channel_id=1, source_target_pairs={{0,1},{2,3},{4,5},{6,7},{1,0},{3,2},{5,4},{7,6},{8,9},{10,11},{12,... | collective-permute-start | bytes 786440 | tf_op jit(solution)/shard_map/ppermute | solution.py:453
  60.7 10.7 %collective-permute-start.14 = (bf16[128,1024]{1,0:T(8,128)(2,1)S(1)}, bf16[128,1024]{1,0:T(8,128)(2,1)S(1)}, u32[]{:S(2)}, u32[]{:S(2)}) collective-permute-start(bf16[128,1024]{1,0:T(8,128)(2,1)S(1)} %get-tuple-element.212), channel_id=1, source_target_pairs={{0,2},{1,3},{4,6},{5,7},{2,0},{3,1},{6,4},{7,5},{8,10},{9,11},{12,... | collective-permute-start | bytes 786440 | tf_op jit(solution)/shard_map/ppermute | solution.py:453
  65.5 6.1 %collective-permute-start.22 = (bf16[128,1024]{1,0:T(8,128)(2,1)S(1)}, bf16[128,1024]{1,0:T(8,128)(2,1)S(1)}, u32[]{:S(2)}, u32[]{:S(2)}) collective-permute-start(bf16[128,1024]{1,0:T(8,128)(2,1)S(1)} %get-tuple-element.238), channel_id=1, source_target_pairs={{0,8},{8,0},{1,9},{9,1},{2,10},{10,2},{3,11},{11,3},{4,12},{12,4},... | collective-permute-start | bytes 786440 | tf_op jit(solution)/shard_map/ppermute | solution.py:453
  66.0 9.0 %collective-permute-start.21 = (bf16[128,1024]{1,0:T(8,128)(2,1)S(1)}, bf16[128,1024]{1,0:T(8,128)(2,1)S(1)}, u32[]{:S(2)}, u32[]{:S(2)}) collective-permute-start(bf16[128,1024]{1,0:T(8,128)(2,1)S(1)} %get-tuple-element.236), channel_id=1, source_target_pairs={{0,1},{2,3},{4,5},{6,7},{1,0},{3,2},{5,4},{7,6},{8,9},{10,11},{12,... | collective-permute-start | bytes 786440 | tf_op jit(solution)/shard_map/ppermute | solution.py:453
  71.6 5.2 %collective-permute-start.20 = (bf16[128,1024]{1,0:T(8,128)(2,1)S(1)}, bf16[128,1024]{1,0:T(8,128)(2,1)S(1)}, u32[]{:S(2)}, u32[]{:S(2)}) collective-permute-start(bf16[128,1024]{1,0:T(8,128)(2,1)S(1)} %get-tuple-element.231), channel_id=1, source_target_pairs={{0,8},{8,0},{1,9},{9,1},{2,10},{10,2},{3,11},{11,3},{4,12},{12,4},... | collective-permute-start | bytes 786440 | tf_op jit(solution)/shard_map/ppermute | solution.py:453
  72.0 9.3 %collective-permute-start.24 = (bf16[128,1024]{1,0:T(8,128)(2,1)S(1)}, bf16[128,1024]{1,0:T(8,128)(2,1)S(1)}, u32[]{:S(2)}, u32[]{:S(2)}) collective-permute-start(bf16[128,1024]{1,0:T(8,128)(2,1)S(1)} %get-tuple-element.251), channel_id=1, source_target_pairs={{0,1},{2,3},{4,5},{6,7},{1,0},{3,2},{5,4},{7,6},{8,9},{10,11},{12,... | collective-permute-start | bytes 786440 | tf_op jit(solution)/shard_map/ppermute | solution.py:453
  77.2 9.2 %collective-permute-start.23 = (bf16[128,1024]{1,0:T(8,128)(2,1)S(1)}, bf16[128,1024]{1,0:T(8,128)(2,1)S(1)}, u32[]{:S(2)}, u32[]{:S(2)}) collective-permute-start(bf16[128,1024]{1,0:T(8,128)(2,1)S(1)} %get-tuple-element.248), channel_id=1, source_target_pairs={{0,1},{2,3},{4,5},{6,7},{1,0},{3,2},{5,4},{7,6},{8,9},{10,11},{12,... | collective-permute-start | bytes 786440 | tf_op jit(solution)/shard_map/ppermute | solution.py:453
